TPU v7x, 256 devices: a whole 4x4x8 slice. The times are simulated.
256 devices in a mesh: dp: 32 (over x, z), fsdp: 4 (over y), tensor: 2 (over core).
Axes of the slice: x: 4, y: 4, z: 8, core: 2. Of those that a mesh axis runs over, the one named last changes fastest.
Arguments:
- activations: bfloat16 [32768, 8192], P(('dp', 'fsdp')), may hold values from -6 to 6
- out_grads: bfloat16 [32768, 2, 2048], P(('dp', 'fsdp'), 'tensor'), may hold values from -0.032958984 to 0.032958984
- basis: bfloat16 [8192, 1024], P('dp'), may hold values from -0.0625 to 0.0625
- weights: bfloat16 [2, 2048, 8192], P('tensor', ('dp', 'fsdp')), may hold values from -3 to 3
- first_moment: float32 [2, 2048, 1024], P('tensor', ('dp', 'fsdp')), may hold values from -2 to 2
- second_moment: float32 [2, 2048, 1024], P('tensor', ('dp', 'fsdp')), may hold values from 0.0001 to 0.01
Outputs:
- new_weights: bfloat16 [2, 2048, 8192], P('tensor', 'dp')
- first_new: float32 [2, 2048, 1024], P('tensor', ('dp', 'fsdp'))
- second_new: float32 [2, 2048, 1024], P('tensor', ('dp', 'fsdp'))
All inputs are finite; a program needn't handle non-finite values.
Results may differ from a plain program's by a relative error of at most 0.012.
Values may be sent and summed in bfloat16 or wider, within the bound.
No kernel may reach another device: no remote copies, remote signals or barrier semaphores. Data moves between devices by JAX's collectives and lax.ppermute only.
A program may use at most 128 MiB of HBM per device.

v0:
```python
import jax
import jax.numpy as jnp
from jax import lax
from jax.experimental import pallas as pl
from jax.experimental.pallas import tpu as pltpu
from jax.sharding import PartitionSpec as P

STEP = 10

beta_one = 0.9
beta_two = 0.999
epsilon = 1e-08
step_scale = 0.25

NX, NZ, NY = 4, 8, 4
f32 = jnp.float32
bf16 = jnp.bfloat16


def along_x(value, d):
    pairs = [(x * NZ + z, (x + d) % NX * NZ + z) for x in range(NX) for z in range(NZ)]
    return lax.ppermute(value, "dp", pairs)


def along_z(value, d):
    pairs = [(x * NZ + z, x * NZ + (z + d) % NZ) for x in range(NX) for z in range(NZ)]
    return lax.ppermute(value, "dp", pairs)


def along_y(value, d):
    return lax.ppermute(value, "fsdp", [(y, (y + d) % NY) for y in range(NY)])


def across(value):
    return lax.ppermute(value, "tensor", [(0, 1), (1, 0)])


def fetch(value, sources):
    pairs = [
        (((x + sources[y % 2]) % NX * NZ + z) * NY + y, (x * NZ + z) * NY + y)
        for x in range(NX)
        for z in range(NZ)
        for y in range(NY)
    ]
    return lax.ppermute(value, ("dp", "fsdp"), pairs)


def rows(array, start, size):
    return lax.dynamic_slice_in_dim(array, start, size, axis=0)


def columns(array, start, size):
    return lax.dynamic_slice_in_dim(array, start, size, axis=1)


def put(whole, part, start, axis):
    return lax.dynamic_update_slice_in_dim(whole, part, start, axis=axis)


def gather_y(block, y):
    n = block.shape[0]
    whole = jnp.zeros((NY * n, block.shape[1]), block.dtype)
    whole = put(whole, block, y * n, 0)
    for d in range(1, NY):
        whole = put(whole, along_y(block, d), lax.rem(y + NY - d, NY) * n, 0)
    return whole


def dot(a, b, dims):
    return lax.dot_general(a, b, ((dims[0], dims[1]), ((), ())), preferred_element_type=f32)


def cut(activations, place):
    pair, quarter = activations.shape[0] // 2, activations.shape[1] // NX

    def kernel(place_ref, act_ref, *refs):
        outs, sems = refs[:-1], refs[-1]
        copies = []
        for n, out in enumerate(outs):
            row = pl.multiple_of(place_ref[0, n], pair)
            col = pl.multiple_of(place_ref[1, n], quarter)
            source = act_ref.at[pl.ds(row, pair), pl.ds(col, quarter)]
            copies.append(pltpu.make_async_copy(source, out, sems.at[n]))
        for copy in copies:
            copy.start()
        for copy in copies:
            copy.wait()

    shape = jax.ShapeDtypeStruct((pair, quarter), activations.dtype)
    return pl.pallas_call(
        kernel,
        out_shape=[shape] * (NX + 1),
        in_specs=[pl.BlockSpec(memory_space=pltpu.SMEM), pl.BlockSpec(memory_space=pl.ANY)],
        out_specs=[pl.BlockSpec(memory_space=pltpu.VMEM)] * (NX + 1),
        scratch_shapes=[pltpu.SemaphoreType.DMA((NX + 1,))],
    )(place, activations)


def shards(activations, out_grads, basis, weights, first_moment, second_moment):
    dp, y, core = lax.axis_index("dp"), lax.axis_index("fsdp"), lax.axis_index("tensor")
    x, z = lax.div(dp, NZ), lax.rem(dp, NZ)
    tokens, width = activations.shape
    rank = basis.shape[1]
    half, quarter, pair = rank // 2, width // NX, tokens // 2

    mine = columns(basis, core * half, half)
    n, h = mine.shape[0], mine.shape[0] // 2
    ahead, back = along_z(mine, 1), along_z(mine, -1)
    places = [(core, x), (1 - core, x)] + [(core, lax.rem(x + d, NX)) for d in range(1, NX)]
    place = jnp.stack(
        [jnp.stack([r * pair for r, _ in places]), jnp.stack([q * quarter for _, q in places])]
    )
    here, there, *leaving = cut(activations, place)
    ahead, back, *leaving = lax.optimization_barrier((ahead, back, *leaving))
    own, other = [here], [there]
    for d in range(1, NX):
        own.append(along_x(leaving[d - 1], d))

    held = jnp.zeros((NZ * n, half), bf16)
    held = put(held, mine, z * n, 0)
    for s in range(1, NZ // 2):
        if s > 1:
            ahead, back = along_z(ahead, 1), along_z(back, -1)
        held = put(held, ahead, lax.rem(z + NZ - s, NZ) * n, 0)
        held = put(held, back, lax.rem(z + s, NZ) * n, 0)
    back, out_grads = lax.optimization_barrier((back, out_grads))
    turned = out_grads[:, 0, :].T.reshape(NX * NZ, NY, 16, tokens)
    parts = []
    for d in range(NY):
        part = lax.dynamic_index_in_dim(turned, lax.rem(y + d, NY), axis=1, keepdims=False)
        parts.append(part if d == 0 else along_y(part, d))

    own, _, parts = lax.optimization_barrier((own, back, parts))

    far = lax.rem(z + NZ // 2, NZ) * n
    held = put(held, along_z(ahead[:h], 1), far, 0)
    held = put(held, along_z(back[h:], -1), far + h, 0)
    for d in range(1, NX):
        other.append(across(own[d]))

    odd = lax.rem(y, 2)
    span = [[lax.rem(x + o, NX) * quarter, lax.rem(x + o + 2, NX) * quarter] for o in (0, 1)]
    here_at = [jnp.where(odd == 1, q, p) for p, q in zip(*span)]
    there_at = [jnp.where(odd == 1, p, q) for p, q in zip(*span)]
    sources = ((0, 1), (2, 3))
    cuts = (0, quarter // 4, quarter)
    pieces = [held[i:j] for i, j in zip(cuts, cuts[1:])]
    slots = [[fetch(pieces[0], o)] for o in sources]

    first = core == 0
    near = dot(jnp.concatenate(own, axis=0), held, ((1,), (0,))).reshape(NX, pair, half)
    away = dot(jnp.concatenate(other, axis=0), held, ((1,), (0,))).reshape(NX, pair, half)
    partial = jnp.concatenate(
        [jnp.where(first, near, away), jnp.where(first, away, near)], axis=1
    )
    sent = partial.astype(bf16)
    sent, slots[0][0], slots[1][0] = lax.optimization_barrier((sent, slots[0][0], slots[1][0]))
    features = jnp.concatenate(parts, axis=2)
    crossed = across(features)
    features = jnp.stack(
        [jnp.where(first, features, crossed), jnp.where(first, crossed, features)], axis=1
    )

    total = partial[0]
    for d in range(1, NX):
        total = total + along_x(sent[d], -d).astype(f32)
    low_rank = total.astype(bf16)

    low_rank, pieces[1] = lax.optimization_barrier((low_rank, pieces[1]))
    low = jnp.concatenate([low_rank] + [along_y(low_rank, d) for d in range(1, NY)], axis=0)

    for slot, o in zip(slots, sources):
        slot.append(fetch(pieces[1], o))

    weights, low = lax.optimization_barrier((weights[0], low))
    kept = jnp.concatenate([columns(weights, at, quarter) for at in here_at], axis=1)
    given = jnp.concatenate([columns(weights, at, quarter) for at in there_at], axis=1)
    old = jnp.zeros((NY * 16, 2 * quarter), bf16)
    old = put(old, kept, y * 16, 0)
    for d in range(1, NY):
        old = put(old, along_y(given if d % 2 else kept, d), lax.rem(y + NY - d, NY) * 16, 0)

    projected = dot(features.reshape(-1, NY * tokens), low, ((1,), (0,)))
    projected = projected.astype(bf16).reshape(2 * NX * NZ, 16, half)
    got = lax.all_to_all(projected, ("dp", "tensor"), split_axis=0, concat_axis=0, tiled=True)
    got = got.reshape(NX * NZ, 2, 16, half).astype(f32).sum(axis=0)
    projected = jnp.concatenate([got[0], got[1]], axis=1)[None]

    first_new = beta_one * first_moment + (1.0 - beta_one) * projected
    second_new = beta_two * second_moment + (1.0 - beta_two) * projected * projected
    corrected = first_new / (1.0 - beta_one**STEP)
    scaled = jnp.sqrt(second_new / (1.0 - beta_two**STEP)) + epsilon
    direction = (corrected / scaled).astype(bf16)[0]

    halves = jnp.stack([direction[:, :half], direction[:, half:]])
    directions = lax.all_to_all(
        jnp.broadcast_to(halves[None], (NY, 2, 16, half)).reshape(NY * 2, 16, half),
        ("fsdp", "tensor"),
        split_axis=0,
        concat_axis=0,
        tiled=True,
    )
    directions = directions.reshape(NY, 2, 16, half).transpose(1, 0, 2, 3).reshape(2, NY * 16, half)
    new_weights = jnp.zeros((NY * 16, width), bf16)
    stacked = directions.reshape(-1, half)
    both = [dot(stacked, piece, ((1,), (1,))) for slot in slots for piece in slot]
    both = jnp.concatenate(both, axis=1).reshape(2, NY * 16, 2 * quarter)
    ours, theirs = jnp.where(first, both[0], both[1]), jnp.where(first, both[1], both[0])
    update = ours + across(theirs.astype(bf16)).astype(f32)
    done = (old.astype(f32) - step_scale * update).astype(bf16)
    for n, turn in enumerate((-1, 1)):
        part = done[:, n * quarter : (n + 1) * quarter]
        new_weights = put(new_weights, part, here_at[n], 1)
        new_weights = put(new_weights, along_y(part, turn), there_at[n], 1)
    return (new_weights[None], first_new, second_new)


def solution(mesh):
    return jax.shard_map(
        shards,
        mesh=mesh,
        in_specs=(
            P(("dp", "fsdp"), None),
            P(("dp", "fsdp"), "tensor", None),
            P("dp", None),
            P("tensor", ("dp", "fsdp"), None),
            P("tensor", ("dp", "fsdp"), None),
            P("tensor", ("dp", "fsdp"), None),
        ),
        out_specs=(
            P("tensor", "dp", None),
            P("tensor", ("dp", "fsdp"), None),
            P("tensor", ("dp", "fsdp"), None),
        ),
        check_vma=False,
    )
```

profile of v0, /device:TPU:1, one launch (start us, length us, event | category | flops | bytes accessed | tf_op | source)
XLA Modules:
  0.0 168.7 jit_solution(8242265142629268346)
XLA Ops:
  0.8 0.9 copy-done.6
  1.7 2.5 %collective-permute-start = (bf16[256,512]{1,0:T(8,128)(2,1)S(1)}, bf16[256,512]{1,0:T(8,128)(2,1)S(1)}, u32[]{:S(2)}, u32[]{:S(2)}) collective-permute-start(bf16[256,512]{1,0:T(8,128)(2,1)S(1)} %get-tuple-element.61), channel_id=1, source_target_pairs={{0,8},{8,16},{16,24},{24,32},{32,40},{40,48},{48,56},{56,0},{64,72... | collective-permute-start | bytes 786440 | tf_op jit(solution)/shard_map/ppermute | solution.py:27
  4.3 4.0 %collective-permute-start.1 = (bf16[256,512]{1,0:T(8,128)(2,1)S(1)}, bf16[256,512]{1,0:T(8,128)(2,1)S(1)}, u32[]{:S(2)}, u32[]{:S(2)}) collective-permute-start(bf16[256,512]{1,0:T(8,128)(2,1)S(1)} %get-tuple-element.61), channel_id=1, source_target_pairs={{0,56},{8,0},{16,8},{24,16},{32,24},{40,32},{48,40},{56,48},{64,12... | collective-permute-start | bytes 786440 | tf_op jit(solution)/shard_map/ppermute | solution.py:27
  8.5 0.6 pad_add_fusion.place_ref
  9.0 3.9 %shard_map.85 = (bf16[128,2048]{1,0:T(8,128)(2,1)}, bf16[128,2048]{1,0:T(8,128)(2,1)}, bf16[128,2048]{1,0:T(8,128)(2,1)}, bf16[128,2048]{1,0:T(8,128)(2,1)}, bf16[128,2048]{1,0:T(8,128)(2,1)}) custom-call(s32[2,5]{1,0:T(2,128)} %pad_add_fusion.place_ref, bf16[256,8192]{1,0:T(8,128)(2,1)} %act_ref.1), custom_call_target="tpu_custom_call" | custom-call | tf_op jit(solution)/shard_map/pallas_call | solution.py:90
  12.9 1.3 collective-permute-done
  14.2 2.7 %collective-permute-start.5 = (bf16[256,512]{1,0:T(8,128)(2,1)S(1)}, bf16[256,512]{1,0:T(8,128)(2,1)S(1)}, u32[]{:S(2)}, u32[]{:S(2)}) collective-permute-start(bf16[256,512]{1,0:T(8,128)(2,1)S(1)} %collective-permute-done.1), channel_id=1, source_target_pairs={{0,56},{8,0},{16,8},{24,16},{32,24},{40,32},{48,40},{56,48},{64,12... | collective-permute-start | bytes 786440 | tf_op jit(solution)/shard_map/ppermute | solution.py:27
  16.9 1.2 collective-permute-start.2
  18.1 2.5 %collective-permute-start.3 = (bf16[128,2048]{1,0:T(8,128)(2,1)}, bf16[128,2048]{1,0:T(8,128)(2,1)}, u32[]{:S(2)}, u32[]{:S(2)}) collective-permute-start(bf16[128,2048]{1,0:T(8,128)(2,1)} %get-tuple-element.35), channel_id=1, source_target_pairs={{0,128},{8,136},{16,144},{24,152},{32,160},{40,168},{48,176},{56,1... | collective-permute-start | bytes 1572872 | tf_op jit(solution)/shard_map/ppermute | solution.py:22
  20.6 1.2 collective-permute-start.4
  22.0 2.7 %collective-permute-start.6 = (bf16[256,512]{1,0:T(8,128)(2,1)S(1)}, bf16[256,512]{1,0:T(8,128)(2,1)S(1)}, u32[]{:S(2)}, u32[]{:S(2)}) collective-permute-start(bf16[256,512]{1,0:T(8,128)(2,1)S(1)} %collective-permute-done.5), channel_id=1, source_target_pairs={{0,56},{8,0},{16,8},{24,16},{32,24},{40,32},{48,40},{56,48},{64,12... | collective-permute-start | bytes 786440 | tf_op jit(solution)/shard_map/ppermute | solution.py:27
  24.8 4.1 %collective-permute-done.11 = bf16[256,512]{1,0:T(8,128)(2,1)S(1)} collective-permute-done((bf16[256,512]{1,0:T(8,128)(2,1)S(1)}, bf16[256,512]{1,0:T(8,128)(2,1)S(1)}, u32[]{:S(2)}, u32[]{:S(2)}) %collective-permute-start.11) | collective-permute-done | bytes 262176 | tf_op jit(solution)/shard_map/ppermute | solution.py:27
  28.8 0.7 slice.68
  29.5 0.7 slice.53
  30.2 2.7 %collective-permute-start.13 = (bf16[128,512]{1,0:T(8,128)(2,1)}, bf16[128,512]{1,0:T(8,128)(2,1)}, u32[]{:S(2)}, u32[]{:S(2)}) collective-permute-start(bf16[128,512]{1,0:T(8,128)(2,1)} %slice.53), channel_id=1, source_target_pairs={{0,56},{8,0},{16,8},{24,16},{32,24},{40,32},{48,40},{56,48},{64,12... | collective-permute-start | bytes 393224 | tf_op jit(solution)/shard_map/ppermute | solution.py:27
  32.9 1.5 copy.11
  34.5 1.4 collective-permute-start.7
  35.9 2.6 %collective-permute-start.8 = (bf16[32,16,256]{2,1,0:T(8,128)(2,1)S(1)}, bf16[32,16,256]{2,1,0:T(8,128)(2,1)S(1)}, u32[]{:S(2)}, u32[]{:S(2)}) collective-permute-start(bf16[32,16,256]{2,1,0:T(8,128)(2,1)S(1)} %get-tuple-element.70), channel_id=1, source_target_pairs={{0,4},{2,6},{4,0},{6,2},{1,5},{3,7},{5,1},{7,3},{8,12},{10,14},{12... | collective-permute-start | bytes 786440 | tf_op jit(solution)/shard_map/ppermute | solution.py:31
  38.5 1.1 collective-permute-start.9
  39.6 0.9 constant_dynamic-update-slice_fusion.8
  40.6 1.7 collective-permute-done.3
  42.3 0.7 collective-permute-start.17
  43.1 1.4 collective-permute-start.18
  44.4 2.0 %collective-permute-done.8 = bf16[32,16,256]{2,1,0:T(8,128)(2,1)S(1)} collective-permute-done((bf16[32,16,256]{2,1,0:T(8,128)(2,1)S(1)}, bf16[32,16,256]{2,1,0:T(8,128)(2,1)S(1)}, u32[]{:S(2)}, u32[]{:S(2)}) %collective-permute-start.8) | collective-permute-done | bytes 262176 | tf_op jit(solution)/shard_map/ppermute | solution.py:31
  46.4 5.0 %collective-permute-start.14 = (bf16[128,2048]{1,0:T(8,128)(2,1)}, bf16[128,2048]{1,0:T(8,128)(2,1)S(1)}, u32[]{:S(2)}, u32[]{:S(2)}) collective-permute-start(bf16[128,2048]{1,0:T(8,128)(2,1)} %collective-permute-done.2), channel_id=1, source_target_pairs={{0,1},{1,0},{2,3},{3,2},{4,5},{5,4},{6,7},{7,6},{8,9},{9,8},{10,11... | collective-permute-start | bytes 1572872 | tf_op jit(solution)/shard_map/ppermute | solution.py:35
  51.4 0.5 collective-permute-start.16
  52.1 2.7 %fusion.1 = f32[512,512]{1,0:T(8,128)S(1)} fusion(bf16[2048,512]{1,0:T(8,128)(2,1)S(1)} %constant_dynamic-update-slice_fusion.8, bf16[128,2048]{1,0:T(8,128)(2,1)} %collective-permute-done.4, bf16[128,2048]{1,0:T(8,128)(2,1)} %collective-permute-done.3, bf16[128,2048]{1,0:T(8,128)(2,1)} %collective-permute-done.2, bf16[128,2048]{1,0:T(8,128)(2,1)S(1)} %copy-done.8), kind=kOutput, calls=%fused_computation.4 | convolution fusion | flops 1082130432 | bytes 5242880 | tf_op jit(solution)/shard_map/dot_general | solution.py:70
  54.9 1.3 broadcast_select_fusion
  56.4 3.3 %collective-permute-start.19 = (bf16[256,512]{1,0:T(8,128)(2,1)S(1)}, bf16[256,512]{1,0:T(8,128)(2,1)S(1)}, u32[]{:S(2)}, u32[]{:S(2)}) collective-permute-start(bf16[256,512]{1,0:T(8,128)(2,1)S(1)} %get-tuple-element.66), channel_id=1, source_target_pairs={{0,192},{8,200},{16,208},{24,216},{32,224},{40,232},{48,240},{56,2... | collective-permute-start | bytes 786440 | tf_op jit(solution)/shard_map/ppermute | solution.py:22
  59.7 0.7 collective-permute-start.21
  60.3 1.3 slice.72
  61.6 3.1 %collective-permute-done.19 = bf16[256,512]{1,0:T(8,128)(2,1)S(1)} collective-permute-done((bf16[256,512]{1,0:T(8,128)(2,1)S(1)}, bf16[256,512]{1,0:T(8,128)(2,1)S(1)}, u32[]{:S(2)}, u32[]{:S(2)}) %collective-permute-start.19) | collective-permute-done | bytes 262176 | tf_op jit(solution)/shard_map/ppermute | solution.py:22
  64.7 1.8 %collective-permute-done.20 = bf16[256,512]{1,0:T(8,128)(2,1)S(1)} collective-permute-done((bf16[256,512]{1,0:T(8,128)(2,1)S(1)}, bf16[256,512]{1,0:T(8,128)(2,1)S(1)}, u32[]{:S(2)}, u32[]{:S(2)}) %collective-permute-start.20) | collective-permute-done | bytes 262176 | tf_op jit(solution)/shard_map/ppermute | solution.py:22
  66.5 7.1 %collective-permute-done.21 = bf16[256,512]{1,0:T(8,128)(2,1)S(1)} collective-permute-done((bf16[256,512]{1,0:T(8,128)(2,1)S(1)}, bf16[256,512]{1,0:T(8,128)(2,1)S(1)}, u32[]{:S(2)}, u32[]{:S(2)}) %collective-permute-start.21) | collective-permute-done | bytes 262176 | tf_op jit(solution)/shard_map/ppermute | solution.py:22
  73.8 2.1 %collective-permute-start.22 = (bf16[256,512]{1,0:T(8,128)(2,1)S(1)}, bf16[256,512]{1,0:T(8,128)(2,1)S(1)}, u32[]{:S(2)}, u32[]{:S(2)}) collective-permute-start(bf16[256,512]{1,0:T(8,128)(2,1)S(1)} %fusion.22), channel_id=1, source_target_pairs={{0,2},{2,4},{4,6},{6,0},{1,3},{3,5},{5,7},{7,1},{8,10},{10,12},{12... | collective-permute-start | bytes 786440 | tf_op jit(solution)/shard_map/ppermute | solution.py:31
  75.9 3.2 %collective-permute-start.23 = (bf16[256,512]{1,0:T(8,128)(2,1)S(1)}, bf16[256,512]{1,0:T(8,128)(2,1)S(1)}, u32[]{:S(2)}, u32[]{:S(2)}) collective-permute-start(bf16[256,512]{1,0:T(8,128)(2,1)S(1)} %fusion.22), channel_id=1, source_target_pairs={{0,4},{2,6},{4,0},{6,2},{1,5},{3,7},{5,1},{7,3},{8,12},{10,14},{12... | collective-permute-start | bytes 786440 | tf_op jit(solution)/shard_map/ppermute | solution.py:31
  79.1 2.0 %collective-permute-start.24 = (bf16[256,512]{1,0:T(8,128)(2,1)S(1)}, bf16[256,512]{1,0:T(8,128)(2,1)S(1)}, u32[]{:S(2)}, u32[]{:S(2)}) collective-permute-start(bf16[256,512]{1,0:T(8,128)(2,1)S(1)} %fusion.22), channel_id=1, source_target_pairs={{0,6},{2,0},{4,2},{6,4},{1,7},{3,1},{5,3},{7,5},{8,14},{10,8},{12,... | collective-permute-start | bytes 786440 | tf_op jit(solution)/shard_map/ppermute | solution.py:31
  81.2 9.2 %collective-permute-done.23 = bf16[256,512]{1,0:T(8,128)(2,1)S(1)} collective-permute-done((bf16[256,512]{1,0:T(8,128)(2,1)S(1)}, bf16[256,512]{1,0:T(8,128)(2,1)S(1)}, u32[]{:S(2)}, u32[]{:S(2)}) %collective-permute-start.23) | collective-permute-done | bytes 262176 | tf_op jit(solution)/shard_map/ppermute | solution.py:31
  91.0 2.2 %convolution_convert_fusion = bf16[1024,512]{1,0:T(8,128)(2,1)} fusion(bf16[1024,1024]{1,0:T(8,128)(2,1)S(1)} %bitcast.89, bf16[1024,512]{1,0:T(8,128)(2,1)S(1)} %pad_maximum_fusion.3), kind=kOutput, calls=%fused_computation.23 | convolution fusion | flops 1074266112 | bytes 4194304 | tf_op jit(solution)/shard_map/dot_general | solution.py:70
  93.3 7.6 %all-to-all-start = ((bf16[64,16,512]{2,1,0:T(8,128)(2,1)}), bf16[64,16,512]{2,1,0:T(8,128)(2,1)S(1)}, u32[]{:S(2)}, u32[]{:S(2)}) async-start(bf16[64,16,512]{2,1,0:T(8,128)(2,1)} %bitcast.90), calls=%async_computation | async-start | bytes 2097152 | tf_op jit(solution)/shard_map/all_to_all | solution.py:185
  100.9 1.8 %collective-permute-start.29 = (bf16[1536,512]{1,0:T(8,128)(2,1)S(1)}, bf16[1536,512]{1,0:T(8,128)(2,1)}, u32[]{:S(2)}, u32[]{:S(2)}) collective-permute-start(bf16[1536,512]{1,0:T(8,128)(2,1)S(1)} %copy-done), channel_id=1, source_target_pairs={{0,0},{66,2},{4,4},{70,6},{8,8},{74,10},{12,12},{78,14},{16,16},{8... | collective-permute-start | bytes 4718600 | tf_op jit(solution)/shard_map/ppermute | solution.py:45
  102.7 3.0 %collective-permute-start.30 = (bf16[1536,512]{1,0:T(8,128)(2,1)S(1)}, bf16[1536,512]{1,0:T(8,128)(2,1)}, u32[]{:S(2)}, u32[]{:S(2)}) collective-permute-start(bf16[1536,512]{1,0:T(8,128)(2,1)S(1)} %copy-done), channel_id=1, source_target_pairs={{128,0},{194,2},{132,4},{198,6},{136,8},{202,10},{140,12},{206,14}... | collective-permute-start | bytes 4718600 | tf_op jit(solution)/shard_map/ppermute | solution.py:45
  105.7 1.5 collective-permute-start.25
  107.2 1.5 collective-permute-start.27
  108.8 2.2 %collective-permute-start.26 = (bf16[16,4096]{1,0:T(8,128)(2,1)S(1)}, bf16[16,4096]{1,0:T(8,128)(2,1)}, u32[]{:S(2)}, u32[]{:S(2)}) collective-permute-start(bf16[16,4096]{1,0:T(8,128)(2,1)S(1)} %get-tuple-element.79), channel_id=1, source_target_pairs={{0,4},{2,6},{4,0},{6,2},{1,5},{3,7},{5,1},{7,3},{8,12},{10,14},{12... | collective-permute-start | bytes 393224 | tf_op jit(solution)/shard_map/ppermute | solution.py:31
  111.0 18.4 %all-to-all-done = bf16[64,16,512]{2,1,0:T(8,128)(2,1)S(1)} async-done(((bf16[64,16,512]{2,1,0:T(8,128)(2,1)}), bf16[64,16,512]{2,1,0:T(8,128)(2,1)S(1)}, u32[]{:S(2)}, u32[]{:S(2)}) %all-to-all-start) | async-done | bytes 1048608 | tf_op jit(solution)/shard_map/all_to_all | solution.py:185
  129.6 1.6 fusion.24
  131.2 0.7 broadcast_in_dim.28
  131.9 5.1 %all-to-all-start.1 = ((bf16[8,16,512]{2,1,0:T(8,128)(2,1)}), bf16[8,16,512]{2,1,0:T(8,128)(2,1)S(1)}, u32[]{:S(2)}, u32[]{:S(2)}) async-start(bf16[8,16,512]{2,1,0:T(8,128)(2,1)} %bitcast.32), calls=%async_computation.1 | async-start | bytes 262144 | tf_op jit(solution)/shard_map/all_to_all | solution.py:196
  137.0 0.9 constant_dynamic-update-slice_fusion.6
  137.9 4.8 %all-to-all-done.1 = bf16[8,16,512]{2,1,0:T(8,128)(2,1)S(1)} async-done(((bf16[8,16,512]{2,1,0:T(8,128)(2,1)}), bf16[8,16,512]{2,1,0:T(8,128)(2,1)S(1)}, u32[]{:S(2)}, u32[]{:S(2)}) %all-to-all-start.1) | async-done | bytes 131104 | tf_op jit(solution)/shard_map/all_to_all | solution.py:196
  142.6 1.3 fusion.30
  144.0 0.3 fusion.32
  144.3 2.0 %fusion.31 = f32[128,1536]{1,0:T(8,128)S(1)} fusion(bf16[128,512]{1,0:T(8,128)(2,1)S(1)} %bitcast.87, bf16[1536,512]{1,0:T(8,128)(2,1)} %collective-permute-done.29), kind=kOutput, calls=%fused_computation.87 | convolution fusion | flops 201326592 | bytes 2490368 | tf_op jit(solution)/shard_map/dot_general | solution.py:70
  146.4 3.4 %collective-permute-done.30 = bf16[1536,512]{1,0:T(8,128)(2,1)} collective-permute-done((bf16[1536,512]{1,0:T(8,128)(2,1)S(1)}, bf16[1536,512]{1,0:T(8,128)(2,1)}, u32[]{:S(2)}, u32[]{:S(2)}) %collective-permute-start.30) | collective-permute-done | bytes 1572896 | tf_op jit(solution)/shard_map/ppermute | solution.py:45
  149.7 2.0 %fusion.33 = f32[128,1536]{1,0:T(8,128)S(1)} fusion(bf16[128,512]{1,0:T(8,128)(2,1)S(1)} %bitcast.88, bf16[1536,512]{1,0:T(8,128)(2,1)} %collective-permute-done.30), kind=kOutput, calls=%fused_computation.89 | convolution fusion | flops 201326592 | bytes 2490368 | tf_op jit(solution)/shard_map/dot_general | solution.py:70
  152.0 1.4 collective-permute-start.31
  153.4 0.9 constant_dynamic-update-slice_fusion.5
  154.3 0.6 collective-permute-done.31
  154.9 0.3 subtract_convert_fusion
  155.2 4.1 %collective-permute-start.32 = (bf16[64,2048]{1,0:T(8,128)(2,1)S(1)}, bf16[64,2048]{1,0:T(8,128)(2,1)S(1)}, u32[]{:S(2)}, u32[]{:S(2)}) collective-permute-start(bf16[64,2048]{1,0:T(8,128)(2,1)S(1)} %get-tuple-element.74), channel_id=1, source_target_pairs={{0,6},{2,0},{4,2},{6,4},{1,7},{3,1},{5,3},{7,5},{8,14},{10,8},{12,... | collective-permute-start | bytes 786440 | tf_op jit(solution)/shard_map/ppermute | solution.py:31
  159.4 5.3 %collective-permute-done.32 = bf16[64,2048]{1,0:T(8,128)(2,1)S(1)} collective-permute-done((bf16[64,2048]{1,0:T(8,128)(2,1)S(1)}, bf16[64,2048]{1,0:T(8,128)(2,1)S(1)}, u32[]{:S(2)}, u32[]{:S(2)}) %collective-permute-start.32) | collective-permute-done | bytes 262176 | tf_op jit(solution)/shard_map/ppermute | solution.py:31
  164.8 2.9 %collective-permute-done.33 = bf16[64,2048]{1,0:T(8,128)(2,1)S(1)} collective-permute-done((bf16[64,2048]{1,0:T(8,128)(2,1)S(1)}, bf16[64,2048]{1,0:T(8,128)(2,1)S(1)}, u32[]{:S(2)}, u32[]{:S(2)}) %collective-permute-start.33) | collective-permute-done | bytes 262176 | tf_op jit(solution)/shard_map/ppermute | solution.py:31
  167.8 1.0 copy-done.1
  (87 shorter events, 3.1 us)
Async XLA Ops:
  0.6 1.0 copy-start.6
  1.7 12.5 %collective-permute-start = (bf16[256,512]{1,0:T(8,128)(2,1)S(1)}, bf16[256,512]{1,0:T(8,128)(2,1)S(1)}, u32[]{:S(2)}, u32[]{:S(2)}) collective-permute-start(bf16[256,512]{1,0:T(8,128)(2,1)S(1)} %get-tuple-element.61), channel_id=1, source_target_pairs={{0,8},{8,16},{16,24},{24,32},{32,40},{40,48},{48,56},{56,0},{64,72... | collective-permute-start | bytes 786440 | tf_op jit(solution)/shard_map/ppermute | solution.py:27
  4.3 10.0 %collective-permute-start.1 = (bf16[256,512]{1,0:T(8,128)(2,1)S(1)}, bf16[256,512]{1,0:T(8,128)(2,1)S(1)}, u32[]{:S(2)}, u32[]{:S(2)}) collective-permute-start(bf16[256,512]{1,0:T(8,128)(2,1)S(1)} %get-tuple-element.61), channel_id=1, source_target_pairs={{0,56},{8,0},{16,8},{24,16},{32,24},{40,32},{48,40},{56,48},{64,12... | collective-permute-start | bytes 786440 | tf_op jit(solution)/shard_map/ppermute | solution.py:27
  14.2 7.8 %collective-permute-start.10 = (bf16[256,512]{1,0:T(8,128)(2,1)S(1)}, bf16[256,512]{1,0:T(8,128)(2,1)S(1)}, u32[]{:S(2)}, u32[]{:S(2)}) collective-permute-start(bf16[256,512]{1,0:T(8,128)(2,1)S(1)} %collective-permute-done), channel_id=1, source_target_pairs={{0,8},{8,16},{16,24},{24,32},{32,40},{40,48},{48,56},{56,0},{64,72... | collective-permute-start | bytes 786440 | tf_op jit(solution)/shard_map/ppermute | solution.py:27
  14.2 7.8 %collective-permute-start.5 = (bf16[256,512]{1,0:T(8,128)(2,1)S(1)}, bf16[256,512]{1,0:T(8,128)(2,1)S(1)}, u32[]{:S(2)}, u32[]{:S(2)}) collective-permute-start(bf16[256,512]{1,0:T(8,128)(2,1)S(1)} %collective-permute-done.1), channel_id=1, source_target_pairs={{0,56},{8,0},{16,8},{24,16},{32,24},{40,32},{48,40},{56,48},{64,12... | collective-permute-start | bytes 786440 | tf_op jit(solution)/shard_map/ppermute | solution.py:27
  16.9 17.6 %collective-permute-start.2 = (bf16[128,2048]{1,0:T(8,128)(2,1)}, bf16[128,2048]{1,0:T(8,128)(2,1)}, u32[]{:S(2)}, u32[]{:S(2)}) collective-permute-start(bf16[128,2048]{1,0:T(8,128)(2,1)} %get-tuple-element.34), channel_id=1, source_target_pairs={{0,64},{8,72},{16,80},{24,88},{32,96},{40,104},{48,112},{56,120},{... | collective-permute-start | bytes 1572872 | tf_op jit(solution)/shard_map/ppermute | solution.py:22
  18.1 24.2 %collective-permute-start.3 = (bf16[128,2048]{1,0:T(8,128)(2,1)}, bf16[128,2048]{1,0:T(8,128)(2,1)}, u32[]{:S(2)}, u32[]{:S(2)}) collective-permute-start(bf16[128,2048]{1,0:T(8,128)(2,1)} %get-tuple-element.35), channel_id=1, source_target_pairs={{0,128},{8,136},{16,144},{24,152},{32,160},{40,168},{48,176},{56,1... | collective-permute-start | bytes 1572872 | tf_op jit(solution)/shard_map/ppermute | solution.py:22
  20.6 22.5 %collective-permute-start.4 = (bf16[128,2048]{1,0:T(8,128)(2,1)}, bf16[128,2048]{1,0:T(8,128)(2,1)}, u32[]{:S(2)}, u32[]{:S(2)}) collective-permute-start(bf16[128,2048]{1,0:T(8,128)(2,1)} %get-tuple-element.36), channel_id=1, source_target_pairs={{0,192},{8,200},{16,208},{24,216},{32,224},{40,232},{48,240},{56,2... | collective-permute-start | bytes 1572872 | tf_op jit(solution)/shard_map/ppermute | solution.py:22
  22.0 6.8 %collective-permute-start.11 = (bf16[256,512]{1,0:T(8,128)(2,1)S(1)}, bf16[256,512]{1,0:T(8,128)(2,1)S(1)}, u32[]{:S(2)}, u32[]{:S(2)}) collective-permute-start(bf16[256,512]{1,0:T(8,128)(2,1)S(1)} %collective-permute-done.10), channel_id=1, source_target_pairs={{0,8},{8,16},{16,24},{24,32},{32,40},{40,48},{48,56},{56,0},{64,72... | collective-permute-start | bytes 786440 | tf_op jit(solution)/shard_map/ppermute | solution.py:27
  22.0 7.5 %collective-permute-start.6 = (bf16[256,512]{1,0:T(8,128)(2,1)S(1)}, bf16[256,512]{1,0:T(8,128)(2,1)S(1)}, u32[]{:S(2)}, u32[]{:S(2)}) collective-permute-start(bf16[256,512]{1,0:T(8,128)(2,1)S(1)} %collective-permute-done.5), channel_id=1, source_target_pairs={{0,56},{8,0},{16,8},{24,16},{32,24},{40,32},{48,40},{56,48},{64,12... | collective-permute-start | bytes 786440 | tf_op jit(solution)/shard_map/ppermute | solution.py:27
  29.5 6.4 %collective-permute-start.12 = (bf16[128,512]{1,0:T(8,128)(2,1)}, bf16[128,512]{1,0:T(8,128)(2,1)S(1)}, u32[]{:S(2)}, u32[]{:S(2)}) collective-permute-start(bf16[128,512]{1,0:T(8,128)(2,1)} %slice.68), channel_id=1, source_target_pairs={{0,8},{8,16},{16,24},{24,32},{32,40},{40,48},{48,56},{56,0},{64,72... | collective-permute-start | bytes 393224 | tf_op jit(solution)/shard_map/ppermute | solution.py:27
  30.2 8.3 %collective-permute-start.13 = (bf16[128,512]{1,0:T(8,128)(2,1)}, bf16[128,512]{1,0:T(8,128)(2,1)}, u32[]{:S(2)}, u32[]{:S(2)}) collective-permute-start(bf16[128,512]{1,0:T(8,128)(2,1)} %slice.53), channel_id=1, source_target_pairs={{0,56},{8,0},{16,8},{24,16},{32,24},{40,32},{48,40},{56,48},{64,12... | collective-permute-start | bytes 393224 | tf_op jit(solution)/shard_map/ppermute | solution.py:27
  34.5 9.9 %collective-permute-start.7 = (bf16[32,16,256]{2,1,0:T(8,128)(2,1)S(1)}, bf16[32,16,256]{2,1,0:T(8,128)(2,1)S(1)}, u32[]{:S(2)}, u32[]{:S(2)}) collective-permute-start(bf16[32,16,256]{2,1,0:T(8,128)(2,1)S(1)} %get-tuple-element.71), channel_id=1, source_target_pairs={{0,2},{2,4},{4,6},{6,0},{1,3},{3,5},{5,7},{7,1},{8,10},{10,12},{12... | collective-permute-start | bytes 786440 | tf_op jit(solution)/shard_map/ppermute | solution.py:31
  35.9 10.5 %collective-permute-start.8 = (bf16[32,16,256]{2,1,0:T(8,128)(2,1)S(1)}, bf16[32,16,256]{2,1,0:T(8,128)(2,1)S(1)}, u32[]{:S(2)}, u32[]{:S(2)}) collective-permute-start(bf16[32,16,256]{2,1,0:T(8,128)(2,1)S(1)} %get-tuple-element.70), channel_id=1, source_target_pairs={{0,4},{2,6},{4,0},{6,2},{1,5},{3,7},{5,1},{7,3},{8,12},{10,14},{12... | collective-permute-start | bytes 786440 | tf_op jit(solution)/shard_map/ppermute | solution.py:31
  38.5 13.5 %copy-start.8 = (bf16[128,2048]{1,0:T(8,128)(2,1)S(1)}, bf16[128,2048]{1,0:T(8,128)(2,1)}, u32[]{:S(2)}) copy-start(bf16[128,2048]{1,0:T(8,128)(2,1)} %get-tuple-element.40) | copy-start | bytes 1572868
  38.5 7.9 %collective-permute-start.9 = (bf16[32,16,256]{2,1,0:T(8,128)(2,1)S(1)}, bf16[32,16,256]{2,1,0:T(8,128)(2,1)S(1)}, u32[]{:S(2)}, u32[]{:S(2)}) collective-permute-start(bf16[32,16,256]{2,1,0:T(8,128)(2,1)S(1)} %get-tuple-element.69), channel_id=1, source_target_pairs={{0,6},{2,0},{4,2},{6,4},{1,7},{3,1},{5,3},{7,5},{8,14},{10,8},{12,... | collective-permute-start | bytes 786440 | tf_op jit(solution)/shard_map/ppermute | solution.py:31
  42.3 14.0 %collective-permute-start.17 = (bf16[512,512]{1,0:T(8,128)(2,1)S(1)}, bf16[512,512]{1,0:T(8,128)(2,1)S(1)}, u32[]{:S(2)}, u32[]{:S(2)}) collective-permute-start(bf16[512,512]{1,0:T(8,128)(2,1)S(1)} %slice.71), channel_id=1, source_target_pairs={{0,0},{66,2},{4,4},{70,6},{8,8},{74,10},{12,12},{78,14},{16,16},{8... | collective-permute-start | bytes 1572872 | tf_op jit(solution)/shard_map/ppermute | solution.py:45
  43.1 13.2 %collective-permute-start.18 = (bf16[512,512]{1,0:T(8,128)(2,1)S(1)}, bf16[512,512]{1,0:T(8,128)(2,1)S(1)}, u32[]{:S(2)}, u32[]{:S(2)}) collective-permute-start(bf16[512,512]{1,0:T(8,128)(2,1)S(1)} %slice.71), channel_id=1, source_target_pairs={{128,0},{194,2},{132,4},{198,6},{136,8},{202,10},{140,12},{206,14}... | collective-permute-start | bytes 1572872 | tf_op jit(solution)/shard_map/ppermute | solution.py:45
  46.4 8.3 %collective-permute-start.14 = (bf16[128,2048]{1,0:T(8,128)(2,1)}, bf16[128,2048]{1,0:T(8,128)(2,1)S(1)}, u32[]{:S(2)}, u32[]{:S(2)}) collective-permute-start(bf16[128,2048]{1,0:T(8,128)(2,1)} %collective-permute-done.2), channel_id=1, source_target_pairs={{0,1},{1,0},{2,3},{3,2},{4,5},{5,4},{6,7},{7,6},{8,9},{9,8},{10,11... | collective-permute-start | bytes 1572872 | tf_op jit(solution)/shard_map/ppermute | solution.py:35
  51.4 3.4 %collective-permute-start.15 = (bf16[128,2048]{1,0:T(8,128)(2,1)}, bf16[128,2048]{1,0:T(8,128)(2,1)S(1)}, u32[]{:S(2)}, u32[]{:S(2)}) collective-permute-start(bf16[128,2048]{1,0:T(8,128)(2,1)} %collective-permute-done.3), channel_id=1, source_target_pairs={{0,1},{1,0},{2,3},{3,2},{4,5},{5,4},{6,7},{7,6},{8,9},{9,8},{10,11... | collective-permute-start | bytes 1572872 | tf_op jit(solution)/shard_map/ppermute | solution.py:35
  51.4 3.5 %collective-permute-start.16 = (bf16[128,2048]{1,0:T(8,128)(2,1)}, bf16[128,2048]{1,0:T(8,128)(2,1)S(1)}, u32[]{:S(2)}, u32[]{:S(2)}) collective-permute-start(bf16[128,2048]{1,0:T(8,128)(2,1)} %collective-permute-done.4), channel_id=1, source_target_pairs={{0,1},{1,0},{2,3},{3,2},{4,5},{5,4},{6,7},{7,6},{8,9},{9,8},{10,11... | collective-permute-start | bytes 1572872 | tf_op jit(solution)/shard_map/ppermute | solution.py:35
  52.0 2.8 %copy-start.7 = (bf16[128,2048]{1,0:T(8,128)(2,1)S(1)}, bf16[128,2048]{1,0:T(8,128)(2,1)}, u32[]{:S(2)}) copy-start(bf16[128,2048]{1,0:T(8,128)(2,1)} %get-tuple-element.45) | copy-start | bytes 1572868
  54.7 35.8 %collective-permute-start.28 = (bf16[32,16,1024]{2,1,0:T(8,128)(2,1)S(1)}, bf16[32,16,1024]{2,1,0:T(8,128)(2,1)S(1)}, u32[]{:S(2)}, u32[]{:S(2)}) collective-permute-start(bf16[32,16,1024]{2,1,0:T(8,128)(2,1)S(1)} %constant_dynamic-update-slice_fusion), channel_id=1, source_target_pairs={{0,1},{1,0},{2,3},{3,2},{4,5},{5,4},{6,7},{7,6},{8,9},{9,8},{10,11... | collective-permute-start | bytes 3145736 | tf_op jit(solution)/shard_map/ppermute | solution.py:35
  56.3 5.3 %copy-start.2 = (bf16[512,512]{1,0:T(8,128)(2,1)}, bf16[512,512]{1,0:T(8,128)(2,1)S(1)}, u32[]{:S(2)}) copy-start(bf16[512,512]{1,0:T(8,128)(2,1)S(1)} %collective-permute-done.17) | copy-start | bytes 1572868
  56.3 5.3 %copy-start.3 = (bf16[512,512]{1,0:T(8,128)(2,1)}, bf16[512,512]{1,0:T(8,128)(2,1)S(1)}, u32[]{:S(2)}) copy-start(bf16[512,512]{1,0:T(8,128)(2,1)S(1)} %collective-permute-done.18) | copy-start | bytes 1572868
  56.4 8.3 %collective-permute-start.19 = (bf16[256,512]{1,0:T(8,128)(2,1)S(1)}, bf16[256,512]{1,0:T(8,128)(2,1)S(1)}, u32[]{:S(2)}, u32[]{:S(2)}) collective-permute-start(bf16[256,512]{1,0:T(8,128)(2,1)S(1)} %get-tuple-element.66), channel_id=1, source_target_pairs={{0,192},{8,200},{16,208},{24,216},{32,224},{40,232},{48,240},{56,2... | collective-permute-start | bytes 786440 | tf_op jit(solution)/shard_map/ppermute | solution.py:22
  59.7 6.8 %collective-permute-start.20 = (bf16[256,512]{1,0:T(8,128)(2,1)S(1)}, bf16[256,512]{1,0:T(8,128)(2,1)S(1)}, u32[]{:S(2)}, u32[]{:S(2)}) collective-permute-start(bf16[256,512]{1,0:T(8,128)(2,1)S(1)} %get-tuple-element.68), channel_id=1, source_target_pairs={{0,128},{8,136},{16,144},{24,152},{32,160},{40,168},{48,176},{56,1... | collective-permute-start | bytes 786440 | tf_op jit(solution)/shard_map/ppermute | solution.py:22
  59.7 13.9 %collective-permute-start.21 = (bf16[256,512]{1,0:T(8,128)(2,1)S(1)}, bf16[256,512]{1,0:T(8,128)(2,1)S(1)}, u32[]{:S(2)}, u32[]{:S(2)}) collective-permute-start(bf16[256,512]{1,0:T(8,128)(2,1)S(1)} %get-tuple-element.67), channel_id=1, source_target_pairs={{0,64},{8,72},{16,80},{24,88},{32,96},{40,104},{48,112},{56,120},{... | collective-permute-start | bytes 786440 | tf_op jit(solution)/shard_map/ppermute | solution.py:22
  73.8 7.5 %collective-permute-start.22 = (bf16[256,512]{1,0:T(8,128)(2,1)S(1)}, bf16[256,512]{1,0:T(8,128)(2,1)S(1)}, u32[]{:S(2)}, u32[]{:S(2)}) collective-permute-start(bf16[256,512]{1,0:T(8,128)(2,1)S(1)} %fusion.22), channel_id=1, source_target_pairs={{0,2},{2,4},{4,6},{6,0},{1,3},{3,5},{5,7},{7,1},{8,10},{10,12},{12... | collective-permute-start | bytes 786440 | tf_op jit(solution)/shard_map/ppermute | solution.py:31
  75.9 14.6 %collective-permute-start.23 = (bf16[256,512]{1,0:T(8,128)(2,1)S(1)}, bf16[256,512]{1,0:T(8,128)(2,1)S(1)}, u32[]{:S(2)}, u32[]{:S(2)}) collective-permute-start(bf16[256,512]{1,0:T(8,128)(2,1)S(1)} %fusion.22), channel_id=1, source_target_pairs={{0,4},{2,6},{4,0},{6,2},{1,5},{3,7},{5,1},{7,3},{8,12},{10,14},{12... | collective-permute-start | bytes 786440 | tf_op jit(solution)/shard_map/ppermute | solution.py:31
  79.1 11.4 %collective-permute-start.24 = (bf16[256,512]{1,0:T(8,128)(2,1)S(1)}, bf16[256,512]{1,0:T(8,128)(2,1)S(1)}, u32[]{:S(2)}, u32[]{:S(2)}) collective-permute-start(bf16[256,512]{1,0:T(8,128)(2,1)S(1)} %fusion.22), channel_id=1, source_target_pairs={{0,6},{2,0},{4,2},{6,4},{1,7},{3,1},{5,3},{7,5},{8,14},{10,8},{12,... | collective-permute-start | bytes 786440 | tf_op jit(solution)/shard_map/ppermute | solution.py:31
  93.3 7.6 %copy-start = (bf16[1536,512]{1,0:T(8,128)(2,1)S(1)}, bf16[1536,512]{1,0:T(8,128)(2,1)}, u32[]{:S(2)}) copy-start(bf16[1536,512]{1,0:T(8,128)(2,1)} %slice.72) | copy-start | bytes 4718596
  93.3 12.4 %copy-start.5 = (bf16[1,16,8192]{2,1,0:T(8,128)(2,1)S(1)}, bf16[1,16,8192]{2,1,0:T(8,128)(2,1)}, u32[]{:S(2)}) copy-start(bf16[1,16,8192]{2,1,0:T(8,128)(2,1)} %param.9) | copy-start | bytes 786436
  93.3 36.1 %all-to-all-start = ((bf16[64,16,512]{2,1,0:T(8,128)(2,1)}), bf16[64,16,512]{2,1,0:T(8,128)(2,1)S(1)}, u32[]{:S(2)}, u32[]{:S(2)}) async-start(bf16[64,16,512]{2,1,0:T(8,128)(2,1)} %bitcast.90), calls=%async_computation | async-start | bytes 2097152 | tf_op jit(solution)/shard_map/all_to_all | solution.py:185
  100.9 43.4 %collective-permute-start.29 = (bf16[1536,512]{1,0:T(8,128)(2,1)S(1)}, bf16[1536,512]{1,0:T(8,128)(2,1)}, u32[]{:S(2)}, u32[]{:S(2)}) collective-permute-start(bf16[1536,512]{1,0:T(8,128)(2,1)S(1)} %copy-done), channel_id=1, source_target_pairs={{0,0},{66,2},{4,4},{70,6},{8,8},{74,10},{12,12},{78,14},{16,16},{8... | collective-permute-start | bytes 4718600 | tf_op jit(solution)/shard_map/ppermute | solution.py:45
  102.7 47.0 %collective-permute-start.30 = (bf16[1536,512]{1,0:T(8,128)(2,1)S(1)}, bf16[1536,512]{1,0:T(8,128)(2,1)}, u32[]{:S(2)}, u32[]{:S(2)}) collective-permute-start(bf16[1536,512]{1,0:T(8,128)(2,1)S(1)} %copy-done), channel_id=1, source_target_pairs={{128,0},{194,2},{132,4},{198,6},{136,8},{202,10},{140,12},{206,14}... | collective-permute-start | bytes 4718600 | tf_op jit(solution)/shard_map/ppermute | solution.py:45
  105.7 31.2 %collective-permute-start.25 = (bf16[16,4096]{1,0:T(8,128)(2,1)S(1)}, bf16[16,4096]{1,0:T(8,128)(2,1)}, u32[]{:S(2)}, u32[]{:S(2)}) collective-permute-start(bf16[16,4096]{1,0:T(8,128)(2,1)S(1)} %pad_maximum_fusion.5), channel_id=1, source_target_pairs={{0,2},{2,4},{4,6},{6,0},{1,3},{3,5},{5,7},{7,1},{8,10},{10,12},{12... | collective-permute-start | bytes 393224 | tf_op jit(solution)/shard_map/ppermute | solution.py:31
  107.2 47.1 %collective-permute-start.27 = (bf16[16,4096]{1,0:T(8,128)(2,1)S(1)}, bf16[16,4096]{1,0:T(8,128)(2,1)S(1)}, u32[]{:S(2)}, u32[]{:S(2)}) collective-permute-start(bf16[16,4096]{1,0:T(8,128)(2,1)S(1)} %pad_maximum_fusion.5), channel_id=1, source_target_pairs={{0,6},{2,0},{4,2},{6,4},{1,7},{3,1},{5,3},{7,5},{8,14},{10,8},{12,... | collective-permute-start | bytes 393224 | tf_op jit(solution)/shard_map/ppermute | solution.py:31
  108.8 44.6 %collective-permute-start.26 = (bf16[16,4096]{1,0:T(8,128)(2,1)S(1)}, bf16[16,4096]{1,0:T(8,128)(2,1)}, u32[]{:S(2)}, u32[]{:S(2)}) collective-permute-start(bf16[16,4096]{1,0:T(8,128)(2,1)S(1)} %get-tuple-element.79), channel_id=1, source_target_pairs={{0,4},{2,6},{4,0},{6,2},{1,5},{3,7},{5,1},{7,3},{8,12},{10,14},{12... | collective-permute-start | bytes 393224 | tf_op jit(solution)/shard_map/ppermute | solution.py:31
  129.5 14.4 %copy-start.4 = (bf16[512,512]{1,0:T(8,128)(2,1)S(1)}, bf16[512,512]{1,0:T(8,128)(2,1)}, u32[]{:S(2)}) copy-start(bf16[512,512]{1,0:T(8,128)(2,1)} %copy-done.3) | copy-start | bytes 1572868
  131.9 10.8 %all-to-all-start.1 = ((bf16[8,16,512]{2,1,0:T(8,128)(2,1)}), bf16[8,16,512]{2,1,0:T(8,128)(2,1)S(1)}, u32[]{:S(2)}, u32[]{:S(2)}) async-start(bf16[8,16,512]{2,1,0:T(8,128)(2,1)} %bitcast.32), calls=%async_computation.1 | async-start | bytes 262144 | tf_op jit(solution)/shard_map/all_to_all | solution.py:196
  152.0 2.9 %collective-permute-start.31 = (bf16[64,4096]{1,0:T(8,128)(2,1)S(1)}, bf16[64,4096]{1,0:T(8,128)(2,1)S(1)}, u32[]{:S(2)}, u32[]{:S(2)}) collective-permute-start(bf16[64,4096]{1,0:T(8,128)(2,1)S(1)} %select_convert_fusion), channel_id=1, source_target_pairs={{0,1},{1,0},{2,3},{3,2},{4,5},{5,4},{6,7},{7,6},{8,9},{9,8},{10,11... | collective-permute-start | bytes 1572872 | tf_op jit(solution)/shard_map/ppermute | solution.py:35
  155.2 9.5 %collective-permute-start.32 = (bf16[64,2048]{1,0:T(8,128)(2,1)S(1)}, bf16[64,2048]{1,0:T(8,128)(2,1)S(1)}, u32[]{:S(2)}, u32[]{:S(2)}) collective-permute-start(bf16[64,2048]{1,0:T(8,128)(2,1)S(1)} %get-tuple-element.74), channel_id=1, source_target_pairs={{0,6},{2,0},{4,2},{6,4},{1,7},{3,1},{5,3},{7,5},{8,14},{10,8},{12,... | collective-permute-start | bytes 786440 | tf_op jit(solution)/shard_map/ppermute | solution.py:31
  159.3 8.4 %collective-permute-start.33 = (bf16[64,2048]{1,0:T(8,128)(2,1)S(1)}, bf16[64,2048]{1,0:T(8,128)(2,1)S(1)}, u32[]{:S(2)}, u32[]{:S(2)}) collective-permute-start(bf16[64,2048]{1,0:T(8,128)(2,1)S(1)} %get-tuple-element.73), channel_id=1, source_target_pairs={{0,2},{2,4},{4,6},{6,0},{1,3},{3,5},{5,7},{7,1},{8,10},{10,12},{12... | collective-permute-start | bytes 786440 | tf_op jit(solution)/shard_map/ppermute | solution.py:31
  167.7 1.0 copy-start.1
where the time goes:
time: 169 us
  starting transfers between devices  71.4 us (42%)
  waiting for transfers between devices  66.1 us (39%)
  matrix products  11.9 us (7%)
  local copies, waits for them, and re-layouts  10.7 us (6%)
  Pallas kernels  3.89 us (2%)
  other arithmetic  3.58 us (2%)
    ppermute x11, starting transfers between devices, along_y(): return lax.ppermute(value, 'fsdp', [(y, (y + d) % NY) for y in range(NY)])  21.6 us
    ppermute x11, waiting for transfers between devices, along_y(): return lax.ppermute(value, 'fsdp', [(y, (y + d) % NY) for y in range(NY)])  19.6 us
    all_to_all x1, waiting for transfers between devices, shards(): lax.all_to_all(projected, ('dp', 'tensor'), split_axis=0, concat_axis=0,...  18.4 us
    ppermute x8, starting transfers between devices, along_z(): return lax.ppermute(value, 'dp', pairs)  14.6 us
    ppermute x6, waiting for transfers between devices, along_x(): return lax.ppermute(value, 'dp', pairs)  13.8 us
    dot_general x7, matrix products, dot(): lax.dot_general(a, b, ((dims[0], dims[1]), ((), ())), preferred_element_t...  11.9 us
    ppermute x6, starting transfers between devices, along_x(): return lax.ppermute(value, 'dp', pairs)  8.76 us
    all_to_all x1, starting transfers between devices, shards(): lax.all_to_all(projected, ('dp', 'tensor'), split_axis=0, concat_axis=0,...  7.55 us
  transfers between devices with their start and end apart: 36, of which 17 were waited for; matrix products, arithmetic and copies ran while one was open for 12% of the time, Pallas kernels for 2%

commit v1 on v0

v1 whole, which is shorter than its diff:
```python
import jax
import jax.numpy as jnp
from jax import lax
from jax.experimental import pallas as pl
from jax.experimental.pallas import tpu as pltpu
from jax.sharding import PartitionSpec as P

STEP = 10

beta_one = 0.9
beta_two = 0.999
epsilon = 1e-08
step_scale = 0.25

NX, NZ, NY = 4, 8, 4
FAR = (2, 1, 3)
f32 = jnp.float32
bf16 = jnp.bfloat16


def along_x(value, d):
    pairs = [(x * NZ + z, (x + d) % NX * NZ + z) for x in range(NX) for z in range(NZ)]
    return lax.ppermute(value, "dp", pairs)


def along_z(value, d):
    pairs = [(x * NZ + z, x * NZ + (z + d) % NZ) for x in range(NX) for z in range(NZ)]
    return lax.ppermute(value, "dp", pairs)


def along_y(value, d):
    return lax.ppermute(value, "fsdp", [(y, (y + d) % NY) for y in range(NY)])


def across(value):
    return lax.ppermute(value, "tensor", [(0, 1), (1, 0)])


def rows(array, start, size):
    return lax.dynamic_slice_in_dim(array, start, size, axis=0)


def columns(array, start, size):
    return lax.dynamic_slice_in_dim(array, start, size, axis=1)


def put(whole, part, start, axis):
    return lax.dynamic_update_slice_in_dim(whole, part, start, axis=axis)


def gather_y(block, y):
    n = block.shape[0]
    whole = jnp.zeros((NY * n, block.shape[1]), block.dtype)
    whole = put(whole, block, y * n, 0)
    for d in range(1, NY):
        whole = put(whole, along_y(block, d), lax.rem(y + NY - d, NY) * n, 0)
    return whole


def dot(a, b, dims):
    return lax.dot_general(a, b, ((dims[0], dims[1]), ((), ())), preferred_element_type=f32)


def cut(activations, places):
    pair, quarter = activations.shape[0] // 2, activations.shape[1] // NX

    def kernel(act_ref, *refs):
        outs, sems = refs[:-1], refs[-1]
        core, x = lax.axis_index("tensor"), lax.div(lax.axis_index("dp"), NZ)
        copies = []
        for n, (out, (other, d)) in enumerate(zip(outs, places)):
            row = pl.multiple_of((1 - core if other else core) * pair, pair)
            col = pl.multiple_of(lax.rem(x + d, NX) * quarter, quarter)
            source = act_ref.at[pl.ds(row, pair), pl.ds(col, quarter)]
            copies.append(pltpu.make_async_copy(source, out, sems.at[n]))
        for copy in copies:
            copy.start()
        for copy in copies:
            copy.wait()

    shape = jax.ShapeDtypeStruct((pair, quarter), activations.dtype)
    return pl.pallas_call(
        kernel,
        out_shape=[shape] * len(places),
        in_specs=[pl.BlockSpec(memory_space=pl.ANY)],
        out_specs=[pl.BlockSpec(memory_space=pltpu.VMEM)] * len(places),
        scratch_shapes=[pltpu.SemaphoreType.DMA((len(places),))],
    )(activations)


def cut_weights(weights):
    count, width = weights.shape
    quarter, slab = width // NX, width // NX // NY

    def kernel(weights_ref, *refs):
        outs, sems = refs[:-1], refs[-1]
        x, y = lax.div(lax.axis_index("dp"), NZ), lax.axis_index("fsdp")
        copies = []
        for n, (out, e) in enumerate(zip(outs, (0,) + FAR)):
            for k, d in enumerate((0,) + FAR):
                col = lax.rem(x + NX - d, NX) * quarter + lax.rem(y + e, NY) * slab
                source = weights_ref.at[:, pl.ds(pl.multiple_of(col, slab), slab)]
                target = out.at[:, pl.ds(k * slab, slab)]
                copies.append(pltpu.make_async_copy(source, target, sems.at[n, k]))
        for copy in copies:
            copy.start()
        for copy in copies:
            copy.wait()

    shape = jax.ShapeDtypeStruct((count, quarter), weights.dtype)
    return pl.pallas_call(
        kernel,
        out_shape=[shape] * NY,
        in_specs=[pl.BlockSpec(memory_space=pl.ANY)],
        out_specs=[pl.BlockSpec(memory_space=pltpu.VMEM)] * NY,
        scratch_shapes=[pltpu.SemaphoreType.DMA((NY, NX))],
    )(weights)


def place(parts):
    count, quarter = parts[0].shape
    slab = quarter // NY

    def kernel(*refs):
        ins, out = refs[:-1], refs[-1]
        x, y = lax.div(lax.axis_index("dp"), NZ), lax.axis_index("fsdp")
        for part, e in zip(ins, (0,) + FAR):
            for k, d in enumerate((0,) + FAR):
                col = lax.rem(x + NX - d, NX) * quarter + lax.rem(y + NY - e, NY) * slab
                out[:, pl.ds(pl.multiple_of(col, slab), slab)] = part[:, k * slab : (k + 1) * slab]

    return pl.pallas_call(
        kernel,
        out_shape=jax.ShapeDtypeStruct((count, quarter * NX), parts[0].dtype),
        in_specs=[pl.BlockSpec(memory_space=pltpu.VMEM)] * NY,
        out_specs=pl.BlockSpec(memory_space=pltpu.VMEM),
    )(*parts)


def shards(activations, out_grads, basis, weights, first_moment, second_moment):
    dp, y, core = lax.axis_index("dp"), lax.axis_index("fsdp"), lax.axis_index("tensor")
    x, z = lax.div(dp, NZ), lax.rem(dp, NZ)
    tokens, width = activations.shape
    rank = basis.shape[1]
    half, quarter, pair = rank // 2, width // NX, tokens // 2

    mine = columns(basis, core * half, half)
    n = mine.shape[0]
    ahead, back = along_z(mine, 1), along_z(mine, -1)
    here, there, *leaving = cut(activations, [(False, 0), (True, 0)] + [(False, d) for d in FAR])
    ahead, back, leaving = lax.optimization_barrier((ahead, back, leaving))
    own = [along_x(piece, d) for d, piece in zip(FAR, leaving)]

    held = jnp.zeros((NZ * n, half), bf16)
    held = put(held, mine, z * n, 0)
    for s in range(1, NZ // 2):
        if s > 1:
            ahead, back = along_z(ahead, 1), along_z(back, -1)
        held = put(held, ahead, lax.rem(z + NZ - s, NZ) * n, 0)
        held = put(held, back, lax.rem(z + s, NZ) * n, 0)
    back, out_grads = lax.optimization_barrier((back, out_grads))
    turned = out_grads[:, 0, :].T.reshape(NX * NZ, NY, 16, tokens)
    parts = []
    for d in (0,) + FAR:
        part = lax.dynamic_index_in_dim(turned, lax.rem(y + d, NY), axis=1, keepdims=False)
        parts.append(part if d == 0 else along_y(part, d))

    own, _, parts = lax.optimization_barrier((own, back, parts))
    back, activations = lax.optimization_barrier((back, activations))

    far = lax.rem(z + NZ // 2, NZ) * n
    held = put(held, along_z(ahead, 1), far, 0)
    other = [there] + [across(piece) for piece in own]
    own = [here] + own

    first = core == 0
    near = dot(jnp.concatenate(own, axis=0), held, ((1,), (0,))).reshape(NX, pair, half)
    away = dot(jnp.concatenate(other, axis=0), held, ((1,), (0,))).reshape(NX, pair, half)
    partial = jnp.concatenate(
        [jnp.where(first, near, away), jnp.where(first, away, near)], axis=1
    )
    sent = partial.astype(bf16)
    features = jnp.concatenate(parts, axis=2)
    crossed = across(features)
    features = jnp.stack(
        [jnp.where(first, features, crossed), jnp.where(first, crossed, features)], axis=1
    )

    total = partial[0]
    for n, d in enumerate(FAR, 1):
        total = total + along_x(sent[n], -d).astype(f32)
    low_rank = total.astype(bf16)

    low_rank, held = lax.optimization_barrier((low_rank, held))
    slab = quarter // NY
    piece = rows(held, y * slab, slab)
    kept = jnp.concatenate([piece] + [along_x(piece, d) for d in FAR], axis=0)
    low = jnp.concatenate([low_rank] + [along_y(low_rank, d) for d in FAR], axis=0)

    weights, low = lax.optimization_barrier((weights[0], low))
    mine, *leaving = cut_weights(weights)
    old = put(jnp.zeros((NY * 16, quarter), bf16), mine, y * 16, 0)
    for d, piece in zip(FAR, leaving):
        old = put(old, along_y(piece, d), lax.rem(y + NY - d, NY) * 16, 0)

    projected = dot(features.reshape(-1, NY * tokens), low, ((1,), (0,)))
    projected = projected.astype(bf16).reshape(2 * NX * NZ, 16, half)
    got = lax.all_to_all(projected, ("dp", "tensor"), split_axis=0, concat_axis=0, tiled=True)
    got = got.reshape(NX * NZ, 2, 16, half).astype(f32).sum(axis=0)
    projected = jnp.concatenate([got[0], got[1]], axis=1)[None]

    first_new = beta_one * first_moment + (1.0 - beta_one) * projected
    second_new = beta_two * second_moment + (1.0 - beta_two) * projected * projected
    corrected = first_new / (1.0 - beta_one**STEP)
    scaled = jnp.sqrt(second_new / (1.0 - beta_two**STEP)) + epsilon
    direction = (corrected / scaled).astype(bf16)[0]

    halves = jnp.stack([direction[:, :half], direction[:, half:]])
    directions = lax.all_to_all(
        jnp.broadcast_to(halves[None], (NY, 2, 16, half)).reshape(NY * 2, 16, half),
        ("fsdp", "tensor"),
        split_axis=0,
        concat_axis=0,
        tiled=True,
    )
    directions = directions.reshape(NY, 2, 16, half).transpose(1, 0, 2, 3).reshape(2, NY * 16, half)
    both = dot(directions.reshape(-1, half), kept, ((1,), (1,))).reshape(2, NY * 16, quarter)
    ours, theirs = jnp.where(first, both[0], both[1]), jnp.where(first, both[1], both[0])
    update = ours + across(theirs.astype(bf16)).astype(f32)
    done = (old.astype(f32) - step_scale * update).astype(bf16)
    new_weights = place([done] + [along_y(done, d) for d in FAR])
    return (new_weights[None], first_new, second_new)


def solution(mesh):
    return jax.shard_map(
        shards,
        mesh=mesh,
        in_specs=(
            P(("dp", "fsdp"), None),
            P(("dp", "fsdp"), "tensor", None),
            P("dp", None),
            P("tensor", ("dp", "fsdp"), None),
            P("tensor", ("dp", "fsdp"), None),
            P("tensor", ("dp", "fsdp"), None),
        ),
        out_specs=(
            P("tensor", "dp", None),
            P("tensor", ("dp", "fsdp"), None),
            P("tensor", ("dp", "fsdp"), None),
        ),
        check_vma=False,
    )
```

time: 169 us -> 162 us (0.959)
  starting transfers between devices: 71.4 us -> 59.8 us
  waiting for transfers between devices: 66.1 us -> 72.3 us
  matrix products: 11.9 us -> 8.39 us
  Pallas kernels: 3.89 us -> 7.18 us
  other arithmetic: 3.58 us -> 1.74 us
    ppermute x4 -> x0, starting transfers between devices: 6.83 us -> none  [fetch(): return lax.ppermute(value, ('dp', 'fsdp'), pairs)]
    ppermute x6 -> x9, waiting for transfers between devices: 13.8 us -> 20 us  [along_x(): return lax.ppermute(value, 'dp', pairs)]
    ppermute x8 -> x7, waiting for transfers between devices: 5.64 us -> 10.4 us  [along_z(): return lax.ppermute(value, 'dp', pairs)]
    ppermute x6 -> x9, starting transfers between devices: 8.76 us -> 12.7 us  [along_x(): return lax.ppermute(value, 'dp', pairs)]
    dot_general x7 -> x4, matrix products: 11.9 us -> 8.39 us  [dot(): lax.dot_general(a, b, ((dims[0], dims[1]), ((), ())), preferred_element_t...]
    ppermute x4 -> x0, waiting for transfers between devices: 3.36 us -> none  [fetch(): return lax.ppermute(value, ('dp', 'fsdp'), pairs)]
    pallas_call x1 -> x3, Pallas kernels: 3.89 us -> 7.18 us  [the longest x1 3.22 us: cut(): pl.pallas_call(kernel, out_shape=[shape] * len(places), in_specs=[pl.Bloc...]
    ppermute x5, starting transfers between devices: 6.95 us -> 4.1 us  [across(): return lax.ppermute(value, 'tensor', [(0, 1), (1, 0)])]
  transfers between devices with their start and end apart: 36 -> 35, of which waited for: 17 -> 14; matrix products, arithmetic and copies ran while one was open for 12% -> 9% of each run, Pallas kernels for 2% -> 3%
where the time goes in v1:
time: 162 us; the launch traced here: 161 us
  waiting for transfers between devices  72.3 us (45%)
  starting transfers between devices  59.8 us (37%)
  local copies, waits for them, and re-layouts  10.7 us (7%)
  matrix products  8.39 us (5%)
  Pallas kernels  7.18 us (4%)
  other arithmetic  1.74 us (1%)
    ppermute x12, waiting for transfers between devices, along_y(): return lax.ppermute(value, 'fsdp', [(y, (y + d) % NY) for y in range(NY)])  21.8 us
    ppermute x12, starting transfers between devices, along_y(): return lax.ppermute(value, 'fsdp', [(y, (y + d) % NY) for y in range(NY)])  20.5 us
    ppermute x9, waiting for transfers between devices, along_x(): return lax.ppermute(value, 'dp', pairs)  20 us
    all_to_all x1, waiting for transfers between devices, shards(): lax.all_to_all(projected, ('dp', 'tensor'), split_axis=0, concat_axis=0,...  16.4 us
    ppermute x9, starting transfers between devices, along_x(): return lax.ppermute(value, 'dp', pairs)  12.7 us
    ppermute x7, starting transfers between devices, along_z(): return lax.ppermute(value, 'dp', pairs)  11.8 us
    ppermute x7, waiting for transfers between devices, along_z(): return lax.ppermute(value, 'dp', pairs)  10.4 us
    dot_general x4, matrix products, dot(): lax.dot_general(a, b, ((dims[0], dims[1]), ((), ())), preferred_element_t...  8.39 us
  transfers between devices with their start and end apart: 35, of which 14 were waited for; matrix products, arithmetic and copies ran while one was open for 9% of the time, Pallas kernels for 3%

profile of v1, /device:TPU:1, one launch (start us, length us, event | category | flops | bytes accessed | tf_op | source)
XLA Modules:
  0.0 161.2 jit_solution(9792003246923470110)
XLA Ops:
  0.8 0.9 copy-done.4
  1.7 2.5 %collective-permute-start = (bf16[256,512]{1,0:T(8,128)(2,1)S(1)}, bf16[256,512]{1,0:T(8,128)(2,1)S(1)}, u32[]{:S(2)}, u32[]{:S(2)}) collective-permute-start(bf16[256,512]{1,0:T(8,128)(2,1)S(1)} %get-tuple-element.59), channel_id=1, source_target_pairs={{0,8},{8,16},{16,24},{24,32},{32,40},{40,48},{48,56},{56,0},{64,72... | collective-permute-start | bytes 786440 | tf_op jit(solution)/shard_map/ppermute | solution.py:28
  4.3 4.0 %collective-permute-start.1 = (bf16[256,512]{1,0:T(8,128)(2,1)S(1)}, bf16[256,512]{1,0:T(8,128)(2,1)S(1)}, u32[]{:S(2)}, u32[]{:S(2)}) collective-permute-start(bf16[256,512]{1,0:T(8,128)(2,1)S(1)} %get-tuple-element.59), channel_id=1, source_target_pairs={{0,56},{8,0},{16,8},{24,16},{32,24},{40,32},{48,40},{56,48},{64,12... | collective-permute-start | bytes 786440 | tf_op jit(solution)/shard_map/ppermute | solution.py:28
  8.3 3.2 %shard_map.85 = (bf16[128,2048]{1,0:T(8,128)(2,1)}, bf16[128,2048]{1,0:T(8,128)(2,1)}, bf16[128,2048]{1,0:T(8,128)(2,1)}, bf16[128,2048]{1,0:T(8,128)(2,1)}, bf16[128,2048]{1,0:T(8,128)(2,1)}) custom-call(bf16[256,8192]{1,0:T(8,128)(2,1)} %act_ref.1), custom_call_target="tpu_custom_call" | custom-call | tf_op jit(solution)/shard_map/pallas_call | solution.py:82
  11.5 2.7 %collective-permute-done = bf16[256,512]{1,0:T(8,128)(2,1)S(1)} collective-permute-done((bf16[256,512]{1,0:T(8,128)(2,1)S(1)}, bf16[256,512]{1,0:T(8,128)(2,1)S(1)}, u32[]{:S(2)}, u32[]{:S(2)}) %collective-permute-start) | collective-permute-done | bytes 262176 | tf_op jit(solution)/shard_map/ppermute | solution.py:28
  14.2 2.4 %collective-permute-start.5 = (bf16[256,512]{1,0:T(8,128)(2,1)S(1)}, bf16[256,512]{1,0:T(8,128)(2,1)S(1)}, u32[]{:S(2)}, u32[]{:S(2)}) collective-permute-start(bf16[256,512]{1,0:T(8,128)(2,1)S(1)} %collective-permute-done.1), channel_id=1, source_target_pairs={{0,56},{8,0},{16,8},{24,16},{32,24},{40,32},{48,40},{56,48},{64,12... | collective-permute-start | bytes 786440 | tf_op jit(solution)/shard_map/ppermute | solution.py:28
  16.7 2.7 %collective-permute-start.2 = (bf16[128,2048]{1,0:T(8,128)(2,1)}, bf16[128,2048]{1,0:T(8,128)(2,1)}, u32[]{:S(2)}, u32[]{:S(2)}) collective-permute-start(bf16[128,2048]{1,0:T(8,128)(2,1)} %get-tuple-element.33), channel_id=1, source_target_pairs={{0,128},{8,136},{16,144},{24,152},{32,160},{40,168},{48,176},{56,1... | collective-permute-start | bytes 1572872 | tf_op jit(solution)/shard_map/ppermute | solution.py:23
  19.4 0.3 collective-permute-start.3
  19.7 2.4 %collective-permute-start.4 = (bf16[128,2048]{1,0:T(8,128)(2,1)}, bf16[128,2048]{1,0:T(8,128)(2,1)}, u32[]{:S(2)}, u32[]{:S(2)}) collective-permute-start(bf16[128,2048]{1,0:T(8,128)(2,1)} %get-tuple-element.35), channel_id=1, source_target_pairs={{0,192},{8,200},{16,208},{24,216},{32,224},{40,232},{48,240},{56,2... | collective-permute-start | bytes 1572872 | tf_op jit(solution)/shard_map/ppermute | solution.py:23
  22.1 2.7 %collective-permute-start.6 = (bf16[256,512]{1,0:T(8,128)(2,1)S(1)}, bf16[256,512]{1,0:T(8,128)(2,1)}, u32[]{:S(2)}, u32[]{:S(2)}) collective-permute-start(bf16[256,512]{1,0:T(8,128)(2,1)S(1)} %collective-permute-done.5), channel_id=1, source_target_pairs={{0,56},{8,0},{16,8},{24,16},{32,24},{40,32},{48,40},{56,48},{64,12... | collective-permute-start | bytes 786440 | tf_op jit(solution)/shard_map/ppermute | solution.py:28
  24.9 1.0 constant_dynamic-update-slice_fusion.12
  25.9 2.2 %collective-permute-done.6 = bf16[256,512]{1,0:T(8,128)(2,1)} collective-permute-done((bf16[256,512]{1,0:T(8,128)(2,1)S(1)}, bf16[256,512]{1,0:T(8,128)(2,1)}, u32[]{:S(2)}, u32[]{:S(2)}) %collective-permute-start.6) | collective-permute-done | bytes 262176 | tf_op jit(solution)/shard_map/ppermute | solution.py:28
  28.1 1.5 copy.11
  29.7 3.0 %collective-permute-start.7 = (bf16[32,16,256]{2,1,0:T(8,128)(2,1)S(1)}, bf16[32,16,256]{2,1,0:T(8,128)(2,1)S(1)}, u32[]{:S(2)}, u32[]{:S(2)}) collective-permute-start(bf16[32,16,256]{2,1,0:T(8,128)(2,1)S(1)} %get-tuple-element.69), channel_id=1, source_target_pairs={{0,4},{2,6},{4,0},{6,2},{1,5},{3,7},{5,1},{7,3},{8,12},{10,14},{12... | collective-permute-start | bytes 786440 | tf_op jit(solution)/shard_map/ppermute | solution.py:32
  32.7 0.5 collective-permute-start.8
  33.2 2.2 %collective-permute-start.9 = (bf16[32,16,256]{2,1,0:T(8,128)(2,1)S(1)}, bf16[32,16,256]{2,1,0:T(8,128)(2,1)S(1)}, u32[]{:S(2)}, u32[]{:S(2)}) collective-permute-start(bf16[32,16,256]{2,1,0:T(8,128)(2,1)S(1)} %get-tuple-element.67), channel_id=1, source_target_pairs={{0,6},{2,0},{4,2},{6,4},{1,7},{3,1},{5,3},{7,5},{8,14},{10,8},{12,... | collective-permute-start | bytes 786440 | tf_op jit(solution)/shard_map/ppermute | solution.py:32
  35.4 1.0 constant_dynamic-update-slice_fusion.10
  36.4 1.0 constant_dynamic-update-slice_fusion.9
  37.4 6.2 %collective-permute-done.3 = bf16[128,2048]{1,0:T(8,128)(2,1)} collective-permute-done((bf16[128,2048]{1,0:T(8,128)(2,1)}, bf16[128,2048]{1,0:T(8,128)(2,1)}, u32[]{:S(2)}, u32[]{:S(2)}) %collective-permute-start.3) | collective-permute-done | bytes 524320 | tf_op jit(solution)/shard_map/ppermute | solution.py:23
  43.6 2.4 %collective-permute-start.13 = (bf16[128,2048]{1,0:T(8,128)(2,1)}, bf16[128,2048]{1,0:T(8,128)(2,1)S(1)}, u32[]{:S(2)}, u32[]{:S(2)}) collective-permute-start(bf16[128,2048]{1,0:T(8,128)(2,1)} %collective-permute-done.2), channel_id=1, source_target_pairs={{0,1},{1,0},{2,3},{3,2},{4,5},{5,4},{6,7},{7,6},{8,9},{9,8},{10,11... | collective-permute-start | bytes 1572872 | tf_op jit(solution)/shard_map/ppermute | solution.py:36
  46.0 0.5 collective-permute-start.15
  46.6 0.3 collective-permute-start.25
  46.9 5.5 %collective-permute-done.12 = bf16[256,512]{1,0:T(8,128)(2,1)S(1)} collective-permute-done((bf16[256,512]{1,0:T(8,128)(2,1)}, bf16[256,512]{1,0:T(8,128)(2,1)S(1)}, u32[]{:S(2)}, u32[]{:S(2)}) %collective-permute-start.12) | collective-permute-done | bytes 262176 | tf_op jit(solution)/shard_map/ppermute | solution.py:28
  52.5 1.2 fusion.9
  53.7 2.6 %broadcast_select_fusion = (f32[512,512]{1,0:T(8,128)S(1)}, f32[512,512]{1,0:T(8,128)S(1)}) fusion(f32[512,512]{1,0:T(8,128)S(1)} %fusion.9, pred[]{:T(512)S(6)} %eq.3, bf16[2048,512]{1,0:T(8,128)(2,1)S(1)} %constant_dynamic-update-slice_fusion.8, bf16[128,2048]{1,0:T(8,128)(2,1)} %collective-permute-done.4, bf16[128,2048]{1,0:T(8,128)(2,1)} %collective-permute-done.3, ...), kind=kOutput, calls=%fused_computation.42 | convolution fusion | flops 1082654720 | bytes 7340033 | tf_op jit(solution)/shard_map/dot_general | solution.py:61
  56.6 0.5 collective-permute-start.17
  57.1 1.1 collective-permute-start.18
  58.2 6.5 %collective-permute-done.16 = bf16[256,512]{1,0:T(8,128)(2,1)S(1)} collective-permute-done((bf16[256,512]{1,0:T(8,128)(2,1)S(1)}, bf16[256,512]{1,0:T(8,128)(2,1)S(1)}, u32[]{:S(2)}, u32[]{:S(2)}) %collective-permute-start.16) | collective-permute-done | bytes 262176 | tf_op jit(solution)/shard_map/ppermute | solution.py:23
  64.6 3.1 %collective-permute-done.17 = bf16[256,512]{1,0:T(8,128)(2,1)S(1)} collective-permute-done((bf16[256,512]{1,0:T(8,128)(2,1)S(1)}, bf16[256,512]{1,0:T(8,128)(2,1)S(1)}, u32[]{:S(2)}, u32[]{:S(2)}) %collective-permute-start.17) | collective-permute-done | bytes 262176 | tf_op jit(solution)/shard_map/ppermute | solution.py:23
  67.8 4.2 %collective-permute-done.18 = bf16[256,512]{1,0:T(8,128)(2,1)S(1)} collective-permute-done((bf16[256,512]{1,0:T(8,128)(2,1)S(1)}, bf16[256,512]{1,0:T(8,128)(2,1)S(1)}, u32[]{:S(2)}, u32[]{:S(2)}) %collective-permute-start.18) | collective-permute-done | bytes 262176 | tf_op jit(solution)/shard_map/ppermute | solution.py:23
  72.1 3.0 %collective-permute-start.19 = (bf16[256,512]{1,0:T(8,128)(2,1)S(1)}, bf16[256,512]{1,0:T(8,128)(2,1)S(1)}, u32[]{:S(2)}, u32[]{:S(2)}) collective-permute-start(bf16[256,512]{1,0:T(8,128)(2,1)S(1)} %fusion.30), channel_id=1, source_target_pairs={{0,4},{2,6},{4,0},{6,2},{1,5},{3,7},{5,1},{7,3},{8,12},{10,14},{12... | collective-permute-start | bytes 786440 | tf_op jit(solution)/shard_map/ppermute | solution.py:32
  75.1 0.4 collective-permute-start.20
  75.5 2.3 %collective-permute-start.21 = (bf16[256,512]{1,0:T(8,128)(2,1)S(1)}, bf16[256,512]{1,0:T(8,128)(2,1)S(1)}, u32[]{:S(2)}, u32[]{:S(2)}) collective-permute-start(bf16[256,512]{1,0:T(8,128)(2,1)S(1)} %fusion.30), channel_id=1, source_target_pairs={{0,6},{2,0},{4,2},{6,4},{1,7},{3,1},{5,3},{7,5},{8,14},{10,8},{12,... | collective-permute-start | bytes 786440 | tf_op jit(solution)/shard_map/ppermute | solution.py:32
  77.8 3.3 %collective-permute-done.19 = bf16[256,512]{1,0:T(8,128)(2,1)S(1)} collective-permute-done((bf16[256,512]{1,0:T(8,128)(2,1)S(1)}, bf16[256,512]{1,0:T(8,128)(2,1)S(1)}, u32[]{:S(2)}, u32[]{:S(2)}) %collective-permute-start.19) | collective-permute-done | bytes 262176 | tf_op jit(solution)/shard_map/ppermute | solution.py:32
  81.2 6.4 %collective-permute-done.20 = bf16[256,512]{1,0:T(8,128)(2,1)S(1)} collective-permute-done((bf16[256,512]{1,0:T(8,128)(2,1)S(1)}, bf16[256,512]{1,0:T(8,128)(2,1)S(1)}, u32[]{:S(2)}, u32[]{:S(2)}) %collective-permute-start.20) | collective-permute-done | bytes 262176 | tf_op jit(solution)/shard_map/ppermute | solution.py:32
  88.0 0.3 copy.12
  88.3 2.2 %convolution_convert_fusion = bf16[1024,512]{1,0:T(8,128)(2,1)} fusion(bf16[1024,1024]{1,0:T(8,128)(2,1)S(1)} %bitcast.63, bf16[1024,512]{1,0:T(8,128)(2,1)S(1)} %pad_maximum_fusion.2), kind=kOutput, calls=%fused_computation.30 | convolution fusion | flops 1074266112 | bytes 4194304 | tf_op jit(solution)/shard_map/dot_general | solution.py:61
  90.5 6.7 %all-to-all-start = ((bf16[64,16,512]{2,1,0:T(8,128)(2,1)}), bf16[64,16,512]{2,1,0:T(8,128)(2,1)S(1)}, u32[]{:S(2)}, u32[]{:S(2)}) async-start(bf16[64,16,512]{2,1,0:T(8,128)(2,1)} %bitcast.64), calls=%async_computation | async-start | bytes 2097152 | tf_op jit(solution)/shard_map/all_to_all | solution.py:208
  97.3 0.8 constant_dynamic-slice_fusion
  98.1 3.0 %collective-permute-start.26 = (bf16[512,512]{1,0:T(8,128)(2,1)}, bf16[512,512]{1,0:T(8,128)(2,1)S(1)}, u32[]{:S(2)}, u32[]{:S(2)}) collective-permute-start(bf16[512,512]{1,0:T(8,128)(2,1)} %constant_dynamic-slice_fusion), channel_id=1, source_target_pairs={{0,128},{8,136},{16,144},{24,152},{32,160},{40,168},{48,176},{56,1... | collective-permute-start | bytes 1572872 | tf_op jit(solution)/shard_map/ppermute | solution.py:23
  101.1 0.4 collective-permute-start.27
  101.5 2.3 %collective-permute-start.28 = (bf16[512,512]{1,0:T(8,128)(2,1)}, bf16[512,512]{1,0:T(8,128)(2,1)}, u32[]{:S(2)}, u32[]{:S(2)}) collective-permute-start(bf16[512,512]{1,0:T(8,128)(2,1)} %constant_dynamic-slice_fusion), channel_id=1, source_target_pairs={{0,192},{8,200},{16,208},{24,216},{32,224},{40,232},{48,240},{56,2... | collective-permute-start | bytes 1572872 | tf_op jit(solution)/shard_map/ppermute | solution.py:23
  103.8 1.7 %shard_map.86 = (bf16[16,2048]{1,0:T(8,128)(2,1)}, bf16[16,2048]{1,0:T(8,128)(2,1)}, bf16[16,2048]{1,0:T(8,128)(2,1)}, bf16[16,2048]{1,0:T(8,128)(2,1)}) custom-call(bf16[16,8192]{1,0:T(8,128)(2,1)} %bitcast.67), custom_call_target="tpu_custom_call" | custom-call | tf_op jit(solution)/shard_map/pallas_call | solution.py:111
  105.5 1.8 %collective-permute-start.22 = (bf16[16,2048]{1,0:T(8,128)(2,1)}, bf16[16,2048]{1,0:T(8,128)(2,1)S(1)}, u32[]{:S(2)}, u32[]{:S(2)}) collective-permute-start(bf16[16,2048]{1,0:T(8,128)(2,1)} %get-tuple-element.46), channel_id=1, source_target_pairs={{0,4},{2,6},{4,0},{6,2},{1,5},{3,7},{5,1},{7,3},{8,12},{10,14},{12... | collective-permute-start | bytes 196616 | tf_op jit(solution)/shard_map/ppermute | solution.py:32
  107.3 1.2 collective-permute-start.23
  108.5 0.9 constant_dynamic-update-slice_fusion.7
  109.4 16.4 %all-to-all-done = bf16[64,16,512]{2,1,0:T(8,128)(2,1)S(1)} async-done(((bf16[64,16,512]{2,1,0:T(8,128)(2,1)}), bf16[64,16,512]{2,1,0:T(8,128)(2,1)S(1)}, u32[]{:S(2)}, u32[]{:S(2)}) %all-to-all-start) | async-done | bytes 1048608 | tf_op jit(solution)/shard_map/all_to_all | solution.py:208
  126.0 0.7 fusion.32
  126.7 0.7 broadcast_in_dim.18
  127.3 4.0 %all-to-all-start.1 = ((bf16[8,16,512]{2,1,0:T(8,128)(2,1)}), bf16[8,16,512]{2,1,0:T(8,128)(2,1)S(1)}, u32[]{:S(2)}, u32[]{:S(2)}) async-start(bf16[8,16,512]{2,1,0:T(8,128)(2,1)} %bitcast.24), calls=%async_computation.1 | async-start | bytes 262144 | tf_op jit(solution)/shard_map/all_to_all | solution.py:219
  131.4 2.7 %collective-permute-start.24 = (bf16[16,2048]{1,0:T(8,128)(2,1)S(1)}, bf16[16,2048]{1,0:T(8,128)(2,1)S(1)}, u32[]{:S(2)}, u32[]{:S(2)}) collective-permute-start(bf16[16,2048]{1,0:T(8,128)(2,1)S(1)} %copy-done.10), channel_id=1, source_target_pairs={{0,6},{2,0},{4,2},{6,4},{1,7},{3,1},{5,3},{7,5},{8,14},{10,8},{12,... | collective-permute-start | bytes 196616 | tf_op jit(solution)/shard_map/ppermute | solution.py:32
  134.1 2.6 %all-to-all-done.1 = bf16[8,16,512]{2,1,0:T(8,128)(2,1)S(1)} async-done(((bf16[8,16,512]{2,1,0:T(8,128)(2,1)}), bf16[8,16,512]{2,1,0:T(8,128)(2,1)S(1)}, u32[]{:S(2)}, u32[]{:S(2)}) %all-to-all-start.1) | async-done | bytes 131104 | tf_op jit(solution)/shard_map/all_to_all | solution.py:219
  136.7 0.8 copy-done.9
  137.5 2.3 %fusion.17 = f32[128,2048]{1,0:T(8,128)S(1)} fusion(bf16[128,512]{1,0:T(8,128)(2,1)S(1)} %bitcast.68, bf16[512,512]{1,0:T(8,128)(2,1)} %collective-permute-done.28, bf16[512,512]{1,0:T(8,128)(2,1)} %collective-permute-done.27, bf16[512,512]{1,0:T(8,128)(2,1)} %copy-done.9, bf16[512,512]{1,0:T(8,128)(2,1)} %constant_dynamic-slice_fusion), kind=kOutput, calls=%fused_computation.21 | convolution fusion | flops 276824064 | bytes 3276800 | tf_op jit(solution)/shard_map/dot_general | solution.py:61
  139.9 1.0 collective-permute-start.29
  140.9 1.1 collective-permute-done.29
  142.1 0.7 collective-permute-start.30
  142.9 1.3 collective-permute-start.31
  144.1 1.4 collective-permute-start.32
  145.5 5.7 %collective-permute-done.30.refs_1_ = bf16[64,2048]{1,0:T(8,128)(2,1)S(1)} collective-permute-done((bf16[64,2048]{1,0:T(8,128)(2,1)S(1)}, bf16[64,2048]{1,0:T(8,128)(2,1)S(1)}, u32[]{:S(2)}, u32[]{:S(2)}) %collective-permute-start.30) | collective-permute-done | bytes 262176 | tf_op jit(solution)/shard_map/ppermute | solution.py:32
  151.3 6.3 %collective-permute-done.31.refs_2_ = bf16[64,2048]{1,0:T(8,128)(2,1)S(1)} collective-permute-done((bf16[64,2048]{1,0:T(8,128)(2,1)S(1)}, bf16[64,2048]{1,0:T(8,128)(2,1)S(1)}, u32[]{:S(2)}, u32[]{:S(2)}) %collective-permute-start.31) | collective-permute-done | bytes 262176 | tf_op jit(solution)/shard_map/ppermute | solution.py:32
  157.6 0.7 copy-done.2
  158.2 0.7 copy-done.3
  158.9 2.2 %shard_map.87 = bf16[64,8192]{1,0:T(8,128)(2,1)} custom-call(bf16[64,2048]{1,0:T(8,128)(2,1)} %copy-done, bf16[64,2048]{1,0:T(8,128)(2,1)} %copy-done.1, bf16[64,2048]{1,0:T(8,128)(2,1)} %copy-done.2, bf16[64,2048]{1,0:T(8,128)(2,1)} %copy-done.3), custom_call_target="tpu_custom_call" | custom-call | tf_op jit(solution)/shard_map/pallas_call | solution.py:132
  (72 shorter events, 1.9 us)
Async XLA Ops:
  0.6 1.0 copy-start.4
  1.7 12.5 %collective-permute-start = (bf16[256,512]{1,0:T(8,128)(2,1)S(1)}, bf16[256,512]{1,0:T(8,128)(2,1)S(1)}, u32[]{:S(2)}, u32[]{:S(2)}) collective-permute-start(bf16[256,512]{1,0:T(8,128)(2,1)S(1)} %get-tuple-element.59), channel_id=1, source_target_pairs={{0,8},{8,16},{16,24},{24,32},{32,40},{40,48},{48,56},{56,0},{64,72... | collective-permute-start | bytes 786440 | tf_op jit(solution)/shard_map/ppermute | solution.py:28
  4.3 10.0 %collective-permute-start.1 = (bf16[256,512]{1,0:T(8,128)(2,1)S(1)}, bf16[256,512]{1,0:T(8,128)(2,1)S(1)}, u32[]{:S(2)}, u32[]{:S(2)}) collective-permute-start(bf16[256,512]{1,0:T(8,128)(2,1)S(1)} %get-tuple-element.59), channel_id=1, source_target_pairs={{0,56},{8,0},{16,8},{24,16},{32,24},{40,32},{48,40},{56,48},{64,12... | collective-permute-start | bytes 786440 | tf_op jit(solution)/shard_map/ppermute | solution.py:28
  14.2 7.9 %collective-permute-start.5 = (bf16[256,512]{1,0:T(8,128)(2,1)S(1)}, bf16[256,512]{1,0:T(8,128)(2,1)S(1)}, u32[]{:S(2)}, u32[]{:S(2)}) collective-permute-start(bf16[256,512]{1,0:T(8,128)(2,1)S(1)} %collective-permute-done.1), channel_id=1, source_target_pairs={{0,56},{8,0},{16,8},{24,16},{32,24},{40,32},{48,40},{56,48},{64,12... | collective-permute-start | bytes 786440 | tf_op jit(solution)/shard_map/ppermute | solution.py:28
  16.7 8.1 %collective-permute-start.10 = (bf16[256,512]{1,0:T(8,128)(2,1)S(1)}, bf16[256,512]{1,0:T(8,128)(2,1)}, u32[]{:S(2)}, u32[]{:S(2)}) collective-permute-start(bf16[256,512]{1,0:T(8,128)(2,1)S(1)} %collective-permute-done), channel_id=1, source_target_pairs={{0,8},{8,16},{16,24},{24,32},{32,40},{40,48},{48,56},{56,0},{64,72... | collective-permute-start | bytes 786440 | tf_op jit(solution)/shard_map/ppermute | solution.py:28
  16.7 16.6 %collective-permute-start.2 = (bf16[128,2048]{1,0:T(8,128)(2,1)}, bf16[128,2048]{1,0:T(8,128)(2,1)}, u32[]{:S(2)}, u32[]{:S(2)}) collective-permute-start(bf16[128,2048]{1,0:T(8,128)(2,1)} %get-tuple-element.33), channel_id=1, source_target_pairs={{0,128},{8,136},{16,144},{24,152},{32,160},{40,168},{48,176},{56,1... | collective-permute-start | bytes 1572872 | tf_op jit(solution)/shard_map/ppermute | solution.py:23
  19.4 24.2 %collective-permute-start.3 = (bf16[128,2048]{1,0:T(8,128)(2,1)}, bf16[128,2048]{1,0:T(8,128)(2,1)}, u32[]{:S(2)}, u32[]{:S(2)}) collective-permute-start(bf16[128,2048]{1,0:T(8,128)(2,1)} %get-tuple-element.34), channel_id=1, source_target_pairs={{0,64},{8,72},{16,80},{24,88},{32,96},{40,104},{48,112},{56,120},{... | collective-permute-start | bytes 1572872 | tf_op jit(solution)/shard_map/ppermute | solution.py:23
  19.7 23.9 %collective-permute-start.4 = (bf16[128,2048]{1,0:T(8,128)(2,1)}, bf16[128,2048]{1,0:T(8,128)(2,1)}, u32[]{:S(2)}, u32[]{:S(2)}) collective-permute-start(bf16[128,2048]{1,0:T(8,128)(2,1)} %get-tuple-element.35), channel_id=1, source_target_pairs={{0,192},{8,200},{16,208},{24,216},{32,224},{40,232},{48,240},{56,2... | collective-permute-start | bytes 1572872 | tf_op jit(solution)/shard_map/ppermute | solution.py:23
  22.1 6.0 %collective-permute-start.6 = (bf16[256,512]{1,0:T(8,128)(2,1)S(1)}, bf16[256,512]{1,0:T(8,128)(2,1)}, u32[]{:S(2)}, u32[]{:S(2)}) collective-permute-start(bf16[256,512]{1,0:T(8,128)(2,1)S(1)} %collective-permute-done.5), channel_id=1, source_target_pairs={{0,56},{8,0},{16,8},{24,16},{32,24},{40,32},{48,40},{56,48},{64,12... | collective-permute-start | bytes 786440 | tf_op jit(solution)/shard_map/ppermute | solution.py:28
  24.8 7.9 %collective-permute-start.11 = (bf16[256,512]{1,0:T(8,128)(2,1)}, bf16[256,512]{1,0:T(8,128)(2,1)}, u32[]{:S(2)}, u32[]{:S(2)}) collective-permute-start(bf16[256,512]{1,0:T(8,128)(2,1)} %collective-permute-done.10), channel_id=1, source_target_pairs={{0,8},{8,16},{16,24},{24,32},{32,40},{40,48},{48,56},{56,0},{64,72... | collective-permute-start | bytes 786440 | tf_op jit(solution)/shard_map/ppermute | solution.py:28
  29.7 13.9 %collective-permute-start.7 = (bf16[32,16,256]{2,1,0:T(8,128)(2,1)S(1)}, bf16[32,16,256]{2,1,0:T(8,128)(2,1)S(1)}, u32[]{:S(2)}, u32[]{:S(2)}) collective-permute-start(bf16[32,16,256]{2,1,0:T(8,128)(2,1)S(1)} %get-tuple-element.69), channel_id=1, source_target_pairs={{0,4},{2,6},{4,0},{6,2},{1,5},{3,7},{5,1},{7,3},{8,12},{10,14},{12... | collective-permute-start | bytes 786440 | tf_op jit(solution)/shard_map/ppermute | solution.py:32
  32.7 10.9 %collective-permute-start.8 = (bf16[32,16,256]{2,1,0:T(8,128)(2,1)S(1)}, bf16[32,16,256]{2,1,0:T(8,128)(2,1)S(1)}, u32[]{:S(2)}, u32[]{:S(2)}) collective-permute-start(bf16[32,16,256]{2,1,0:T(8,128)(2,1)S(1)} %get-tuple-element.68), channel_id=1, source_target_pairs={{0,2},{2,4},{4,6},{6,0},{1,3},{3,5},{5,7},{7,1},{8,10},{10,12},{12... | collective-permute-start | bytes 786440 | tf_op jit(solution)/shard_map/ppermute | solution.py:32
  33.2 19.2 %copy-start.8 = (bf16[128,2048]{1,0:T(8,128)(2,1)S(1)}, bf16[128,2048]{1,0:T(8,128)(2,1)}, u32[]{:S(2)}) copy-start(bf16[128,2048]{1,0:T(8,128)(2,1)} %get-tuple-element.42) | copy-start | bytes 1572868
  33.2 10.4 %collective-permute-start.9 = (bf16[32,16,256]{2,1,0:T(8,128)(2,1)S(1)}, bf16[32,16,256]{2,1,0:T(8,128)(2,1)S(1)}, u32[]{:S(2)}, u32[]{:S(2)}) collective-permute-start(bf16[32,16,256]{2,1,0:T(8,128)(2,1)S(1)} %get-tuple-element.67), channel_id=1, source_target_pairs={{0,6},{2,0},{4,2},{6,4},{1,7},{3,1},{5,3},{7,5},{8,14},{10,8},{12,... | collective-permute-start | bytes 786440 | tf_op jit(solution)/shard_map/ppermute | solution.py:32
  43.6 8.8 %collective-permute-start.12 = (bf16[256,512]{1,0:T(8,128)(2,1)}, bf16[256,512]{1,0:T(8,128)(2,1)S(1)}, u32[]{:S(2)}, u32[]{:S(2)}) collective-permute-start(bf16[256,512]{1,0:T(8,128)(2,1)} %collective-permute-done.11), channel_id=1, source_target_pairs={{0,8},{8,16},{16,24},{24,32},{32,40},{40,48},{48,56},{56,0},{64,72... | collective-permute-start | bytes 786440 | tf_op jit(solution)/shard_map/ppermute | solution.py:28
  43.6 8.8 %collective-permute-start.13 = (bf16[128,2048]{1,0:T(8,128)(2,1)}, bf16[128,2048]{1,0:T(8,128)(2,1)S(1)}, u32[]{:S(2)}, u32[]{:S(2)}) collective-permute-start(bf16[128,2048]{1,0:T(8,128)(2,1)} %collective-permute-done.2), channel_id=1, source_target_pairs={{0,1},{1,0},{2,3},{3,2},{4,5},{5,4},{6,7},{7,6},{8,9},{9,8},{10,11... | collective-permute-start | bytes 1572872 | tf_op jit(solution)/shard_map/ppermute | solution.py:36
  46.0 6.5 %collective-permute-start.14 = (bf16[128,2048]{1,0:T(8,128)(2,1)}, bf16[128,2048]{1,0:T(8,128)(2,1)S(1)}, u32[]{:S(2)}, u32[]{:S(2)}) collective-permute-start(bf16[128,2048]{1,0:T(8,128)(2,1)} %collective-permute-done.3), channel_id=1, source_target_pairs={{0,1},{1,0},{2,3},{3,2},{4,5},{5,4},{6,7},{7,6},{8,9},{9,8},{10,11... | collective-permute-start | bytes 1572872 | tf_op jit(solution)/shard_map/ppermute | solution.py:36
  46.0 6.5 %collective-permute-start.15 = (bf16[128,2048]{1,0:T(8,128)(2,1)}, bf16[128,2048]{1,0:T(8,128)(2,1)S(1)}, u32[]{:S(2)}, u32[]{:S(2)}) collective-permute-start(bf16[128,2048]{1,0:T(8,128)(2,1)} %collective-permute-done.4), channel_id=1, source_target_pairs={{0,1},{1,0},{2,3},{3,2},{4,5},{5,4},{6,7},{7,6},{8,9},{9,8},{10,11... | collective-permute-start | bytes 1572872 | tf_op jit(solution)/shard_map/ppermute | solution.py:36
  46.6 41.0 %collective-permute-start.25 = (bf16[32,16,1024]{2,1,0:T(8,128)(2,1)S(1)}, bf16[32,16,1024]{2,1,0:T(8,128)(2,1)S(1)}, u32[]{:S(2)}, u32[]{:S(2)}) collective-permute-start(bf16[32,16,1024]{2,1,0:T(8,128)(2,1)S(1)} %constant_dynamic-update-slice_fusion), channel_id=1, source_target_pairs={{0,1},{1,0},{2,3},{3,2},{4,5},{5,4},{6,7},{7,6},{8,9},{9,8},{10,11... | collective-permute-start | bytes 3145736 | tf_op jit(solution)/shard_map/ppermute | solution.py:36
  52.4 1.3 copy-start.7
  56.5 8.1 %collective-permute-start.16 = (bf16[256,512]{1,0:T(8,128)(2,1)S(1)}, bf16[256,512]{1,0:T(8,128)(2,1)S(1)}, u32[]{:S(2)}, u32[]{:S(2)}) collective-permute-start(bf16[256,512]{1,0:T(8,128)(2,1)S(1)} %get-tuple-element.64), channel_id=1, source_target_pairs={{0,128},{8,136},{16,144},{24,152},{32,160},{40,168},{48,176},{56,1... | collective-permute-start | bytes 786440 | tf_op jit(solution)/shard_map/ppermute | solution.py:23
  56.6 11.1 %collective-permute-start.17 = (bf16[256,512]{1,0:T(8,128)(2,1)S(1)}, bf16[256,512]{1,0:T(8,128)(2,1)S(1)}, u32[]{:S(2)}, u32[]{:S(2)}) collective-permute-start(bf16[256,512]{1,0:T(8,128)(2,1)S(1)} %get-tuple-element.66), channel_id=1, source_target_pairs={{0,192},{8,200},{16,208},{24,216},{32,224},{40,232},{48,240},{56,2... | collective-permute-start | bytes 786440 | tf_op jit(solution)/shard_map/ppermute | solution.py:23
  57.1 14.9 %collective-permute-start.18 = (bf16[256,512]{1,0:T(8,128)(2,1)S(1)}, bf16[256,512]{1,0:T(8,128)(2,1)S(1)}, u32[]{:S(2)}, u32[]{:S(2)}) collective-permute-start(bf16[256,512]{1,0:T(8,128)(2,1)S(1)} %get-tuple-element.65), channel_id=1, source_target_pairs={{0,64},{8,72},{16,80},{24,88},{32,96},{40,104},{48,112},{56,120},{... | collective-permute-start | bytes 786440 | tf_op jit(solution)/shard_map/ppermute | solution.py:23
  72.1 9.0 %collective-permute-start.19 = (bf16[256,512]{1,0:T(8,128)(2,1)S(1)}, bf16[256,512]{1,0:T(8,128)(2,1)S(1)}, u32[]{:S(2)}, u32[]{:S(2)}) collective-permute-start(bf16[256,512]{1,0:T(8,128)(2,1)S(1)} %fusion.30), channel_id=1, source_target_pairs={{0,4},{2,6},{4,0},{6,2},{1,5},{3,7},{5,1},{7,3},{8,12},{10,14},{12... | collective-permute-start | bytes 786440 | tf_op jit(solution)/shard_map/ppermute | solution.py:32
  75.1 12.4 %collective-permute-start.20 = (bf16[256,512]{1,0:T(8,128)(2,1)S(1)}, bf16[256,512]{1,0:T(8,128)(2,1)S(1)}, u32[]{:S(2)}, u32[]{:S(2)}) collective-permute-start(bf16[256,512]{1,0:T(8,128)(2,1)S(1)} %fusion.30), channel_id=1, source_target_pairs={{0,2},{2,4},{4,6},{6,0},{1,3},{3,5},{5,7},{7,1},{8,10},{10,12},{12... | collective-permute-start | bytes 786440 | tf_op jit(solution)/shard_map/ppermute | solution.py:32
  75.5 12.0 %collective-permute-start.21 = (bf16[256,512]{1,0:T(8,128)(2,1)S(1)}, bf16[256,512]{1,0:T(8,128)(2,1)S(1)}, u32[]{:S(2)}, u32[]{:S(2)}) collective-permute-start(bf16[256,512]{1,0:T(8,128)(2,1)S(1)} %fusion.30), channel_id=1, source_target_pairs={{0,6},{2,0},{4,2},{6,4},{1,7},{3,1},{5,3},{7,5},{8,14},{10,8},{12,... | collective-permute-start | bytes 786440 | tf_op jit(solution)/shard_map/ppermute | solution.py:32
  90.5 35.5 %copy-start.5 = (f32[1,16,1024]{2,1,0:T(8,128)S(1)}, f32[1,16,1024]{2,1,0:T(8,128)}, u32[]{:S(2)}) copy-start(f32[1,16,1024]{2,1,0:T(8,128)} %param.10) | copy-start | bytes 196612
  90.5 35.5 %copy-start.6 = (f32[1,16,1024]{2,1,0:T(8,128)S(1)}, f32[1,16,1024]{2,1,0:T(8,128)}, u32[]{:S(2)}) copy-start(f32[1,16,1024]{2,1,0:T(8,128)} %param.11) | copy-start | bytes 196612
  90.5 35.3 %all-to-all-start = ((bf16[64,16,512]{2,1,0:T(8,128)(2,1)}), bf16[64,16,512]{2,1,0:T(8,128)(2,1)S(1)}, u32[]{:S(2)}, u32[]{:S(2)}) async-start(bf16[64,16,512]{2,1,0:T(8,128)(2,1)} %bitcast.64), calls=%async_computation | async-start | bytes 2097152 | tf_op jit(solution)/shard_map/all_to_all | solution.py:208
  98.1 38.6 %collective-permute-start.26 = (bf16[512,512]{1,0:T(8,128)(2,1)}, bf16[512,512]{1,0:T(8,128)(2,1)S(1)}, u32[]{:S(2)}, u32[]{:S(2)}) collective-permute-start(bf16[512,512]{1,0:T(8,128)(2,1)} %constant_dynamic-slice_fusion), channel_id=1, source_target_pairs={{0,128},{8,136},{16,144},{24,152},{32,160},{40,168},{48,176},{56,1... | collective-permute-start | bytes 1572872 | tf_op jit(solution)/shard_map/ppermute | solution.py:23
  101.1 35.6 %collective-permute-start.27 = (bf16[512,512]{1,0:T(8,128)(2,1)}, bf16[512,512]{1,0:T(8,128)(2,1)}, u32[]{:S(2)}, u32[]{:S(2)}) collective-permute-start(bf16[512,512]{1,0:T(8,128)(2,1)} %constant_dynamic-slice_fusion), channel_id=1, source_target_pairs={{0,64},{8,72},{16,80},{24,88},{32,96},{40,104},{48,112},{56,120},{... | collective-permute-start | bytes 1572872 | tf_op jit(solution)/shard_map/ppermute | solution.py:23
  101.5 35.2 %collective-permute-start.28 = (bf16[512,512]{1,0:T(8,128)(2,1)}, bf16[512,512]{1,0:T(8,128)(2,1)}, u32[]{:S(2)}, u32[]{:S(2)}) collective-permute-start(bf16[512,512]{1,0:T(8,128)(2,1)} %constant_dynamic-slice_fusion), channel_id=1, source_target_pairs={{0,192},{8,200},{16,208},{24,216},{32,224},{40,232},{48,240},{56,2... | collective-permute-start | bytes 1572872 | tf_op jit(solution)/shard_map/ppermute | solution.py:23
  105.5 25.9 %copy-start.10 = (bf16[16,2048]{1,0:T(8,128)(2,1)S(1)}, bf16[16,2048]{1,0:T(8,128)(2,1)}, u32[]{:S(2)}) copy-start(bf16[16,2048]{1,0:T(8,128)(2,1)} %get-tuple-element.48) | copy-start | bytes 196612
  105.5 25.9 %collective-permute-start.22 = (bf16[16,2048]{1,0:T(8,128)(2,1)}, bf16[16,2048]{1,0:T(8,128)(2,1)S(1)}, u32[]{:S(2)}, u32[]{:S(2)}) collective-permute-start(bf16[16,2048]{1,0:T(8,128)(2,1)} %get-tuple-element.46), channel_id=1, source_target_pairs={{0,4},{2,6},{4,0},{6,2},{1,5},{3,7},{5,1},{7,3},{8,12},{10,14},{12... | collective-permute-start | bytes 196616 | tf_op jit(solution)/shard_map/ppermute | solution.py:32
  107.3 33.5 %collective-permute-start.23 = (bf16[16,2048]{1,0:T(8,128)(2,1)}, bf16[16,2048]{1,0:T(8,128)(2,1)S(1)}, u32[]{:S(2)}, u32[]{:S(2)}) collective-permute-start(bf16[16,2048]{1,0:T(8,128)(2,1)} %get-tuple-element.47), channel_id=1, source_target_pairs={{0,2},{2,4},{4,6},{6,0},{1,3},{3,5},{5,7},{7,1},{8,10},{10,12},{12... | collective-permute-start | bytes 196616 | tf_op jit(solution)/shard_map/ppermute | solution.py:32
  127.3 9.3 %all-to-all-start.1 = ((bf16[8,16,512]{2,1,0:T(8,128)(2,1)}), bf16[8,16,512]{2,1,0:T(8,128)(2,1)S(1)}, u32[]{:S(2)}, u32[]{:S(2)}) async-start(bf16[8,16,512]{2,1,0:T(8,128)(2,1)} %bitcast.24), calls=%async_computation.1 | async-start | bytes 262144 | tf_op jit(solution)/shard_map/all_to_all | solution.py:219
  131.4 9.4 %collective-permute-start.24 = (bf16[16,2048]{1,0:T(8,128)(2,1)S(1)}, bf16[16,2048]{1,0:T(8,128)(2,1)S(1)}, u32[]{:S(2)}, u32[]{:S(2)}) collective-permute-start(bf16[16,2048]{1,0:T(8,128)(2,1)S(1)} %copy-done.10), channel_id=1, source_target_pairs={{0,6},{2,0},{4,2},{6,4},{1,7},{3,1},{5,3},{7,5},{8,14},{10,8},{12,... | collective-permute-start | bytes 196616 | tf_op jit(solution)/shard_map/ppermute | solution.py:32
  136.7 0.8 copy-start.9
  139.9 2.1 %collective-permute-start.29 = (bf16[64,2048]{1,0:T(8,128)(2,1)S(1)}, bf16[64,2048]{1,0:T(8,128)(2,1)S(1)}, u32[]{:S(2)}, u32[]{:S(2)}) collective-permute-start(bf16[64,2048]{1,0:T(8,128)(2,1)S(1)} %select_convert_fusion), channel_id=1, source_target_pairs={{0,1},{1,0},{2,3},{3,2},{4,5},{5,4},{6,7},{7,6},{8,9},{9,8},{10,11... | collective-permute-start | bytes 786440 | tf_op jit(solution)/shard_map/ppermute | solution.py:36
  142.1 15.5 %copy-start = (bf16[64,2048]{1,0:T(8,128)(2,1)}, bf16[64,2048]{1,0:T(8,128)(2,1)S(1)}, u32[]{:S(2)}) copy-start(bf16[64,2048]{1,0:T(8,128)(2,1)S(1)} %subtract_convert_fusion.refs_0_) | copy-start | bytes 786436
  142.1 9.2 %collective-permute-start.30 = (bf16[64,2048]{1,0:T(8,128)(2,1)S(1)}, bf16[64,2048]{1,0:T(8,128)(2,1)S(1)}, u32[]{:S(2)}, u32[]{:S(2)}) collective-permute-start(bf16[64,2048]{1,0:T(8,128)(2,1)S(1)} %subtract_convert_fusion.refs_0_), channel_id=1, source_target_pairs={{0,4},{2,6},{4,0},{6,2},{1,5},{3,7},{5,1},{7,3},{8,12},{10,14},{12... | collective-permute-start | bytes 786440 | tf_op jit(solution)/shard_map/ppermute | solution.py:32
  142.9 14.7 %collective-permute-start.31 = (bf16[64,2048]{1,0:T(8,128)(2,1)S(1)}, bf16[64,2048]{1,0:T(8,128)(2,1)S(1)}, u32[]{:S(2)}, u32[]{:S(2)}) collective-permute-start(bf16[64,2048]{1,0:T(8,128)(2,1)S(1)} %subtract_convert_fusion.refs_0_), channel_id=1, source_target_pairs={{0,2},{2,4},{4,6},{6,0},{1,3},{3,5},{5,7},{7,1},{8,10},{10,12},{12... | collective-permute-start | bytes 786440 | tf_op jit(solution)/shard_map/ppermute | solution.py:32
  144.1 13.4 %collective-permute-start.32 = (bf16[64,2048]{1,0:T(8,128)(2,1)S(1)}, bf16[64,2048]{1,0:T(8,128)(2,1)S(1)}, u32[]{:S(2)}, u32[]{:S(2)}) collective-permute-start(bf16[64,2048]{1,0:T(8,128)(2,1)S(1)} %subtract_convert_fusion.refs_0_), channel_id=1, source_target_pairs={{0,6},{2,0},{4,2},{6,4},{1,7},{3,1},{5,3},{7,5},{8,14},{10,8},{12,... | collective-permute-start | bytes 786440 | tf_op jit(solution)/shard_map/ppermute | solution.py:32
  151.3 6.3 %copy-start.1 = (bf16[64,2048]{1,0:T(8,128)(2,1)}, bf16[64,2048]{1,0:T(8,128)(2,1)S(1)}, u32[]{:S(2)}) copy-start(bf16[64,2048]{1,0:T(8,128)(2,1)S(1)} %collective-permute-done.30.refs_1_) | copy-start | bytes 786436
  157.5 0.7 copy-start.2
  158.2 0.7 copy-start.3

commit v2 on v1

--- a/solution.py
+++ b/solution.py
@@ -115,26 +115,6 @@
         out_specs=[pl.BlockSpec(memory_space=pltpu.VMEM)] * NY,
         scratch_shapes=[pltpu.SemaphoreType.DMA((NY, NX))],
     )(weights)
-
-
-def place(parts):
-    count, quarter = parts[0].shape
-    slab = quarter // NY
-
-    def kernel(*refs):
-        ins, out = refs[:-1], refs[-1]
-        x, y = lax.div(lax.axis_index("dp"), NZ), lax.axis_index("fsdp")
-        for part, e in zip(ins, (0,) + FAR):
-            for k, d in enumerate((0,) + FAR):
-                col = lax.rem(x + NX - d, NX) * quarter + lax.rem(y + NY - e, NY) * slab
-                out[:, pl.ds(pl.multiple_of(col, slab), slab)] = part[:, k * slab : (k + 1) * slab]
-
-    return pl.pallas_call(
-        kernel,
-        out_shape=jax.ShapeDtypeStruct((count, quarter * NX), parts[0].dtype),
-        in_specs=[pl.BlockSpec(memory_space=pltpu.VMEM)] * NY,
-        out_specs=pl.BlockSpec(memory_space=pltpu.VMEM),
-    )(*parts)
 
 
 def shards(activations, out_grads, basis, weights, first_moment, second_moment):
@@ -228,7 +208,12 @@
     ours, theirs = jnp.where(first, both[0], both[1]), jnp.where(first, both[1], both[0])
     update = ours + across(theirs.astype(bf16)).astype(f32)
     done = (old.astype(f32) - step_scale * update).astype(bf16)
-    new_weights = place([done] + [along_y(done, d) for d in FAR])
+    new_weights = jnp.zeros((NY * 16, width), bf16)
+    for e in (0,) + FAR:
+        part = along_y(done, e) if e else done
+        for k, d in enumerate((0,) + FAR):
+            at = lax.rem(x + NX - d, NX) * quarter + lax.rem(y + NY - e, NY) * slab
+            new_weights = put(new_weights, part[:, k * slab : (k + 1) * slab], at, 1)
     return (new_weights[None], first_new, second_new)
 
 

time: 162 us -> 158 us (0.975)
  Pallas kernels: 7.18 us -> 4.96 us
    pallas_call x1 -> x0, Pallas kernels: 2.25 us -> none  [place(): pl.pallas_call(kernel, out_shape=jax.ShapeDtypeStruct((count, quarter * N...]
    dynamic_update_slice x12 -> x28, local copies, waits for them, and re-layouts: 3.95 us -> 4.14 us  [put(): return lax.dynamic_update_slice_in_dim(whole, part, start, axis=axis)]
where the time goes in v2:
time: 158 us; the launch traced here: 157 us
  waiting for transfers between devices  71.8 us (45%)
  starting transfers between devices  59.7 us (38%)
  local copies, waits for them, and re-layouts  9.76 us (6%)
  matrix products  8.08 us (5%)
  Pallas kernels  4.96 us (3%)
  other arithmetic  1.76 us (1%)
    ppermute x12, waiting for transfers between devices, along_y(): return lax.ppermute(value, 'fsdp', [(y, (y + d) % NY) for y in range(NY)])  21.6 us
    ppermute x12, starting transfers between devices, along_y(): return lax.ppermute(value, 'fsdp', [(y, (y + d) % NY) for y in range(NY)])  20.5 us
    ppermute x9, waiting for transfers between devices, along_x(): return lax.ppermute(value, 'dp', pairs)  20 us
    all_to_all x1, waiting for transfers between devices, shards(): lax.all_to_all(projected, ('dp', 'tensor'), split_axis=0, concat_axis=0,...  16.2 us
    ppermute x9, starting transfers between devices, along_x(): return lax.ppermute(value, 'dp', pairs)  12.7 us
    ppermute x7, starting transfers between devices, along_z(): return lax.ppermute(value, 'dp', pairs)  11.8 us
    ppermute x7, waiting for transfers between devices, along_z(): return lax.ppermute(value, 'dp', pairs)  10.3 us
    dot_general x4, matrix products, dot(): lax.dot_general(a, b, ((dims[0], dims[1]), ((), ())), preferred_element_t...  8.08 us
  transfers between devices with their start and end apart: 35, of which 14 were waited for; matrix products, arithmetic and copies ran while one was open for 9% of the time, Pallas kernels for 3%

profile of v2, /device:TPU:1, one launch (start us, length us, event | category | flops | bytes accessed | tf_op | source)
XLA Modules:
  0.0 157.5 jit_solution(17743721762294186900)
XLA Ops:
  0.8 0.9 copy-done.1
  1.7 2.5 %collective-permute-start = (bf16[256,512]{1,0:T(8,128)(2,1)S(1)}, bf16[256,512]{1,0:T(8,128)(2,1)S(1)}, u32[]{:S(2)}, u32[]{:S(2)}) collective-permute-start(bf16[256,512]{1,0:T(8,128)(2,1)S(1)} %get-tuple-element.59), channel_id=1, source_target_pairs={{0,8},{8,16},{16,24},{24,32},{32,40},{40,48},{48,56},{56,0},{64,72... | collective-permute-start | bytes 786440 | tf_op jit(solution)/shard_map/ppermute | solution.py:28
  4.3 4.0 %collective-permute-start.1 = (bf16[256,512]{1,0:T(8,128)(2,1)S(1)}, bf16[256,512]{1,0:T(8,128)(2,1)S(1)}, u32[]{:S(2)}, u32[]{:S(2)}) collective-permute-start(bf16[256,512]{1,0:T(8,128)(2,1)S(1)} %get-tuple-element.59), channel_id=1, source_target_pairs={{0,56},{8,0},{16,8},{24,16},{32,24},{40,32},{48,40},{56,48},{64,12... | collective-permute-start | bytes 786440 | tf_op jit(solution)/shard_map/ppermute | solution.py:28
  8.3 3.2 %shard_map.85 = (bf16[128,2048]{1,0:T(8,128)(2,1)}, bf16[128,2048]{1,0:T(8,128)(2,1)}, bf16[128,2048]{1,0:T(8,128)(2,1)}, bf16[128,2048]{1,0:T(8,128)(2,1)}, bf16[128,2048]{1,0:T(8,128)(2,1)}) custom-call(bf16[256,8192]{1,0:T(8,128)(2,1)} %act_ref.1), custom_call_target="tpu_custom_call" | custom-call | tf_op jit(solution)/shard_map/pallas_call | solution.py:82
  11.5 2.7 %collective-permute-done = bf16[256,512]{1,0:T(8,128)(2,1)S(1)} collective-permute-done((bf16[256,512]{1,0:T(8,128)(2,1)S(1)}, bf16[256,512]{1,0:T(8,128)(2,1)S(1)}, u32[]{:S(2)}, u32[]{:S(2)}) %collective-permute-start) | collective-permute-done | bytes 262176 | tf_op jit(solution)/shard_map/ppermute | solution.py:28
  14.2 2.4 %collective-permute-start.5 = (bf16[256,512]{1,0:T(8,128)(2,1)S(1)}, bf16[256,512]{1,0:T(8,128)(2,1)S(1)}, u32[]{:S(2)}, u32[]{:S(2)}) collective-permute-start(bf16[256,512]{1,0:T(8,128)(2,1)S(1)} %collective-permute-done.1), channel_id=1, source_target_pairs={{0,56},{8,0},{16,8},{24,16},{32,24},{40,32},{48,40},{56,48},{64,12... | collective-permute-start | bytes 786440 | tf_op jit(solution)/shard_map/ppermute | solution.py:28
  16.7 2.7 %collective-permute-start.2 = (bf16[128,2048]{1,0:T(8,128)(2,1)}, bf16[128,2048]{1,0:T(8,128)(2,1)}, u32[]{:S(2)}, u32[]{:S(2)}) collective-permute-start(bf16[128,2048]{1,0:T(8,128)(2,1)} %get-tuple-element.33), channel_id=1, source_target_pairs={{0,128},{8,136},{16,144},{24,152},{32,160},{40,168},{48,176},{56,1... | collective-permute-start | bytes 1572872 | tf_op jit(solution)/shard_map/ppermute | solution.py:23
  19.4 0.3 collective-permute-start.3
  19.7 2.4 %collective-permute-start.4 = (bf16[128,2048]{1,0:T(8,128)(2,1)}, bf16[128,2048]{1,0:T(8,128)(2,1)}, u32[]{:S(2)}, u32[]{:S(2)}) collective-permute-start(bf16[128,2048]{1,0:T(8,128)(2,1)} %get-tuple-element.35), channel_id=1, source_target_pairs={{0,192},{8,200},{16,208},{24,216},{32,224},{40,232},{48,240},{56,2... | collective-permute-start | bytes 1572872 | tf_op jit(solution)/shard_map/ppermute | solution.py:23
  22.1 2.7 %collective-permute-start.6 = (bf16[256,512]{1,0:T(8,128)(2,1)S(1)}, bf16[256,512]{1,0:T(8,128)(2,1)}, u32[]{:S(2)}, u32[]{:S(2)}) collective-permute-start(bf16[256,512]{1,0:T(8,128)(2,1)S(1)} %collective-permute-done.5), channel_id=1, source_target_pairs={{0,56},{8,0},{16,8},{24,16},{32,24},{40,32},{48,40},{56,48},{64,12... | collective-permute-start | bytes 786440 | tf_op jit(solution)/shard_map/ppermute | solution.py:28
  24.9 1.0 constant_dynamic-update-slice_fusion.12
  25.9 2.2 %collective-permute-done.6 = bf16[256,512]{1,0:T(8,128)(2,1)} collective-permute-done((bf16[256,512]{1,0:T(8,128)(2,1)S(1)}, bf16[256,512]{1,0:T(8,128)(2,1)}, u32[]{:S(2)}, u32[]{:S(2)}) %collective-permute-start.6) | collective-permute-done | bytes 262176 | tf_op jit(solution)/shard_map/ppermute | solution.py:28
  28.1 1.5 copy.11
  29.7 3.0 %collective-permute-start.7 = (bf16[32,16,256]{2,1,0:T(8,128)(2,1)S(1)}, bf16[32,16,256]{2,1,0:T(8,128)(2,1)S(1)}, u32[]{:S(2)}, u32[]{:S(2)}) collective-permute-start(bf16[32,16,256]{2,1,0:T(8,128)(2,1)S(1)} %get-tuple-element.69), channel_id=1, source_target_pairs={{0,4},{2,6},{4,0},{6,2},{1,5},{3,7},{5,1},{7,3},{8,12},{10,14},{12... | collective-permute-start | bytes 786440 | tf_op jit(solution)/shard_map/ppermute | solution.py:32
  32.7 0.5 collective-permute-start.8
  33.2 2.2 %collective-permute-start.9 = (bf16[32,16,256]{2,1,0:T(8,128)(2,1)S(1)}, bf16[32,16,256]{2,1,0:T(8,128)(2,1)S(1)}, u32[]{:S(2)}, u32[]{:S(2)}) collective-permute-start(bf16[32,16,256]{2,1,0:T(8,128)(2,1)S(1)} %get-tuple-element.67), channel_id=1, source_target_pairs={{0,6},{2,0},{4,2},{6,4},{1,7},{3,1},{5,3},{7,5},{8,14},{10,8},{12,... | collective-permute-start | bytes 786440 | tf_op jit(solution)/shard_map/ppermute | solution.py:32
  35.4 1.0 constant_dynamic-update-slice_fusion.10
  36.4 1.0 constant_dynamic-update-slice_fusion.9
  37.4 6.2 %collective-permute-done.3 = bf16[128,2048]{1,0:T(8,128)(2,1)} collective-permute-done((bf16[128,2048]{1,0:T(8,128)(2,1)}, bf16[128,2048]{1,0:T(8,128)(2,1)}, u32[]{:S(2)}, u32[]{:S(2)}) %collective-permute-start.3) | collective-permute-done | bytes 524320 | tf_op jit(solution)/shard_map/ppermute | solution.py:23
  43.6 2.4 %collective-permute-start.13 = (bf16[128,2048]{1,0:T(8,128)(2,1)}, bf16[128,2048]{1,0:T(8,128)(2,1)S(1)}, u32[]{:S(2)}, u32[]{:S(2)}) collective-permute-start(bf16[128,2048]{1,0:T(8,128)(2,1)} %collective-permute-done.2), channel_id=1, source_target_pairs={{0,1},{1,0},{2,3},{3,2},{4,5},{5,4},{6,7},{7,6},{8,9},{9,8},{10,11... | collective-permute-start | bytes 1572872 | tf_op jit(solution)/shard_map/ppermute | solution.py:36
  46.0 0.5 collective-permute-start.15
  46.6 0.3 collective-permute-start.25
  46.9 5.5 %collective-permute-done.12 = bf16[256,512]{1,0:T(8,128)(2,1)S(1)} collective-permute-done((bf16[256,512]{1,0:T(8,128)(2,1)}, bf16[256,512]{1,0:T(8,128)(2,1)S(1)}, u32[]{:S(2)}, u32[]{:S(2)}) %collective-permute-start.12) | collective-permute-done | bytes 262176 | tf_op jit(solution)/shard_map/ppermute | solution.py:28
  52.5 1.2 fusion.9
  53.7 2.6 %broadcast_select_fusion = (f32[512,512]{1,0:T(8,128)S(1)}, f32[512,512]{1,0:T(8,128)S(1)}) fusion(f32[512,512]{1,0:T(8,128)S(1)} %fusion.9, pred[]{:T(512)S(6)} %eq.3, bf16[2048,512]{1,0:T(8,128)(2,1)S(1)} %constant_dynamic-update-slice_fusion.8, bf16[128,2048]{1,0:T(8,128)(2,1)} %collective-permute-done.4, bf16[128,2048]{1,0:T(8,128)(2,1)} %collective-permute-done.3, ...), kind=kOutput, calls=%fused_computation.42 | convolution fusion | flops 1082654720 | bytes 7340033 | tf_op jit(solution)/shard_map/dot_general | solution.py:61
  56.6 0.5 collective-permute-start.17
  57.1 1.1 collective-permute-start.18
  58.2 6.5 %collective-permute-done.16 = bf16[256,512]{1,0:T(8,128)(2,1)S(1)} collective-permute-done((bf16[256,512]{1,0:T(8,128)(2,1)S(1)}, bf16[256,512]{1,0:T(8,128)(2,1)S(1)}, u32[]{:S(2)}, u32[]{:S(2)}) %collective-permute-start.16) | collective-permute-done | bytes 262176 | tf_op jit(solution)/shard_map/ppermute | solution.py:23
  64.6 3.1 %collective-permute-done.17 = bf16[256,512]{1,0:T(8,128)(2,1)S(1)} collective-permute-done((bf16[256,512]{1,0:T(8,128)(2,1)S(1)}, bf16[256,512]{1,0:T(8,128)(2,1)S(1)}, u32[]{:S(2)}, u32[]{:S(2)}) %collective-permute-start.17) | collective-permute-done | bytes 262176 | tf_op jit(solution)/shard_map/ppermute | solution.py:23
  67.8 4.2 %collective-permute-done.18 = bf16[256,512]{1,0:T(8,128)(2,1)S(1)} collective-permute-done((bf16[256,512]{1,0:T(8,128)(2,1)S(1)}, bf16[256,512]{1,0:T(8,128)(2,1)S(1)}, u32[]{:S(2)}, u32[]{:S(2)}) %collective-permute-start.18) | collective-permute-done | bytes 262176 | tf_op jit(solution)/shard_map/ppermute | solution.py:23
  72.0 0.2 fusion.30
  72.1 3.0 %collective-permute-start.19 = (bf16[256,512]{1,0:T(8,128)(2,1)S(1)}, bf16[256,512]{1,0:T(8,128)(2,1)S(1)}, u32[]{:S(2)}, u32[]{:S(2)}) collective-permute-start(bf16[256,512]{1,0:T(8,128)(2,1)S(1)} %fusion.30), channel_id=1, source_target_pairs={{0,4},{2,6},{4,0},{6,2},{1,5},{3,7},{5,1},{7,3},{8,12},{10,14},{12... | collective-permute-start | bytes 786440 | tf_op jit(solution)/shard_map/ppermute | solution.py:32
  75.1 0.4 collective-permute-start.20
  75.5 2.3 %collective-permute-start.21 = (bf16[256,512]{1,0:T(8,128)(2,1)S(1)}, bf16[256,512]{1,0:T(8,128)(2,1)S(1)}, u32[]{:S(2)}, u32[]{:S(2)}) collective-permute-start(bf16[256,512]{1,0:T(8,128)(2,1)S(1)} %fusion.30), channel_id=1, source_target_pairs={{0,6},{2,0},{4,2},{6,4},{1,7},{3,1},{5,3},{7,5},{8,14},{10,8},{12,... | collective-permute-start | bytes 786440 | tf_op jit(solution)/shard_map/ppermute | solution.py:32
  77.8 3.3 %collective-permute-done.19 = bf16[256,512]{1,0:T(8,128)(2,1)S(1)} collective-permute-done((bf16[256,512]{1,0:T(8,128)(2,1)S(1)}, bf16[256,512]{1,0:T(8,128)(2,1)S(1)}, u32[]{:S(2)}, u32[]{:S(2)}) %collective-permute-start.19) | collective-permute-done | bytes 262176 | tf_op jit(solution)/shard_map/ppermute | solution.py:32
  81.2 6.4 %collective-permute-done.20 = bf16[256,512]{1,0:T(8,128)(2,1)S(1)} collective-permute-done((bf16[256,512]{1,0:T(8,128)(2,1)S(1)}, bf16[256,512]{1,0:T(8,128)(2,1)S(1)}, u32[]{:S(2)}, u32[]{:S(2)}) %collective-permute-start.20) | collective-permute-done | bytes 262176 | tf_op jit(solution)/shard_map/ppermute | solution.py:32
  87.8 0.2 pad_maximum_fusion.1
  88.0 0.3 copy.12
  88.3 2.2 %convolution_convert_fusion = bf16[1024,512]{1,0:T(8,128)(2,1)} fusion(bf16[1024,1024]{1,0:T(8,128)(2,1)S(1)} %bitcast.126, bf16[1024,512]{1,0:T(8,128)(2,1)S(1)} %pad_maximum_fusion.2), kind=kOutput, calls=%fused_computation.30 | convolution fusion | flops 1074266112 | bytes 4194304 | tf_op jit(solution)/shard_map/dot_general | solution.py:61
  90.5 6.6 %all-to-all-start = ((bf16[64,16,512]{2,1,0:T(8,128)(2,1)}), bf16[64,16,512]{2,1,0:T(8,128)(2,1)S(1)}, u32[]{:S(2)}, u32[]{:S(2)}) async-start(bf16[64,16,512]{2,1,0:T(8,128)(2,1)} %bitcast.127), calls=%async_computation | async-start | bytes 2097152 | tf_op jit(solution)/shard_map/all_to_all | solution.py:188
  97.3 0.8 constant_dynamic-slice_fusion
  98.1 3.0 %collective-permute-start.26 = (bf16[512,512]{1,0:T(8,128)(2,1)}, bf16[512,512]{1,0:T(8,128)(2,1)S(1)}, u32[]{:S(2)}, u32[]{:S(2)}) collective-permute-start(bf16[512,512]{1,0:T(8,128)(2,1)} %constant_dynamic-slice_fusion), channel_id=1, source_target_pairs={{0,128},{8,136},{16,144},{24,152},{32,160},{40,168},{48,176},{56,1... | collective-permute-start | bytes 1572872 | tf_op jit(solution)/shard_map/ppermute | solution.py:23
  101.1 0.4 collective-permute-start.27
  101.5 2.3 %collective-permute-start.28 = (bf16[512,512]{1,0:T(8,128)(2,1)}, bf16[512,512]{1,0:T(8,128)(2,1)}, u32[]{:S(2)}, u32[]{:S(2)}) collective-permute-start(bf16[512,512]{1,0:T(8,128)(2,1)} %constant_dynamic-slice_fusion), channel_id=1, source_target_pairs={{0,192},{8,200},{16,208},{24,216},{32,224},{40,232},{48,240},{56,2... | collective-permute-start | bytes 1572872 | tf_op jit(solution)/shard_map/ppermute | solution.py:23
  103.8 1.7 %shard_map.86 = (bf16[16,2048]{1,0:T(8,128)(2,1)}, bf16[16,2048]{1,0:T(8,128)(2,1)}, bf16[16,2048]{1,0:T(8,128)(2,1)}, bf16[16,2048]{1,0:T(8,128)(2,1)}) custom-call(bf16[16,8192]{1,0:T(8,128)(2,1)} %bitcast.129), custom_call_target="tpu_custom_call" | custom-call | tf_op jit(solution)/shard_map/pallas_call | solution.py:111
  105.5 1.8 %collective-permute-start.22 = (bf16[16,2048]{1,0:T(8,128)(2,1)}, bf16[16,2048]{1,0:T(8,128)(2,1)S(1)}, u32[]{:S(2)}, u32[]{:S(2)}) collective-permute-start(bf16[16,2048]{1,0:T(8,128)(2,1)} %get-tuple-element.46), channel_id=1, source_target_pairs={{0,4},{2,6},{4,0},{6,2},{1,5},{3,7},{5,1},{7,3},{8,12},{10,14},{12... | collective-permute-start | bytes 196616 | tf_op jit(solution)/shard_map/ppermute | solution.py:32
  107.4 1.2 collective-permute-start.23
  108.6 0.9 constant_dynamic-update-slice_fusion.7
  109.4 16.2 %all-to-all-done = bf16[64,16,512]{2,1,0:T(8,128)(2,1)S(1)} async-done(((bf16[64,16,512]{2,1,0:T(8,128)(2,1)}), bf16[64,16,512]{2,1,0:T(8,128)(2,1)S(1)}, u32[]{:S(2)}, u32[]{:S(2)}) %all-to-all-start) | async-done | bytes 1048608 | tf_op jit(solution)/shard_map/all_to_all | solution.py:188
  125.7 0.2 convert_reduce_fusion
  125.8 0.7 fusion.48
  126.5 0.7 broadcast_in_dim.52
  127.2 4.0 %all-to-all-start.1 = ((bf16[8,16,512]{2,1,0:T(8,128)(2,1)}), bf16[8,16,512]{2,1,0:T(8,128)(2,1)S(1)}, u32[]{:S(2)}, u32[]{:S(2)}) async-start(bf16[8,16,512]{2,1,0:T(8,128)(2,1)} %bitcast.24), calls=%async_computation.1 | async-start | bytes 262144 | tf_op jit(solution)/shard_map/all_to_all | solution.py:199
  131.3 2.7 %collective-permute-start.24 = (bf16[16,2048]{1,0:T(8,128)(2,1)S(1)}, bf16[16,2048]{1,0:T(8,128)(2,1)S(1)}, u32[]{:S(2)}, u32[]{:S(2)}) collective-permute-start(bf16[16,2048]{1,0:T(8,128)(2,1)S(1)} %copy-done.6), channel_id=1, source_target_pairs={{0,6},{2,0},{4,2},{6,4},{1,7},{3,1},{5,3},{7,5},{8,14},{10,8},{12,... | collective-permute-start | bytes 196616 | tf_op jit(solution)/shard_map/ppermute | solution.py:32
  133.9 2.6 %all-to-all-done.1 = bf16[8,16,512]{2,1,0:T(8,128)(2,1)S(1)} async-done(((bf16[8,16,512]{2,1,0:T(8,128)(2,1)}), bf16[8,16,512]{2,1,0:T(8,128)(2,1)S(1)}, u32[]{:S(2)}, u32[]{:S(2)}) %all-to-all-start.1) | async-done | bytes 131104 | tf_op jit(solution)/shard_map/all_to_all | solution.py:199
  136.6 2.0 %fusion.17 = f32[128,2048]{1,0:T(8,128)S(1)} fusion(bf16[128,512]{1,0:T(8,128)(2,1)S(1)} %bitcast.130, bf16[512,512]{1,0:T(8,128)(2,1)} %collective-permute-done.28, bf16[512,512]{1,0:T(8,128)(2,1)S(1)} %collective-permute-done.27, bf16[512,512]{1,0:T(8,128)(2,1)S(1)} %collective-permute-done.26, bf16[512,512]{1,0:T(8,128)(2,1)} %constant_dynamic-slice_fusion), kind=kOutput, calls=%fused_computation.21 | convolution fusion | flops 276824064 | bytes 3276800 | tf_op jit(solution)/shard_map/dot_general | solution.py:61
  138.6 1.0 collective-permute-start.29
  139.6 1.1 collective-permute-done.29
  140.9 0.7 collective-permute-start.30
  141.6 1.3 collective-permute-start.31
  142.9 1.4 collective-permute-start.32
  144.5 5.6 %collective-permute-done.30 = bf16[64,2048]{1,0:T(8,128)(2,1)S(1)} collective-permute-done((bf16[64,2048]{1,0:T(8,128)(2,1)S(1)}, bf16[64,2048]{1,0:T(8,128)(2,1)S(1)}, u32[]{:S(2)}, u32[]{:S(2)}) %collective-permute-start.30) | collective-permute-done | bytes 262176 | tf_op jit(solution)/shard_map/ppermute | solution.py:32
  150.1 6.2 %collective-permute-done.31 = bf16[64,2048]{1,0:T(8,128)(2,1)S(1)} collective-permute-done((bf16[64,2048]{1,0:T(8,128)(2,1)S(1)}, bf16[64,2048]{1,0:T(8,128)(2,1)S(1)}, u32[]{:S(2)}, u32[]{:S(2)}) %collective-permute-start.31) | collective-permute-done | bytes 262176 | tf_op jit(solution)/shard_map/ppermute | solution.py:32
  156.5 1.0 copy-done
  (80 shorter events, 1.7 us)
Async XLA Ops:
  0.6 1.0 copy-start.1
  1.7 12.5 %collective-permute-start = (bf16[256,512]{1,0:T(8,128)(2,1)S(1)}, bf16[256,512]{1,0:T(8,128)(2,1)S(1)}, u32[]{:S(2)}, u32[]{:S(2)}) collective-permute-start(bf16[256,512]{1,0:T(8,128)(2,1)S(1)} %get-tuple-element.59), channel_id=1, source_target_pairs={{0,8},{8,16},{16,24},{24,32},{32,40},{40,48},{48,56},{56,0},{64,72... | collective-permute-start | bytes 786440 | tf_op jit(solution)/shard_map/ppermute | solution.py:28
  4.3 10.0 %collective-permute-start.1 = (bf16[256,512]{1,0:T(8,128)(2,1)S(1)}, bf16[256,512]{1,0:T(8,128)(2,1)S(1)}, u32[]{:S(2)}, u32[]{:S(2)}) collective-permute-start(bf16[256,512]{1,0:T(8,128)(2,1)S(1)} %get-tuple-element.59), channel_id=1, source_target_pairs={{0,56},{8,0},{16,8},{24,16},{32,24},{40,32},{48,40},{56,48},{64,12... | collective-permute-start | bytes 786440 | tf_op jit(solution)/shard_map/ppermute | solution.py:28
  14.2 7.9 %collective-permute-start.5 = (bf16[256,512]{1,0:T(8,128)(2,1)S(1)}, bf16[256,512]{1,0:T(8,128)(2,1)S(1)}, u32[]{:S(2)}, u32[]{:S(2)}) collective-permute-start(bf16[256,512]{1,0:T(8,128)(2,1)S(1)} %collective-permute-done.1), channel_id=1, source_target_pairs={{0,56},{8,0},{16,8},{24,16},{32,24},{40,32},{48,40},{56,48},{64,12... | collective-permute-start | bytes 786440 | tf_op jit(solution)/shard_map/ppermute | solution.py:28
  16.7 8.1 %collective-permute-start.10 = (bf16[256,512]{1,0:T(8,128)(2,1)S(1)}, bf16[256,512]{1,0:T(8,128)(2,1)}, u32[]{:S(2)}, u32[]{:S(2)}) collective-permute-start(bf16[256,512]{1,0:T(8,128)(2,1)S(1)} %collective-permute-done), channel_id=1, source_target_pairs={{0,8},{8,16},{16,24},{24,32},{32,40},{40,48},{48,56},{56,0},{64,72... | collective-permute-start | bytes 786440 | tf_op jit(solution)/shard_map/ppermute | solution.py:28
  16.7 16.6 %collective-permute-start.2 = (bf16[128,2048]{1,0:T(8,128)(2,1)}, bf16[128,2048]{1,0:T(8,128)(2,1)}, u32[]{:S(2)}, u32[]{:S(2)}) collective-permute-start(bf16[128,2048]{1,0:T(8,128)(2,1)} %get-tuple-element.33), channel_id=1, source_target_pairs={{0,128},{8,136},{16,144},{24,152},{32,160},{40,168},{48,176},{56,1... | collective-permute-start | bytes 1572872 | tf_op jit(solution)/shard_map/ppermute | solution.py:23
  19.4 24.2 %collective-permute-start.3 = (bf16[128,2048]{1,0:T(8,128)(2,1)}, bf16[128,2048]{1,0:T(8,128)(2,1)}, u32[]{:S(2)}, u32[]{:S(2)}) collective-permute-start(bf16[128,2048]{1,0:T(8,128)(2,1)} %get-tuple-element.34), channel_id=1, source_target_pairs={{0,64},{8,72},{16,80},{24,88},{32,96},{40,104},{48,112},{56,120},{... | collective-permute-start | bytes 1572872 | tf_op jit(solution)/shard_map/ppermute | solution.py:23
  19.7 23.9 %collective-permute-start.4 = (bf16[128,2048]{1,0:T(8,128)(2,1)}, bf16[128,2048]{1,0:T(8,128)(2,1)}, u32[]{:S(2)}, u32[]{:S(2)}) collective-permute-start(bf16[128,2048]{1,0:T(8,128)(2,1)} %get-tuple-element.35), channel_id=1, source_target_pairs={{0,192},{8,200},{16,208},{24,216},{32,224},{40,232},{48,240},{56,2... | collective-permute-start | bytes 1572872 | tf_op jit(solution)/shard_map/ppermute | solution.py:23
  22.1 6.0 %collective-permute-start.6 = (bf16[256,512]{1,0:T(8,128)(2,1)S(1)}, bf16[256,512]{1,0:T(8,128)(2,1)}, u32[]{:S(2)}, u32[]{:S(2)}) collective-permute-start(bf16[256,512]{1,0:T(8,128)(2,1)S(1)} %collective-permute-done.5), channel_id=1, source_target_pairs={{0,56},{8,0},{16,8},{24,16},{32,24},{40,32},{48,40},{56,48},{64,12... | collective-permute-start | bytes 786440 | tf_op jit(solution)/shard_map/ppermute | solution.py:28
  24.8 7.9 %collective-permute-start.11 = (bf16[256,512]{1,0:T(8,128)(2,1)}, bf16[256,512]{1,0:T(8,128)(2,1)}, u32[]{:S(2)}, u32[]{:S(2)}) collective-permute-start(bf16[256,512]{1,0:T(8,128)(2,1)} %collective-permute-done.10), channel_id=1, source_target_pairs={{0,8},{8,16},{16,24},{24,32},{32,40},{40,48},{48,56},{56,0},{64,72... | collective-permute-start | bytes 786440 | tf_op jit(solution)/shard_map/ppermute | solution.py:28
  29.7 13.9 %collective-permute-start.7 = (bf16[32,16,256]{2,1,0:T(8,128)(2,1)S(1)}, bf16[32,16,256]{2,1,0:T(8,128)(2,1)S(1)}, u32[]{:S(2)}, u32[]{:S(2)}) collective-permute-start(bf16[32,16,256]{2,1,0:T(8,128)(2,1)S(1)} %get-tuple-element.69), channel_id=1, source_target_pairs={{0,4},{2,6},{4,0},{6,2},{1,5},{3,7},{5,1},{7,3},{8,12},{10,14},{12... | collective-permute-start | bytes 786440 | tf_op jit(solution)/shard_map/ppermute | solution.py:32
  32.7 10.9 %collective-permute-start.8 = (bf16[32,16,256]{2,1,0:T(8,128)(2,1)S(1)}, bf16[32,16,256]{2,1,0:T(8,128)(2,1)S(1)}, u32[]{:S(2)}, u32[]{:S(2)}) collective-permute-start(bf16[32,16,256]{2,1,0:T(8,128)(2,1)S(1)} %get-tuple-element.68), channel_id=1, source_target_pairs={{0,2},{2,4},{4,6},{6,0},{1,3},{3,5},{5,7},{7,1},{8,10},{10,12},{12... | collective-permute-start | bytes 786440 | tf_op jit(solution)/shard_map/ppermute | solution.py:32
  33.2 19.2 %copy-start.5 = (bf16[128,2048]{1,0:T(8,128)(2,1)S(1)}, bf16[128,2048]{1,0:T(8,128)(2,1)}, u32[]{:S(2)}) copy-start(bf16[128,2048]{1,0:T(8,128)(2,1)} %get-tuple-element.42) | copy-start | bytes 1572868
  33.2 10.4 %collective-permute-start.9 = (bf16[32,16,256]{2,1,0:T(8,128)(2,1)S(1)}, bf16[32,16,256]{2,1,0:T(8,128)(2,1)S(1)}, u32[]{:S(2)}, u32[]{:S(2)}) collective-permute-start(bf16[32,16,256]{2,1,0:T(8,128)(2,1)S(1)} %get-tuple-element.67), channel_id=1, source_target_pairs={{0,6},{2,0},{4,2},{6,4},{1,7},{3,1},{5,3},{7,5},{8,14},{10,8},{12,... | collective-permute-start | bytes 786440 | tf_op jit(solution)/shard_map/ppermute | solution.py:32
  43.6 8.8 %collective-permute-start.12 = (bf16[256,512]{1,0:T(8,128)(2,1)}, bf16[256,512]{1,0:T(8,128)(2,1)S(1)}, u32[]{:S(2)}, u32[]{:S(2)}) collective-permute-start(bf16[256,512]{1,0:T(8,128)(2,1)} %collective-permute-done.11), channel_id=1, source_target_pairs={{0,8},{8,16},{16,24},{24,32},{32,40},{40,48},{48,56},{56,0},{64,72... | collective-permute-start | bytes 786440 | tf_op jit(solution)/shard_map/ppermute | solution.py:28
  43.6 8.8 %collective-permute-start.13 = (bf16[128,2048]{1,0:T(8,128)(2,1)}, bf16[128,2048]{1,0:T(8,128)(2,1)S(1)}, u32[]{:S(2)}, u32[]{:S(2)}) collective-permute-start(bf16[128,2048]{1,0:T(8,128)(2,1)} %collective-permute-done.2), channel_id=1, source_target_pairs={{0,1},{1,0},{2,3},{3,2},{4,5},{5,4},{6,7},{7,6},{8,9},{9,8},{10,11... | collective-permute-start | bytes 1572872 | tf_op jit(solution)/shard_map/ppermute | solution.py:36
  46.0 6.5 %collective-permute-start.14 = (bf16[128,2048]{1,0:T(8,128)(2,1)}, bf16[128,2048]{1,0:T(8,128)(2,1)S(1)}, u32[]{:S(2)}, u32[]{:S(2)}) collective-permute-start(bf16[128,2048]{1,0:T(8,128)(2,1)} %collective-permute-done.3), channel_id=1, source_target_pairs={{0,1},{1,0},{2,3},{3,2},{4,5},{5,4},{6,7},{7,6},{8,9},{9,8},{10,11... | collective-permute-start | bytes 1572872 | tf_op jit(solution)/shard_map/ppermute | solution.py:36
  46.0 6.5 %collective-permute-start.15 = (bf16[128,2048]{1,0:T(8,128)(2,1)}, bf16[128,2048]{1,0:T(8,128)(2,1)S(1)}, u32[]{:S(2)}, u32[]{:S(2)}) collective-permute-start(bf16[128,2048]{1,0:T(8,128)(2,1)} %collective-permute-done.4), channel_id=1, source_target_pairs={{0,1},{1,0},{2,3},{3,2},{4,5},{5,4},{6,7},{7,6},{8,9},{9,8},{10,11... | collective-permute-start | bytes 1572872 | tf_op jit(solution)/shard_map/ppermute | solution.py:36
  46.6 41.0 %collective-permute-start.25 = (bf16[32,16,1024]{2,1,0:T(8,128)(2,1)S(1)}, bf16[32,16,1024]{2,1,0:T(8,128)(2,1)S(1)}, u32[]{:S(2)}, u32[]{:S(2)}) collective-permute-start(bf16[32,16,1024]{2,1,0:T(8,128)(2,1)S(1)} %constant_dynamic-update-slice_fusion), channel_id=1, source_target_pairs={{0,1},{1,0},{2,3},{3,2},{4,5},{5,4},{6,7},{7,6},{8,9},{9,8},{10,11... | collective-permute-start | bytes 3145736 | tf_op jit(solution)/shard_map/ppermute | solution.py:36
  52.4 1.3 copy-start.4
  56.5 8.1 %collective-permute-start.16 = (bf16[256,512]{1,0:T(8,128)(2,1)S(1)}, bf16[256,512]{1,0:T(8,128)(2,1)S(1)}, u32[]{:S(2)}, u32[]{:S(2)}) collective-permute-start(bf16[256,512]{1,0:T(8,128)(2,1)S(1)} %get-tuple-element.64), channel_id=1, source_target_pairs={{0,128},{8,136},{16,144},{24,152},{32,160},{40,168},{48,176},{56,1... | collective-permute-start | bytes 786440 | tf_op jit(solution)/shard_map/ppermute | solution.py:23
  56.6 11.1 %collective-permute-start.17 = (bf16[256,512]{1,0:T(8,128)(2,1)S(1)}, bf16[256,512]{1,0:T(8,128)(2,1)S(1)}, u32[]{:S(2)}, u32[]{:S(2)}) collective-permute-start(bf16[256,512]{1,0:T(8,128)(2,1)S(1)} %get-tuple-element.66), channel_id=1, source_target_pairs={{0,192},{8,200},{16,208},{24,216},{32,224},{40,232},{48,240},{56,2... | collective-permute-start | bytes 786440 | tf_op jit(solution)/shard_map/ppermute | solution.py:23
  57.1 14.9 %collective-permute-start.18 = (bf16[256,512]{1,0:T(8,128)(2,1)S(1)}, bf16[256,512]{1,0:T(8,128)(2,1)S(1)}, u32[]{:S(2)}, u32[]{:S(2)}) collective-permute-start(bf16[256,512]{1,0:T(8,128)(2,1)S(1)} %get-tuple-element.65), channel_id=1, source_target_pairs={{0,64},{8,72},{16,80},{24,88},{32,96},{40,104},{48,112},{56,120},{... | collective-permute-start | bytes 786440 | tf_op jit(solution)/shard_map/ppermute | solution.py:23
  72.1 9.0 %collective-permute-start.19 = (bf16[256,512]{1,0:T(8,128)(2,1)S(1)}, bf16[256,512]{1,0:T(8,128)(2,1)S(1)}, u32[]{:S(2)}, u32[]{:S(2)}) collective-permute-start(bf16[256,512]{1,0:T(8,128)(2,1)S(1)} %fusion.30), channel_id=1, source_target_pairs={{0,4},{2,6},{4,0},{6,2},{1,5},{3,7},{5,1},{7,3},{8,12},{10,14},{12... | collective-permute-start | bytes 786440 | tf_op jit(solution)/shard_map/ppermute | solution.py:32
  75.1 12.4 %collective-permute-start.20 = (bf16[256,512]{1,0:T(8,128)(2,1)S(1)}, bf16[256,512]{1,0:T(8,128)(2,1)S(1)}, u32[]{:S(2)}, u32[]{:S(2)}) collective-permute-start(bf16[256,512]{1,0:T(8,128)(2,1)S(1)} %fusion.30), channel_id=1, source_target_pairs={{0,2},{2,4},{4,6},{6,0},{1,3},{3,5},{5,7},{7,1},{8,10},{10,12},{12... | collective-permute-start | bytes 786440 | tf_op jit(solution)/shard_map/ppermute | solution.py:32
  75.5 12.0 %collective-permute-start.21 = (bf16[256,512]{1,0:T(8,128)(2,1)S(1)}, bf16[256,512]{1,0:T(8,128)(2,1)S(1)}, u32[]{:S(2)}, u32[]{:S(2)}) collective-permute-start(bf16[256,512]{1,0:T(8,128)(2,1)S(1)} %fusion.30), channel_id=1, source_target_pairs={{0,6},{2,0},{4,2},{6,4},{1,7},{3,1},{5,3},{7,5},{8,14},{10,8},{12,... | collective-permute-start | bytes 786440 | tf_op jit(solution)/shard_map/ppermute | solution.py:32
  90.5 35.2 %all-to-all-start = ((bf16[64,16,512]{2,1,0:T(8,128)(2,1)}), bf16[64,16,512]{2,1,0:T(8,128)(2,1)S(1)}, u32[]{:S(2)}, u32[]{:S(2)}) async-start(bf16[64,16,512]{2,1,0:T(8,128)(2,1)} %bitcast.127), calls=%async_computation | async-start | bytes 2097152 | tf_op jit(solution)/shard_map/all_to_all | solution.py:188
  97.1 28.7 %copy-start.2 = (f32[1,16,1024]{2,1,0:T(8,128)S(1)}, f32[1,16,1024]{2,1,0:T(8,128)}, u32[]{:S(2)}) copy-start(f32[1,16,1024]{2,1,0:T(8,128)} %param.10) | copy-start | bytes 196612
  97.1 28.7 %copy-start.3 = (f32[1,16,1024]{2,1,0:T(8,128)S(1)}, f32[1,16,1024]{2,1,0:T(8,128)}, u32[]{:S(2)}) copy-start(f32[1,16,1024]{2,1,0:T(8,128)} %param.11) | copy-start | bytes 196612
  98.1 38.4 %collective-permute-start.26 = (bf16[512,512]{1,0:T(8,128)(2,1)}, bf16[512,512]{1,0:T(8,128)(2,1)S(1)}, u32[]{:S(2)}, u32[]{:S(2)}) collective-permute-start(bf16[512,512]{1,0:T(8,128)(2,1)} %constant_dynamic-slice_fusion), channel_id=1, source_target_pairs={{0,128},{8,136},{16,144},{24,152},{32,160},{40,168},{48,176},{56,1... | collective-permute-start | bytes 1572872 | tf_op jit(solution)/shard_map/ppermute | solution.py:23
  101.1 35.4 %collective-permute-start.27 = (bf16[512,512]{1,0:T(8,128)(2,1)}, bf16[512,512]{1,0:T(8,128)(2,1)S(1)}, u32[]{:S(2)}, u32[]{:S(2)}) collective-permute-start(bf16[512,512]{1,0:T(8,128)(2,1)} %constant_dynamic-slice_fusion), channel_id=1, source_target_pairs={{0,64},{8,72},{16,80},{24,88},{32,96},{40,104},{48,112},{56,120},{... | collective-permute-start | bytes 1572872 | tf_op jit(solution)/shard_map/ppermute | solution.py:23
  101.5 35.0 %collective-permute-start.28 = (bf16[512,512]{1,0:T(8,128)(2,1)}, bf16[512,512]{1,0:T(8,128)(2,1)}, u32[]{:S(2)}, u32[]{:S(2)}) collective-permute-start(bf16[512,512]{1,0:T(8,128)(2,1)} %constant_dynamic-slice_fusion), channel_id=1, source_target_pairs={{0,192},{8,200},{16,208},{24,216},{32,224},{40,232},{48,240},{56,2... | collective-permute-start | bytes 1572872 | tf_op jit(solution)/shard_map/ppermute | solution.py:23
  105.5 25.7 %copy-start.6 = (bf16[16,2048]{1,0:T(8,128)(2,1)S(1)}, bf16[16,2048]{1,0:T(8,128)(2,1)}, u32[]{:S(2)}) copy-start(bf16[16,2048]{1,0:T(8,128)(2,1)} %get-tuple-element.48) | copy-start | bytes 196612
  105.5 25.7 %collective-permute-start.22 = (bf16[16,2048]{1,0:T(8,128)(2,1)}, bf16[16,2048]{1,0:T(8,128)(2,1)S(1)}, u32[]{:S(2)}, u32[]{:S(2)}) collective-permute-start(bf16[16,2048]{1,0:T(8,128)(2,1)} %get-tuple-element.46), channel_id=1, source_target_pairs={{0,4},{2,6},{4,0},{6,2},{1,5},{3,7},{5,1},{7,3},{8,12},{10,14},{12... | collective-permute-start | bytes 196616 | tf_op jit(solution)/shard_map/ppermute | solution.py:32
  107.4 32.2 %collective-permute-start.23 = (bf16[16,2048]{1,0:T(8,128)(2,1)}, bf16[16,2048]{1,0:T(8,128)(2,1)S(1)}, u32[]{:S(2)}, u32[]{:S(2)}) collective-permute-start(bf16[16,2048]{1,0:T(8,128)(2,1)} %get-tuple-element.47), channel_id=1, source_target_pairs={{0,2},{2,4},{4,6},{6,0},{1,3},{3,5},{5,7},{7,1},{8,10},{10,12},{12... | collective-permute-start | bytes 196616 | tf_op jit(solution)/shard_map/ppermute | solution.py:32
  127.2 9.3 %all-to-all-start.1 = ((bf16[8,16,512]{2,1,0:T(8,128)(2,1)}), bf16[8,16,512]{2,1,0:T(8,128)(2,1)S(1)}, u32[]{:S(2)}, u32[]{:S(2)}) async-start(bf16[8,16,512]{2,1,0:T(8,128)(2,1)} %bitcast.24), calls=%async_computation.1 | async-start | bytes 262144 | tf_op jit(solution)/shard_map/all_to_all | solution.py:199
  131.3 8.4 %collective-permute-start.24 = (bf16[16,2048]{1,0:T(8,128)(2,1)S(1)}, bf16[16,2048]{1,0:T(8,128)(2,1)S(1)}, u32[]{:S(2)}, u32[]{:S(2)}) collective-permute-start(bf16[16,2048]{1,0:T(8,128)(2,1)S(1)} %copy-done.6), channel_id=1, source_target_pairs={{0,6},{2,0},{4,2},{6,4},{1,7},{3,1},{5,3},{7,5},{8,14},{10,8},{12,... | collective-permute-start | bytes 196616 | tf_op jit(solution)/shard_map/ppermute | solution.py:32
  138.6 2.1 %collective-permute-start.29 = (bf16[64,2048]{1,0:T(8,128)(2,1)S(1)}, bf16[64,2048]{1,0:T(8,128)(2,1)S(1)}, u32[]{:S(2)}, u32[]{:S(2)}) collective-permute-start(bf16[64,2048]{1,0:T(8,128)(2,1)S(1)} %select_convert_fusion), channel_id=1, source_target_pairs={{0,1},{1,0},{2,3},{3,2},{4,5},{5,4},{6,7},{7,6},{8,9},{9,8},{10,11... | collective-permute-start | bytes 786440 | tf_op jit(solution)/shard_map/ppermute | solution.py:36
  140.9 9.2 %collective-permute-start.30 = (bf16[64,2048]{1,0:T(8,128)(2,1)S(1)}, bf16[64,2048]{1,0:T(8,128)(2,1)S(1)}, u32[]{:S(2)}, u32[]{:S(2)}) collective-permute-start(bf16[64,2048]{1,0:T(8,128)(2,1)S(1)} %subtract_convert_fusion), channel_id=1, source_target_pairs={{0,4},{2,6},{4,0},{6,2},{1,5},{3,7},{5,1},{7,3},{8,12},{10,14},{12... | collective-permute-start | bytes 786440 | tf_op jit(solution)/shard_map/ppermute | solution.py:32
  141.6 14.7 %collective-permute-start.31 = (bf16[64,2048]{1,0:T(8,128)(2,1)S(1)}, bf16[64,2048]{1,0:T(8,128)(2,1)S(1)}, u32[]{:S(2)}, u32[]{:S(2)}) collective-permute-start(bf16[64,2048]{1,0:T(8,128)(2,1)S(1)} %subtract_convert_fusion), channel_id=1, source_target_pairs={{0,2},{2,4},{4,6},{6,0},{1,3},{3,5},{5,7},{7,1},{8,10},{10,12},{12... | collective-permute-start | bytes 786440 | tf_op jit(solution)/shard_map/ppermute | solution.py:32
  142.9 13.5 %collective-permute-start.32 = (bf16[64,2048]{1,0:T(8,128)(2,1)S(1)}, bf16[64,2048]{1,0:T(8,128)(2,1)S(1)}, u32[]{:S(2)}, u32[]{:S(2)}) collective-permute-start(bf16[64,2048]{1,0:T(8,128)(2,1)S(1)} %subtract_convert_fusion), channel_id=1, source_target_pairs={{0,6},{2,0},{4,2},{6,4},{1,7},{3,1},{5,3},{7,5},{8,14},{10,8},{12,... | collective-permute-start | bytes 786440 | tf_op jit(solution)/shard_map/ppermute | solution.py:32
  156.5 1.0 copy-start

commit v3 on v2

--- a/solution.py
+++ b/solution.py
@@ -174,10 +174,10 @@
     low_rank, held = lax.optimization_barrier((low_rank, held))
     slab = quarter // NY
     piece = rows(held, y * slab, slab)
-    kept = jnp.concatenate([piece] + [along_x(piece, d) for d in FAR], axis=0)
+    kept = [piece] + [along_x(piece, d) for d in FAR]
     low = jnp.concatenate([low_rank] + [along_y(low_rank, d) for d in FAR], axis=0)
 
-    weights, low = lax.optimization_barrier((weights[0], low))
+    weights, low_rank_ = lax.optimization_barrier((weights[0], low_rank))
     mine, *leaving = cut_weights(weights)
     old = put(jnp.zeros((NY * 16, quarter), bf16), mine, y * 16, 0)
     for d, piece in zip(FAR, leaving):
@@ -186,6 +186,7 @@
     projected = dot(features.reshape(-1, NY * tokens), low, ((1,), (0,)))
     projected = projected.astype(bf16).reshape(2 * NX * NZ, 16, half)
     got = lax.all_to_all(projected, ("dp", "tensor"), split_axis=0, concat_axis=0, tiled=True)
+    got, old = lax.optimization_barrier((got, old))
     got = got.reshape(NX * NZ, 2, 16, half).astype(f32).sum(axis=0)
     projected = jnp.concatenate([got[0], got[1]], axis=1)[None]
 
@@ -204,7 +205,9 @@
         tiled=True,
     )
     directions = directions.reshape(NY, 2, 16, half).transpose(1, 0, 2, 3).reshape(2, NY * 16, half)
-    both = dot(directions.reshape(-1, half), kept, ((1,), (1,))).reshape(2, NY * 16, quarter)
+    stacked = directions.reshape(-1, half)
+    both = jnp.concatenate([dot(stacked, part, ((1,), (1,))) for part in kept], axis=1)
+    both = both.reshape(2, NY * 16, quarter)
     ours, theirs = jnp.where(first, both[0], both[1]), jnp.where(first, both[1], both[0])
     update = ours + across(theirs.astype(bf16)).astype(f32)
     done = (old.astype(f32) - step_scale * update).astype(bf16)

time: 158 us -> 166 us (1.051)
  waiting for transfers between devices: 71.8 us -> 78.3 us
    ppermute x9, waiting for transfers between devices: 20 us -> 28 us  [along_x(): return lax.ppermute(value, 'dp', pairs)]
    ppermute x12, waiting for transfers between devices: 21.6 us -> 18.7 us  [along_y(): return lax.ppermute(value, 'fsdp', [(y, (y + d) % NY) for y in range(NY)])]
    dot_general x4 -> x7, matrix products: 8.08 us -> 8.34 us  [dot(): lax.dot_general(a, b, ((dims[0], dims[1]), ((), ())), preferred_element_t...]
  transfers between devices with their start and end apart: 35 -> 35, of which waited for: 14 -> 15; matrix products, arithmetic and copies ran while one was open for 9% -> 9% of each run, Pallas kernels for 3% -> 3%
where the time goes in v3:
time: 166 us; the launch traced here: 165 us
  waiting for transfers between devices  78.3 us (47%)
  starting transfers between devices  60.8 us (37%)
  local copies, waits for them, and re-layouts  9.76 us (6%)
  matrix products  8.34 us (5%)
  Pallas kernels  4.98 us (3%)
  other arithmetic  1.74 us (1%)
    ppermute x9, waiting for transfers between devices, along_x(): return lax.ppermute(value, 'dp', pairs)  28 us
    ppermute x12, starting transfers between devices, along_y(): return lax.ppermute(value, 'fsdp', [(y, (y + d) % NY) for y in range(NY)])  21.5 us
    ppermute x12, waiting for transfers between devices, along_y(): return lax.ppermute(value, 'fsdp', [(y, (y + d) % NY) for y in range(NY)])  18.7 us
    all_to_all x1, waiting for transfers between devices, shards(): lax.all_to_all(projected, ('dp', 'tensor'), split_axis=0, concat_axis=0,...  17.4 us
    ppermute x9, starting transfers between devices, along_x(): return lax.ppermute(value, 'dp', pairs)  12.7 us
    ppermute x7, starting transfers between devices, along_z(): return lax.ppermute(value, 'dp', pairs)  11.8 us
    ppermute x7, waiting for transfers between devices, along_z(): return lax.ppermute(value, 'dp', pairs)  10.4 us
    dot_general x7, matrix products, dot(): lax.dot_general(a, b, ((dims[0], dims[1]), ((), ())), preferred_element_t...  8.34 us
  transfers between devices with their start and end apart: 35, of which 15 were waited for; matrix products, arithmetic and copies ran while one was open for 9% of the time, Pallas kernels for 3%

profile of v3, /device:TPU:1, one launch (start us, length us, event | category | flops | bytes accessed | tf_op | source)
XLA Modules:
  0.0 165.2 jit_solution(4368512874484524964)
XLA Ops:
  0.8 0.9 copy-done.1
  1.7 2.5 %collective-permute-start = (bf16[256,512]{1,0:T(8,128)(2,1)S(1)}, bf16[256,512]{1,0:T(8,128)(2,1)S(1)}, u32[]{:S(2)}, u32[]{:S(2)}) collective-permute-start(bf16[256,512]{1,0:T(8,128)(2,1)S(1)} %get-tuple-element.61), channel_id=1, source_target_pairs={{0,8},{8,16},{16,24},{24,32},{32,40},{40,48},{48,56},{56,0},{64,72... | collective-permute-start | bytes 786440 | tf_op jit(solution)/shard_map/ppermute | solution.py:28
  4.3 4.0 %collective-permute-start.1 = (bf16[256,512]{1,0:T(8,128)(2,1)S(1)}, bf16[256,512]{1,0:T(8,128)(2,1)S(1)}, u32[]{:S(2)}, u32[]{:S(2)}) collective-permute-start(bf16[256,512]{1,0:T(8,128)(2,1)S(1)} %get-tuple-element.61), channel_id=1, source_target_pairs={{0,56},{8,0},{16,8},{24,16},{32,24},{40,32},{48,40},{56,48},{64,12... | collective-permute-start | bytes 786440 | tf_op jit(solution)/shard_map/ppermute | solution.py:28
  8.3 3.2 %shard_map.85 = (bf16[128,2048]{1,0:T(8,128)(2,1)}, bf16[128,2048]{1,0:T(8,128)(2,1)}, bf16[128,2048]{1,0:T(8,128)(2,1)}, bf16[128,2048]{1,0:T(8,128)(2,1)}, bf16[128,2048]{1,0:T(8,128)(2,1)}) custom-call(bf16[256,8192]{1,0:T(8,128)(2,1)} %act_ref.1), custom_call_target="tpu_custom_call" | custom-call | tf_op jit(solution)/shard_map/pallas_call | solution.py:82
  11.5 2.7 %collective-permute-done = bf16[256,512]{1,0:T(8,128)(2,1)S(1)} collective-permute-done((bf16[256,512]{1,0:T(8,128)(2,1)S(1)}, bf16[256,512]{1,0:T(8,128)(2,1)S(1)}, u32[]{:S(2)}, u32[]{:S(2)}) %collective-permute-start) | collective-permute-done | bytes 262176 | tf_op jit(solution)/shard_map/ppermute | solution.py:28
  14.2 2.4 %collective-permute-start.5 = (bf16[256,512]{1,0:T(8,128)(2,1)S(1)}, bf16[256,512]{1,0:T(8,128)(2,1)S(1)}, u32[]{:S(2)}, u32[]{:S(2)}) collective-permute-start(bf16[256,512]{1,0:T(8,128)(2,1)S(1)} %collective-permute-done.1), channel_id=1, source_target_pairs={{0,56},{8,0},{16,8},{24,16},{32,24},{40,32},{48,40},{56,48},{64,12... | collective-permute-start | bytes 786440 | tf_op jit(solution)/shard_map/ppermute | solution.py:28
  16.7 2.7 %collective-permute-start.2 = (bf16[128,2048]{1,0:T(8,128)(2,1)}, bf16[128,2048]{1,0:T(8,128)(2,1)}, u32[]{:S(2)}, u32[]{:S(2)}) collective-permute-start(bf16[128,2048]{1,0:T(8,128)(2,1)} %get-tuple-element.33), channel_id=1, source_target_pairs={{0,128},{8,136},{16,144},{24,152},{32,160},{40,168},{48,176},{56,1... | collective-permute-start | bytes 1572872 | tf_op jit(solution)/shard_map/ppermute | solution.py:23
  19.4 0.3 collective-permute-start.3
  19.7 2.4 %collective-permute-start.4 = (bf16[128,2048]{1,0:T(8,128)(2,1)}, bf16[128,2048]{1,0:T(8,128)(2,1)}, u32[]{:S(2)}, u32[]{:S(2)}) collective-permute-start(bf16[128,2048]{1,0:T(8,128)(2,1)} %get-tuple-element.35), channel_id=1, source_target_pairs={{0,192},{8,200},{16,208},{24,216},{32,224},{40,232},{48,240},{56,2... | collective-permute-start | bytes 1572872 | tf_op jit(solution)/shard_map/ppermute | solution.py:23
  22.1 2.7 %collective-permute-start.6 = (bf16[256,512]{1,0:T(8,128)(2,1)S(1)}, bf16[256,512]{1,0:T(8,128)(2,1)}, u32[]{:S(2)}, u32[]{:S(2)}) collective-permute-start(bf16[256,512]{1,0:T(8,128)(2,1)S(1)} %collective-permute-done.5), channel_id=1, source_target_pairs={{0,56},{8,0},{16,8},{24,16},{32,24},{40,32},{48,40},{56,48},{64,12... | collective-permute-start | bytes 786440 | tf_op jit(solution)/shard_map/ppermute | solution.py:28
  24.9 1.0 constant_dynamic-update-slice_fusion.12
  25.9 2.2 %collective-permute-done.6 = bf16[256,512]{1,0:T(8,128)(2,1)} collective-permute-done((bf16[256,512]{1,0:T(8,128)(2,1)S(1)}, bf16[256,512]{1,0:T(8,128)(2,1)}, u32[]{:S(2)}, u32[]{:S(2)}) %collective-permute-start.6) | collective-permute-done | bytes 262176 | tf_op jit(solution)/shard_map/ppermute | solution.py:28
  28.1 1.5 copy.11
  29.7 3.0 %collective-permute-start.7 = (bf16[32,16,256]{2,1,0:T(8,128)(2,1)S(1)}, bf16[32,16,256]{2,1,0:T(8,128)(2,1)S(1)}, u32[]{:S(2)}, u32[]{:S(2)}) collective-permute-start(bf16[32,16,256]{2,1,0:T(8,128)(2,1)S(1)} %get-tuple-element.71), channel_id=1, source_target_pairs={{0,4},{2,6},{4,0},{6,2},{1,5},{3,7},{5,1},{7,3},{8,12},{10,14},{12... | collective-permute-start | bytes 786440 | tf_op jit(solution)/shard_map/ppermute | solution.py:32
  32.7 0.5 collective-permute-start.8
  33.2 2.2 %collective-permute-start.9 = (bf16[32,16,256]{2,1,0:T(8,128)(2,1)S(1)}, bf16[32,16,256]{2,1,0:T(8,128)(2,1)S(1)}, u32[]{:S(2)}, u32[]{:S(2)}) collective-permute-start(bf16[32,16,256]{2,1,0:T(8,128)(2,1)S(1)} %get-tuple-element.69), channel_id=1, source_target_pairs={{0,6},{2,0},{4,2},{6,4},{1,7},{3,1},{5,3},{7,5},{8,14},{10,8},{12,... | collective-permute-start | bytes 786440 | tf_op jit(solution)/shard_map/ppermute | solution.py:32
  35.4 1.0 constant_dynamic-update-slice_fusion.10
  36.4 1.0 constant_dynamic-update-slice_fusion.9
  37.4 6.2 %collective-permute-done.3 = bf16[128,2048]{1,0:T(8,128)(2,1)} collective-permute-done((bf16[128,2048]{1,0:T(8,128)(2,1)}, bf16[128,2048]{1,0:T(8,128)(2,1)}, u32[]{:S(2)}, u32[]{:S(2)}) %collective-permute-start.3) | collective-permute-done | bytes 524320 | tf_op jit(solution)/shard_map/ppermute | solution.py:23
  43.6 2.4 %collective-permute-start.14 = (bf16[128,2048]{1,0:T(8,128)(2,1)}, bf16[128,2048]{1,0:T(8,128)(2,1)S(1)}, u32[]{:S(2)}, u32[]{:S(2)}) collective-permute-start(bf16[128,2048]{1,0:T(8,128)(2,1)} %collective-permute-done.2), channel_id=1, source_target_pairs={{0,1},{1,0},{2,3},{3,2},{4,5},{5,4},{6,7},{7,6},{8,9},{9,8},{10,11... | collective-permute-start | bytes 1572872 | tf_op jit(solution)/shard_map/ppermute | solution.py:36
  46.0 0.5 collective-permute-start.16
  46.6 0.3 collective-permute-start.10
  46.9 5.5 %collective-permute-done.13 = bf16[256,512]{1,0:T(8,128)(2,1)S(1)} collective-permute-done((bf16[256,512]{1,0:T(8,128)(2,1)}, bf16[256,512]{1,0:T(8,128)(2,1)S(1)}, u32[]{:S(2)}, u32[]{:S(2)}) %collective-permute-start.13) | collective-permute-done | bytes 262176 | tf_op jit(solution)/shard_map/ppermute | solution.py:28
  52.5 1.2 fusion.9
  53.7 2.6 %broadcast_select_fusion = (f32[512,512]{1,0:T(8,128)S(1)}, f32[512,512]{1,0:T(8,128)S(1)}) fusion(f32[512,512]{1,0:T(8,128)S(1)} %fusion.9, pred[]{:T(512)S(6)} %eq.3, bf16[2048,512]{1,0:T(8,128)(2,1)S(1)} %constant_dynamic-update-slice_fusion.8, bf16[128,2048]{1,0:T(8,128)(2,1)} %collective-permute-done.4, bf16[128,2048]{1,0:T(8,128)(2,1)} %collective-permute-done.3, ...), kind=kOutput, calls=%fused_computation.41 | convolution fusion | flops 1082654720 | bytes 7340033 | tf_op jit(solution)/shard_map/dot_general | solution.py:61
  56.6 0.5 collective-permute-start.18
  57.1 1.1 collective-permute-start.19
  58.2 6.5 %collective-permute-done.17 = bf16[256,512]{1,0:T(8,128)(2,1)S(1)} collective-permute-done((bf16[256,512]{1,0:T(8,128)(2,1)S(1)}, bf16[256,512]{1,0:T(8,128)(2,1)S(1)}, u32[]{:S(2)}, u32[]{:S(2)}) %collective-permute-start.17) | collective-permute-done | bytes 262176 | tf_op jit(solution)/shard_map/ppermute | solution.py:23
  64.7 3.1 %collective-permute-done.18 = bf16[256,512]{1,0:T(8,128)(2,1)S(1)} collective-permute-done((bf16[256,512]{1,0:T(8,128)(2,1)S(1)}, bf16[256,512]{1,0:T(8,128)(2,1)S(1)}, u32[]{:S(2)}, u32[]{:S(2)}) %collective-permute-start.18) | collective-permute-done | bytes 262176 | tf_op jit(solution)/shard_map/ppermute | solution.py:23
  67.8 4.2 %collective-permute-done.19 = bf16[256,512]{1,0:T(8,128)(2,1)S(1)} collective-permute-done((bf16[256,512]{1,0:T(8,128)(2,1)S(1)}, bf16[256,512]{1,0:T(8,128)(2,1)S(1)}, u32[]{:S(2)}, u32[]{:S(2)}) %collective-permute-start.19) | collective-permute-done | bytes 262176 | tf_op jit(solution)/shard_map/ppermute | solution.py:23
  72.2 3.0 %collective-permute-start.20 = (bf16[256,512]{1,0:T(8,128)(2,1)S(1)}, bf16[256,512]{1,0:T(8,128)(2,1)S(1)}, u32[]{:S(2)}, u32[]{:S(2)}) collective-permute-start(bf16[256,512]{1,0:T(8,128)(2,1)S(1)} %fusion.29), channel_id=1, source_target_pairs={{0,4},{2,6},{4,0},{6,2},{1,5},{3,7},{5,1},{7,3},{8,12},{10,14},{12... | collective-permute-start | bytes 786440 | tf_op jit(solution)/shard_map/ppermute | solution.py:32
  75.2 0.4 collective-permute-start.21
  75.6 2.3 %collective-permute-start.22 = (bf16[256,512]{1,0:T(8,128)(2,1)S(1)}, bf16[256,512]{1,0:T(8,128)(2,1)S(1)}, u32[]{:S(2)}, u32[]{:S(2)}) collective-permute-start(bf16[256,512]{1,0:T(8,128)(2,1)S(1)} %fusion.29), channel_id=1, source_target_pairs={{0,6},{2,0},{4,2},{6,4},{1,7},{3,1},{5,3},{7,5},{8,14},{10,8},{12,... | collective-permute-start | bytes 786440 | tf_op jit(solution)/shard_map/ppermute | solution.py:32
  78.4 2.7 %collective-permute-done.20 = bf16[256,512]{1,0:T(8,128)(2,1)S(1)} collective-permute-done((bf16[256,512]{1,0:T(8,128)(2,1)S(1)}, bf16[256,512]{1,0:T(8,128)(2,1)S(1)}, u32[]{:S(2)}, u32[]{:S(2)}) %collective-permute-start.20) | collective-permute-done | bytes 262176 | tf_op jit(solution)/shard_map/ppermute | solution.py:32
  81.2 6.4 %collective-permute-done.21 = bf16[256,512]{1,0:T(8,128)(2,1)S(1)} collective-permute-done((bf16[256,512]{1,0:T(8,128)(2,1)S(1)}, bf16[256,512]{1,0:T(8,128)(2,1)S(1)}, u32[]{:S(2)}, u32[]{:S(2)}) %collective-permute-start.21) | collective-permute-done | bytes 262176 | tf_op jit(solution)/shard_map/ppermute | solution.py:32
  87.6 2.2 %convolution_convert_fusion = bf16[1024,512]{1,0:T(8,128)(2,1)} fusion(bf16[1024,1024]{1,0:T(8,128)(2,1)S(1)} %bitcast.136, bf16[256,512]{1,0:T(8,128)(2,1)S(1)} %collective-permute-done.22, bf16[256,512]{1,0:T(8,128)(2,1)S(1)} %collective-permute-done.21, bf16[256,512]{1,0:T(8,128)(2,1)S(1)} %collective-permute-done.20, bf16[256,512]{1,0:T(8,128)(2,1)S(1)} %fusion.29), kind=kOutput, calls=%fused_computation.22 | convolution fusion | flops 1078460416 | bytes 4194304 | tf_op jit(solution)/shard_map/dot_general | solution.py:61
  89.8 6.6 %all-to-all-start = ((bf16[64,16,512]{2,1,0:T(8,128)(2,1)}), bf16[64,16,512]{2,1,0:T(8,128)(2,1)S(1)}, u32[]{:S(2)}, u32[]{:S(2)}) async-start(bf16[64,16,512]{2,1,0:T(8,128)(2,1)} %bitcast.137), calls=%async_computation | async-start | bytes 2097152 | tf_op jit(solution)/shard_map/all_to_all | solution.py:188
  96.5 1.8 %shard_map.86 = (bf16[16,2048]{1,0:T(8,128)(2,1)}, bf16[16,2048]{1,0:T(8,128)(2,1)}, bf16[16,2048]{1,0:T(8,128)(2,1)}, bf16[16,2048]{1,0:T(8,128)(2,1)}) custom-call(bf16[16,8192]{1,0:T(8,128)(2,1)} %bitcast.139), custom_call_target="tpu_custom_call" | custom-call | tf_op jit(solution)/shard_map/pallas_call | solution.py:111
  98.2 1.8 %collective-permute-start.23 = (bf16[16,2048]{1,0:T(8,128)(2,1)}, bf16[16,2048]{1,0:T(8,128)(2,1)S(1)}, u32[]{:S(2)}, u32[]{:S(2)}) collective-permute-start(bf16[16,2048]{1,0:T(8,128)(2,1)} %get-tuple-element.51), channel_id=1, source_target_pairs={{0,4},{2,6},{4,0},{6,2},{1,5},{3,7},{5,1},{7,3},{8,12},{10,14},{12... | collective-permute-start | bytes 196616 | tf_op jit(solution)/shard_map/ppermute | solution.py:32
  100.1 1.2 collective-permute-start.24
  101.3 1.5 collective-permute-start.25
  102.7 0.8 constant_dynamic-slice_fusion
  103.6 3.0 %collective-permute-start.26 = (bf16[512,512]{1,0:T(8,128)(2,1)}, bf16[512,512]{1,0:T(8,128)(2,1)S(1)}, u32[]{:S(2)}, u32[]{:S(2)}) collective-permute-start(bf16[512,512]{1,0:T(8,128)(2,1)} %constant_dynamic-slice_fusion), channel_id=1, source_target_pairs={{0,128},{8,136},{16,144},{24,152},{32,160},{40,168},{48,176},{56,1... | collective-permute-start | bytes 1572872 | tf_op jit(solution)/shard_map/ppermute | solution.py:23
  106.6 0.9 constant_dynamic-update-slice_fusion.7
  107.5 17.4 %all-to-all-done = bf16[64,16,512]{2,1,0:T(8,128)(2,1)S(1)} async-done(((bf16[64,16,512]{2,1,0:T(8,128)(2,1)}), bf16[64,16,512]{2,1,0:T(8,128)(2,1)S(1)}, u32[]{:S(2)}, u32[]{:S(2)}) %all-to-all-start) | async-done | bytes 1048608 | tf_op jit(solution)/shard_map/all_to_all | solution.py:188
  125.2 0.7 fusion.47
  125.9 0.7 broadcast_in_dim.52
  126.5 4.1 %all-to-all-start.1 = ((bf16[8,16,512]{2,1,0:T(8,128)(2,1)}), bf16[8,16,512]{2,1,0:T(8,128)(2,1)S(1)}, u32[]{:S(2)}, u32[]{:S(2)}) async-start(bf16[8,16,512]{2,1,0:T(8,128)(2,1)} %bitcast.24), calls=%async_computation.1 | async-start | bytes 262144 | tf_op jit(solution)/shard_map/all_to_all | solution.py:200
  130.7 1.1 collective-permute-start.27
  131.8 1.6 collective-permute-start.28
  133.4 2.6 %all-to-all-done.1 = bf16[8,16,512]{2,1,0:T(8,128)(2,1)S(1)} async-done(((bf16[8,16,512]{2,1,0:T(8,128)(2,1)}), bf16[8,16,512]{2,1,0:T(8,128)(2,1)S(1)}, u32[]{:S(2)}, u32[]{:S(2)}) %all-to-all-start.1) | async-done | bytes 131104 | tf_op jit(solution)/shard_map/all_to_all | solution.py:200
  136.0 1.3 fusion.53
  137.3 0.3 fusion.54
  137.6 8.0 %collective-permute-done.27 = bf16[512,512]{1,0:T(8,128)(2,1)S(1)} collective-permute-done((bf16[512,512]{1,0:T(8,128)(2,1)}, bf16[512,512]{1,0:T(8,128)(2,1)S(1)}, u32[]{:S(2)}, u32[]{:S(2)}) %collective-permute-start.27) | collective-permute-done | bytes 524320 | tf_op jit(solution)/shard_map/ppermute | solution.py:23
  145.7 0.3 fusion.55
  146.0 0.3 fusion.56
  146.4 0.9 collective-permute-start.29
  147.3 1.2 collective-permute-done.29
  148.6 3.0 %collective-permute-start.30 = (bf16[64,2048]{1,0:T(8,128)(2,1)S(1)}, bf16[64,2048]{1,0:T(8,128)(2,1)S(1)}, u32[]{:S(2)}, u32[]{:S(2)}) collective-permute-start(bf16[64,2048]{1,0:T(8,128)(2,1)S(1)} %subtract_convert_fusion), channel_id=1, source_target_pairs={{0,4},{2,6},{4,0},{6,2},{1,5},{3,7},{5,1},{7,3},{8,12},{10,14},{12... | collective-permute-start | bytes 786440 | tf_op jit(solution)/shard_map/ppermute | solution.py:32
  151.6 0.3 collective-permute-start.31
  151.8 2.4 %collective-permute-start.32 = (bf16[64,2048]{1,0:T(8,128)(2,1)S(1)}, bf16[64,2048]{1,0:T(8,128)(2,1)S(1)}, u32[]{:S(2)}, u32[]{:S(2)}) collective-permute-start(bf16[64,2048]{1,0:T(8,128)(2,1)S(1)} %subtract_convert_fusion), channel_id=1, source_target_pairs={{0,6},{2,0},{4,2},{6,4},{1,7},{3,1},{5,3},{7,5},{8,14},{10,8},{12,... | collective-permute-start | bytes 786440 | tf_op jit(solution)/shard_map/ppermute | solution.py:32
  154.4 3.3 %collective-permute-done.30 = bf16[64,2048]{1,0:T(8,128)(2,1)S(1)} collective-permute-done((bf16[64,2048]{1,0:T(8,128)(2,1)S(1)}, bf16[64,2048]{1,0:T(8,128)(2,1)S(1)}, u32[]{:S(2)}, u32[]{:S(2)}) %collective-permute-start.30) | collective-permute-done | bytes 262176 | tf_op jit(solution)/shard_map/ppermute | solution.py:32
  157.8 6.2 %collective-permute-done.31 = bf16[64,2048]{1,0:T(8,128)(2,1)S(1)} collective-permute-done((bf16[64,2048]{1,0:T(8,128)(2,1)S(1)}, bf16[64,2048]{1,0:T(8,128)(2,1)S(1)}, u32[]{:S(2)}, u32[]{:S(2)}) %collective-permute-start.31) | collective-permute-done | bytes 262176 | tf_op jit(solution)/shard_map/ppermute | solution.py:32
  164.2 1.0 copy-done
  (81 shorter events, 2.4 us)
Async XLA Ops:
  0.6 1.0 copy-start.1
  1.7 12.5 %collective-permute-start = (bf16[256,512]{1,0:T(8,128)(2,1)S(1)}, bf16[256,512]{1,0:T(8,128)(2,1)S(1)}, u32[]{:S(2)}, u32[]{:S(2)}) collective-permute-start(bf16[256,512]{1,0:T(8,128)(2,1)S(1)} %get-tuple-element.61), channel_id=1, source_target_pairs={{0,8},{8,16},{16,24},{24,32},{32,40},{40,48},{48,56},{56,0},{64,72... | collective-permute-start | bytes 786440 | tf_op jit(solution)/shard_map/ppermute | solution.py:28
  4.3 10.0 %collective-permute-start.1 = (bf16[256,512]{1,0:T(8,128)(2,1)S(1)}, bf16[256,512]{1,0:T(8,128)(2,1)S(1)}, u32[]{:S(2)}, u32[]{:S(2)}) collective-permute-start(bf16[256,512]{1,0:T(8,128)(2,1)S(1)} %get-tuple-element.61), channel_id=1, source_target_pairs={{0,56},{8,0},{16,8},{24,16},{32,24},{40,32},{48,40},{56,48},{64,12... | collective-permute-start | bytes 786440 | tf_op jit(solution)/shard_map/ppermute | solution.py:28
  14.2 7.9 %collective-permute-start.5 = (bf16[256,512]{1,0:T(8,128)(2,1)S(1)}, bf16[256,512]{1,0:T(8,128)(2,1)S(1)}, u32[]{:S(2)}, u32[]{:S(2)}) collective-permute-start(bf16[256,512]{1,0:T(8,128)(2,1)S(1)} %collective-permute-done.1), channel_id=1, source_target_pairs={{0,56},{8,0},{16,8},{24,16},{32,24},{40,32},{48,40},{56,48},{64,12... | collective-permute-start | bytes 786440 | tf_op jit(solution)/shard_map/ppermute | solution.py:28
  16.7 8.1 %collective-permute-start.11 = (bf16[256,512]{1,0:T(8,128)(2,1)S(1)}, bf16[256,512]{1,0:T(8,128)(2,1)}, u32[]{:S(2)}, u32[]{:S(2)}) collective-permute-start(bf16[256,512]{1,0:T(8,128)(2,1)S(1)} %collective-permute-done), channel_id=1, source_target_pairs={{0,8},{8,16},{16,24},{24,32},{32,40},{40,48},{48,56},{56,0},{64,72... | collective-permute-start | bytes 786440 | tf_op jit(solution)/shard_map/ppermute | solution.py:28
  16.7 16.6 %collective-permute-start.2 = (bf16[128,2048]{1,0:T(8,128)(2,1)}, bf16[128,2048]{1,0:T(8,128)(2,1)}, u32[]{:S(2)}, u32[]{:S(2)}) collective-permute-start(bf16[128,2048]{1,0:T(8,128)(2,1)} %get-tuple-element.33), channel_id=1, source_target_pairs={{0,128},{8,136},{16,144},{24,152},{32,160},{40,168},{48,176},{56,1... | collective-permute-start | bytes 1572872 | tf_op jit(solution)/shard_map/ppermute | solution.py:23
  19.4 24.2 %collective-permute-start.3 = (bf16[128,2048]{1,0:T(8,128)(2,1)}, bf16[128,2048]{1,0:T(8,128)(2,1)}, u32[]{:S(2)}, u32[]{:S(2)}) collective-permute-start(bf16[128,2048]{1,0:T(8,128)(2,1)} %get-tuple-element.34), channel_id=1, source_target_pairs={{0,64},{8,72},{16,80},{24,88},{32,96},{40,104},{48,112},{56,120},{... | collective-permute-start | bytes 1572872 | tf_op jit(solution)/shard_map/ppermute | solution.py:23
  19.7 23.9 %collective-permute-start.4 = (bf16[128,2048]{1,0:T(8,128)(2,1)}, bf16[128,2048]{1,0:T(8,128)(2,1)}, u32[]{:S(2)}, u32[]{:S(2)}) collective-permute-start(bf16[128,2048]{1,0:T(8,128)(2,1)} %get-tuple-element.35), channel_id=1, source_target_pairs={{0,192},{8,200},{16,208},{24,216},{32,224},{40,232},{48,240},{56,2... | collective-permute-start | bytes 1572872 | tf_op jit(solution)/shard_map/ppermute | solution.py:23
  22.1 6.0 %collective-permute-start.6 = (bf16[256,512]{1,0:T(8,128)(2,1)S(1)}, bf16[256,512]{1,0:T(8,128)(2,1)}, u32[]{:S(2)}, u32[]{:S(2)}) collective-permute-start(bf16[256,512]{1,0:T(8,128)(2,1)S(1)} %collective-permute-done.5), channel_id=1, source_target_pairs={{0,56},{8,0},{16,8},{24,16},{32,24},{40,32},{48,40},{56,48},{64,12... | collective-permute-start | bytes 786440 | tf_op jit(solution)/shard_map/ppermute | solution.py:28
  24.8 7.9 %collective-permute-start.12 = (bf16[256,512]{1,0:T(8,128)(2,1)}, bf16[256,512]{1,0:T(8,128)(2,1)}, u32[]{:S(2)}, u32[]{:S(2)}) collective-permute-start(bf16[256,512]{1,0:T(8,128)(2,1)} %collective-permute-done.11), channel_id=1, source_target_pairs={{0,8},{8,16},{16,24},{24,32},{32,40},{40,48},{48,56},{56,0},{64,72... | collective-permute-start | bytes 786440 | tf_op jit(solution)/shard_map/ppermute | solution.py:28
  29.7 13.9 %collective-permute-start.7 = (bf16[32,16,256]{2,1,0:T(8,128)(2,1)S(1)}, bf16[32,16,256]{2,1,0:T(8,128)(2,1)S(1)}, u32[]{:S(2)}, u32[]{:S(2)}) collective-permute-start(bf16[32,16,256]{2,1,0:T(8,128)(2,1)S(1)} %get-tuple-element.71), channel_id=1, source_target_pairs={{0,4},{2,6},{4,0},{6,2},{1,5},{3,7},{5,1},{7,3},{8,12},{10,14},{12... | collective-permute-start | bytes 786440 | tf_op jit(solution)/shard_map/ppermute | solution.py:32
  32.7 10.9 %collective-permute-start.8 = (bf16[32,16,256]{2,1,0:T(8,128)(2,1)S(1)}, bf16[32,16,256]{2,1,0:T(8,128)(2,1)S(1)}, u32[]{:S(2)}, u32[]{:S(2)}) collective-permute-start(bf16[32,16,256]{2,1,0:T(8,128)(2,1)S(1)} %get-tuple-element.70), channel_id=1, source_target_pairs={{0,2},{2,4},{4,6},{6,0},{1,3},{3,5},{5,7},{7,1},{8,10},{10,12},{12... | collective-permute-start | bytes 786440 | tf_op jit(solution)/shard_map/ppermute | solution.py:32
  33.2 19.2 %copy-start.5 = (bf16[128,2048]{1,0:T(8,128)(2,1)S(1)}, bf16[128,2048]{1,0:T(8,128)(2,1)}, u32[]{:S(2)}) copy-start(bf16[128,2048]{1,0:T(8,128)(2,1)} %get-tuple-element.47) | copy-start | bytes 1572868
  33.2 10.4 %collective-permute-start.9 = (bf16[32,16,256]{2,1,0:T(8,128)(2,1)S(1)}, bf16[32,16,256]{2,1,0:T(8,128)(2,1)S(1)}, u32[]{:S(2)}, u32[]{:S(2)}) collective-permute-start(bf16[32,16,256]{2,1,0:T(8,128)(2,1)S(1)} %get-tuple-element.69), channel_id=1, source_target_pairs={{0,6},{2,0},{4,2},{6,4},{1,7},{3,1},{5,3},{7,5},{8,14},{10,8},{12,... | collective-permute-start | bytes 786440 | tf_op jit(solution)/shard_map/ppermute | solution.py:32
  43.6 8.8 %collective-permute-start.13 = (bf16[256,512]{1,0:T(8,128)(2,1)}, bf16[256,512]{1,0:T(8,128)(2,1)S(1)}, u32[]{:S(2)}, u32[]{:S(2)}) collective-permute-start(bf16[256,512]{1,0:T(8,128)(2,1)} %collective-permute-done.12), channel_id=1, source_target_pairs={{0,8},{8,16},{16,24},{24,32},{32,40},{40,48},{48,56},{56,0},{64,72... | collective-permute-start | bytes 786440 | tf_op jit(solution)/shard_map/ppermute | solution.py:28
  43.6 8.8 %collective-permute-start.14 = (bf16[128,2048]{1,0:T(8,128)(2,1)}, bf16[128,2048]{1,0:T(8,128)(2,1)S(1)}, u32[]{:S(2)}, u32[]{:S(2)}) collective-permute-start(bf16[128,2048]{1,0:T(8,128)(2,1)} %collective-permute-done.2), channel_id=1, source_target_pairs={{0,1},{1,0},{2,3},{3,2},{4,5},{5,4},{6,7},{7,6},{8,9},{9,8},{10,11... | collective-permute-start | bytes 1572872 | tf_op jit(solution)/shard_map/ppermute | solution.py:36
  46.0 6.5 %collective-permute-start.15 = (bf16[128,2048]{1,0:T(8,128)(2,1)}, bf16[128,2048]{1,0:T(8,128)(2,1)S(1)}, u32[]{:S(2)}, u32[]{:S(2)}) collective-permute-start(bf16[128,2048]{1,0:T(8,128)(2,1)} %collective-permute-done.3), channel_id=1, source_target_pairs={{0,1},{1,0},{2,3},{3,2},{4,5},{5,4},{6,7},{7,6},{8,9},{9,8},{10,11... | collective-permute-start | bytes 1572872 | tf_op jit(solution)/shard_map/ppermute | solution.py:36
  46.0 6.5 %collective-permute-start.16 = (bf16[128,2048]{1,0:T(8,128)(2,1)}, bf16[128,2048]{1,0:T(8,128)(2,1)S(1)}, u32[]{:S(2)}, u32[]{:S(2)}) collective-permute-start(bf16[128,2048]{1,0:T(8,128)(2,1)} %collective-permute-done.4), channel_id=1, source_target_pairs={{0,1},{1,0},{2,3},{3,2},{4,5},{5,4},{6,7},{7,6},{8,9},{9,8},{10,11... | collective-permute-start | bytes 1572872 | tf_op jit(solution)/shard_map/ppermute | solution.py:36
  46.6 31.2 %collective-permute-start.10 = (bf16[32,16,1024]{2,1,0:T(8,128)(2,1)S(1)}, bf16[32,16,1024]{2,1,0:T(8,128)(2,1)S(1)}, u32[]{:S(2)}, u32[]{:S(2)}) collective-permute-start(bf16[32,16,1024]{2,1,0:T(8,128)(2,1)S(1)} %constant_dynamic-update-slice_fusion), channel_id=1, source_target_pairs={{0,1},{1,0},{2,3},{3,2},{4,5},{5,4},{6,7},{7,6},{8,9},{9,8},{10,11... | collective-permute-start | bytes 3145736 | tf_op jit(solution)/shard_map/ppermute | solution.py:36
  52.4 1.3 copy-start.4
  56.5 8.1 %collective-permute-start.17 = (bf16[256,512]{1,0:T(8,128)(2,1)S(1)}, bf16[256,512]{1,0:T(8,128)(2,1)S(1)}, u32[]{:S(2)}, u32[]{:S(2)}) collective-permute-start(bf16[256,512]{1,0:T(8,128)(2,1)S(1)} %get-tuple-element.66), channel_id=1, source_target_pairs={{0,128},{8,136},{16,144},{24,152},{32,160},{40,168},{48,176},{56,1... | collective-permute-start | bytes 786440 | tf_op jit(solution)/shard_map/ppermute | solution.py:23
  56.6 11.1 %collective-permute-start.18 = (bf16[256,512]{1,0:T(8,128)(2,1)S(1)}, bf16[256,512]{1,0:T(8,128)(2,1)S(1)}, u32[]{:S(2)}, u32[]{:S(2)}) collective-permute-start(bf16[256,512]{1,0:T(8,128)(2,1)S(1)} %get-tuple-element.68), channel_id=1, source_target_pairs={{0,192},{8,200},{16,208},{24,216},{32,224},{40,232},{48,240},{56,2... | collective-permute-start | bytes 786440 | tf_op jit(solution)/shard_map/ppermute | solution.py:23
  57.1 14.9 %collective-permute-start.19 = (bf16[256,512]{1,0:T(8,128)(2,1)S(1)}, bf16[256,512]{1,0:T(8,128)(2,1)S(1)}, u32[]{:S(2)}, u32[]{:S(2)}) collective-permute-start(bf16[256,512]{1,0:T(8,128)(2,1)S(1)} %get-tuple-element.67), channel_id=1, source_target_pairs={{0,64},{8,72},{16,80},{24,88},{32,96},{40,104},{48,112},{56,120},{... | collective-permute-start | bytes 786440 | tf_op jit(solution)/shard_map/ppermute | solution.py:23
  72.2 9.0 %collective-permute-start.20 = (bf16[256,512]{1,0:T(8,128)(2,1)S(1)}, bf16[256,512]{1,0:T(8,128)(2,1)S(1)}, u32[]{:S(2)}, u32[]{:S(2)}) collective-permute-start(bf16[256,512]{1,0:T(8,128)(2,1)S(1)} %fusion.29), channel_id=1, source_target_pairs={{0,4},{2,6},{4,0},{6,2},{1,5},{3,7},{5,1},{7,3},{8,12},{10,14},{12... | collective-permute-start | bytes 786440 | tf_op jit(solution)/shard_map/ppermute | solution.py:32
  75.2 12.4 %collective-permute-start.21 = (bf16[256,512]{1,0:T(8,128)(2,1)S(1)}, bf16[256,512]{1,0:T(8,128)(2,1)S(1)}, u32[]{:S(2)}, u32[]{:S(2)}) collective-permute-start(bf16[256,512]{1,0:T(8,128)(2,1)S(1)} %fusion.29), channel_id=1, source_target_pairs={{0,2},{2,4},{4,6},{6,0},{1,3},{3,5},{5,7},{7,1},{8,10},{10,12},{12... | collective-permute-start | bytes 786440 | tf_op jit(solution)/shard_map/ppermute | solution.py:32
  75.6 12.0 %collective-permute-start.22 = (bf16[256,512]{1,0:T(8,128)(2,1)S(1)}, bf16[256,512]{1,0:T(8,128)(2,1)S(1)}, u32[]{:S(2)}, u32[]{:S(2)}) collective-permute-start(bf16[256,512]{1,0:T(8,128)(2,1)S(1)} %fusion.29), channel_id=1, source_target_pairs={{0,6},{2,0},{4,2},{6,4},{1,7},{3,1},{5,3},{7,5},{8,14},{10,8},{12,... | collective-permute-start | bytes 786440 | tf_op jit(solution)/shard_map/ppermute | solution.py:32
  89.8 35.2 %all-to-all-start = ((bf16[64,16,512]{2,1,0:T(8,128)(2,1)}), bf16[64,16,512]{2,1,0:T(8,128)(2,1)S(1)}, u32[]{:S(2)}, u32[]{:S(2)}) async-start(bf16[64,16,512]{2,1,0:T(8,128)(2,1)} %bitcast.137), calls=%async_computation | async-start | bytes 2097152 | tf_op jit(solution)/shard_map/all_to_all | solution.py:188
  96.4 28.7 %copy-start.2 = (f32[1,16,1024]{2,1,0:T(8,128)S(1)}, f32[1,16,1024]{2,1,0:T(8,128)}, u32[]{:S(2)}) copy-start(f32[1,16,1024]{2,1,0:T(8,128)} %param.10) | copy-start | bytes 196612
  96.4 28.7 %copy-start.3 = (f32[1,16,1024]{2,1,0:T(8,128)S(1)}, f32[1,16,1024]{2,1,0:T(8,128)}, u32[]{:S(2)}) copy-start(f32[1,16,1024]{2,1,0:T(8,128)} %param.11) | copy-start | bytes 196612
  98.2 9.2 %collective-permute-start.23 = (bf16[16,2048]{1,0:T(8,128)(2,1)}, bf16[16,2048]{1,0:T(8,128)(2,1)S(1)}, u32[]{:S(2)}, u32[]{:S(2)}) collective-permute-start(bf16[16,2048]{1,0:T(8,128)(2,1)} %get-tuple-element.51), channel_id=1, source_target_pairs={{0,4},{2,6},{4,0},{6,2},{1,5},{3,7},{5,1},{7,3},{8,12},{10,14},{12... | collective-permute-start | bytes 196616 | tf_op jit(solution)/shard_map/ppermute | solution.py:32
  100.1 7.4 %collective-permute-start.24 = (bf16[16,2048]{1,0:T(8,128)(2,1)}, bf16[16,2048]{1,0:T(8,128)(2,1)S(1)}, u32[]{:S(2)}, u32[]{:S(2)}) collective-permute-start(bf16[16,2048]{1,0:T(8,128)(2,1)} %get-tuple-element.52), channel_id=1, source_target_pairs={{0,2},{2,4},{4,6},{6,0},{1,3},{3,5},{5,7},{7,1},{8,10},{10,12},{12... | collective-permute-start | bytes 196616 | tf_op jit(solution)/shard_map/ppermute | solution.py:32
  101.3 6.2 %collective-permute-start.25 = (bf16[16,2048]{1,0:T(8,128)(2,1)}, bf16[16,2048]{1,0:T(8,128)(2,1)S(1)}, u32[]{:S(2)}, u32[]{:S(2)}) collective-permute-start(bf16[16,2048]{1,0:T(8,128)(2,1)} %get-tuple-element.53), channel_id=1, source_target_pairs={{0,6},{2,0},{4,2},{6,4},{1,7},{3,1},{5,3},{7,5},{8,14},{10,8},{12,... | collective-permute-start | bytes 196616 | tf_op jit(solution)/shard_map/ppermute | solution.py:32
  103.6 33.7 %collective-permute-start.26 = (bf16[512,512]{1,0:T(8,128)(2,1)}, bf16[512,512]{1,0:T(8,128)(2,1)S(1)}, u32[]{:S(2)}, u32[]{:S(2)}) collective-permute-start(bf16[512,512]{1,0:T(8,128)(2,1)} %constant_dynamic-slice_fusion), channel_id=1, source_target_pairs={{0,128},{8,136},{16,144},{24,152},{32,160},{40,168},{48,176},{56,1... | collective-permute-start | bytes 1572872 | tf_op jit(solution)/shard_map/ppermute | solution.py:23
  126.5 9.4 %all-to-all-start.1 = ((bf16[8,16,512]{2,1,0:T(8,128)(2,1)}), bf16[8,16,512]{2,1,0:T(8,128)(2,1)S(1)}, u32[]{:S(2)}, u32[]{:S(2)}) async-start(bf16[8,16,512]{2,1,0:T(8,128)(2,1)} %bitcast.24), calls=%async_computation.1 | async-start | bytes 262144 | tf_op jit(solution)/shard_map/all_to_all | solution.py:200
  130.7 15.0 %collective-permute-start.27 = (bf16[512,512]{1,0:T(8,128)(2,1)}, bf16[512,512]{1,0:T(8,128)(2,1)S(1)}, u32[]{:S(2)}, u32[]{:S(2)}) collective-permute-start(bf16[512,512]{1,0:T(8,128)(2,1)} %constant_dynamic-slice_fusion), channel_id=1, source_target_pairs={{0,64},{8,72},{16,80},{24,88},{32,96},{40,104},{48,112},{56,120},{... | collective-permute-start | bytes 1572872 | tf_op jit(solution)/shard_map/ppermute | solution.py:23
  131.8 14.2 %collective-permute-start.28 = (bf16[512,512]{1,0:T(8,128)(2,1)}, bf16[512,512]{1,0:T(8,128)(2,1)S(1)}, u32[]{:S(2)}, u32[]{:S(2)}) collective-permute-start(bf16[512,512]{1,0:T(8,128)(2,1)} %constant_dynamic-slice_fusion), channel_id=1, source_target_pairs={{0,192},{8,200},{16,208},{24,216},{32,224},{40,232},{48,240},{56,2... | collective-permute-start | bytes 1572872 | tf_op jit(solution)/shard_map/ppermute | solution.py:23
  146.4 2.0 %collective-permute-start.29 = (bf16[64,2048]{1,0:T(8,128)(2,1)S(1)}, bf16[64,2048]{1,0:T(8,128)(2,1)S(1)}, u32[]{:S(2)}, u32[]{:S(2)}) collective-permute-start(bf16[64,2048]{1,0:T(8,128)(2,1)S(1)} %select_convert_fusion), channel_id=1, source_target_pairs={{0,1},{1,0},{2,3},{3,2},{4,5},{5,4},{6,7},{7,6},{8,9},{9,8},{10,11... | collective-permute-start | bytes 786440 | tf_op jit(solution)/shard_map/ppermute | solution.py:36
  148.6 9.2 %collective-permute-start.30 = (bf16[64,2048]{1,0:T(8,128)(2,1)S(1)}, bf16[64,2048]{1,0:T(8,128)(2,1)S(1)}, u32[]{:S(2)}, u32[]{:S(2)}) collective-permute-start(bf16[64,2048]{1,0:T(8,128)(2,1)S(1)} %subtract_convert_fusion), channel_id=1, source_target_pairs={{0,4},{2,6},{4,0},{6,2},{1,5},{3,7},{5,1},{7,3},{8,12},{10,14},{12... | collective-permute-start | bytes 786440 | tf_op jit(solution)/shard_map/ppermute | solution.py:32
  151.6 12.5 %collective-permute-start.31 = (bf16[64,2048]{1,0:T(8,128)(2,1)S(1)}, bf16[64,2048]{1,0:T(8,128)(2,1)S(1)}, u32[]{:S(2)}, u32[]{:S(2)}) collective-permute-start(bf16[64,2048]{1,0:T(8,128)(2,1)S(1)} %subtract_convert_fusion), channel_id=1, source_target_pairs={{0,2},{2,4},{4,6},{6,0},{1,3},{3,5},{5,7},{7,1},{8,10},{10,12},{12... | collective-permute-start | bytes 786440 | tf_op jit(solution)/shard_map/ppermute | solution.py:32
  151.8 12.3 %collective-permute-start.32 = (bf16[64,2048]{1,0:T(8,128)(2,1)S(1)}, bf16[64,2048]{1,0:T(8,128)(2,1)S(1)}, u32[]{:S(2)}, u32[]{:S(2)}) collective-permute-start(bf16[64,2048]{1,0:T(8,128)(2,1)S(1)} %subtract_convert_fusion), channel_id=1, source_target_pairs={{0,6},{2,0},{4,2},{6,4},{1,7},{3,1},{5,3},{7,5},{8,14},{10,8},{12,... | collective-permute-start | bytes 786440 | tf_op jit(solution)/shard_map/ppermute | solution.py:32
  164.2 1.0 copy-start
